TPU v7x, 32 devices: a whole 2x2x4 slice. The times are simulated.
32 devices in a mesh: gx: 4 (over y, x), gy: 8 (over z, core).
Axes of the slice: x: 2, y: 2, z: 4, core: 2. Of those that a mesh axis runs over, the one named last changes fastest.
Arguments:
- adjoint: float32 [5, 16, 128, 256], P(None, 'gx', 'gy'), may hold values from -6 to 6
- jac_x: bfloat16 [5, 5, 16, 128, 256], P(None, None, 'gx', 'gy'), may hold values from -2.5 to 2.5
- jac_y: bfloat16 [5, 5, 16, 128, 256], P(None, None, 'gx', 'gy'), may hold values from -2.5 to 2.5
- alpha_x: float32 [16], replicated, may hold values from 0.49375 to 0.498125
- metric_x: float32 [16], P('gx'), may hold values from 0.15 to 0.6
- alpha_y: float32 [128], replicated, may hold values from 0.49960938 to 0.49988282
- metric_y: float32 [128], P('gy'), may hold values from 0.15 to 0.6
- surf_values: float32 [32, 5, 512], P(('gx', 'gy')), may hold values from -12 to 12
- surf_cells: int32 [32, 512], P(('gx', 'gy')), may hold values from 0 to 16383
- surf_owner: int32 [32, 512, 1], P(('gx', 'gy')), may hold values from 0 to 31; in each aligned block of 512 rows (0 to 511, 512 to 1023, ..., all dimensions but the last counted through in order) at most 32 rows name the same one
Outputs:
- adjoint_rhs: float32 [5, 16, 128, 256], P(None, 'gx', 'gy')
Inputs may be any that keep to these rules, and one draw needn't show every extreme that they name: `surf_owner`: within the 512 points of one device no owner appears more than 32 times, and some owner appears exactly 32 times.
All inputs are finite; a program needn't handle non-finite values.
Results may differ from a plain program's by a relative error of at most 0.0003.
Values sent between devices are 32-bit elements; how exact they have to be, the bound alone decides.
No kernel may reach another device: no remote copies, remote signals or barrier semaphores. Data moves between devices by JAX's collectives and lax.ppermute only.
A program may use at most 64 MiB of HBM per device.

v0:
```python
import jax
import jax.numpy as jnp
from jax import lax
from jax.sharding import PartitionSpec as P


def padded_2(block, sides, width):
    for axis, dim in sides:
        count = lax.axis_size(axis)
        forward = [(i, i + 1) for i in range(count - 1)]
        backward = [(target, source) for source, target in forward]
        low = lax.ppermute(
            lax.slice_in_dim(block, block.shape[dim] - width, None, axis=dim), axis, forward
        )
        high = lax.ppermute(lax.slice_in_dim(block, 0, width, axis=dim), axis, backward)
        block = jnp.concatenate([low, block, high], axis=dim)
    return block


def shaped(vector, line_axis):
    return vector.reshape((1,) * line_axis + (-1,) + (1,) * (3 - line_axis))


def coefficients(alpha_line):
    lower_diag = alpha_line.at[0].set(0.0)
    upper_diag = alpha_line.at[-1].set(0.0)

    def advance(carried, pieces):
        below_now, above_now = pieces
        pivot_now = 1.0 - below_now * carried
        ratio_now = above_now / pivot_now
        return (ratio_now, (pivot_now, ratio_now))

    _, (pivots, ratios) = lax.scan(advance, jnp.zeros((), jnp.float32), (lower_diag, upper_diag))
    return (lower_diag, pivots, ratios)


def flux_of(jacobian, state_field):
    outputs = []
    for target in range(state_field.shape[0]):
        summed = jacobian[0, target].astype(jnp.float32) * state_field[0]
        for source in range(1, state_field.shape[0]):
            summed = summed + jacobian[source, target].astype(jnp.float32) * state_field[source]
        outputs.append(summed)
    return jnp.stack(outputs)


def reduced_solve(gathered, position):
    tail_maps, head_maps, scalars = gathered

    def forward(carried, pieces):
        gain_now, tail_now = pieces
        return (gain_now * carried + tail_now, carried)

    _, entries = lax.scan(forward, jnp.zeros_like(tail_maps[0]), (scalars[:, 0], tail_maps))
    head_full = head_maps + scalars[:, 1].reshape(-1, 1, 1, 1) * entries

    def backward(carried, pieces):
        gain_now, head_now = pieces
        return (gain_now * carried + head_now, carried)

    _, exit_values = lax.scan(
        backward, jnp.zeros_like(tail_maps[0]), (scalars[:, 2], head_full), reverse=True
    )
    entering = lax.dynamic_index_in_dim(entries, position, 0, keepdims=False)
    leaving = lax.dynamic_index_in_dim(exit_values, position, 0, keepdims=False)
    return (entering, leaving)


def solve_line(flux_field, alpha_line, metric_block, line_axis, direction):
    cells_line = flux_field.shape[line_axis]
    if direction == "x":
        padded = padded_2(flux_field, (("gx", 1),), 2)
        position = lax.axis_index("gx")
    else:
        padded = padded_2(flux_field, (("gy", 2),), 2)
        position = lax.axis_index("gy")
    first_cell = position * cells_line
    alpha_block = lax.dynamic_slice_in_dim(alpha_line, first_cell, cells_line)
    coef_a = shaped(2.0 / 3.0 * (alpha_block + 2.0), line_axis)
    coef_b = shaped((4.0 * alpha_block - 1.0) / 3.0, line_axis)

    def window(offset):
        return lax.slice_in_dim(padded, offset, offset + cells_line, axis=line_axis)

    right_side = 0.5 * coef_a * (window(3) - window(1)) + 0.25 * coef_b * (window(4) - window(0))
    lower_all, pivot_all, ratio_all = coefficients(alpha_line)
    lower_b = lax.dynamic_slice_in_dim(lower_all, first_cell, cells_line)
    pivot_b = lax.dynamic_slice_in_dim(pivot_all, first_cell, cells_line)
    ratio_b = lax.dynamic_slice_in_dim(ratio_all, first_cell, cells_line)
    eliminated = []
    growth = []
    for offset in range(cells_line):
        column = lax.index_in_dim(right_side, offset, line_axis, keepdims=False)
        if offset == 0:
            eliminated.append(column / pivot_b[0])
            growth.append(-lower_b[0] / pivot_b[0])
        else:
            eliminated.append((column - lower_b[offset] * eliminated[offset - 1]) / pivot_b[offset])
            growth.append(-lower_b[offset] / pivot_b[offset] * growth[offset - 1])
    back_e = [None] * cells_line
    back_g = [None] * cells_line
    reaches = [None] * cells_line
    back_e[cells_line - 1] = eliminated[cells_line - 1]
    back_g[cells_line - 1] = growth[cells_line - 1]
    reaches[cells_line - 1] = -ratio_b[cells_line - 1]
    for offset in range(cells_line - 2, -1, -1):
        back_e[offset] = eliminated[offset] - ratio_b[offset] * back_e[offset + 1]
        back_g[offset] = growth[offset] - ratio_b[offset] * back_g[offset + 1]
        reaches[offset] = -ratio_b[offset] * reaches[offset + 1]
    last_e = eliminated[cells_line - 1]
    last_g = growth[cells_line - 1]
    scalars = jnp.stack([last_g, back_g[0], reaches[0]])[None]
    if direction == "x":
        gathered = (
            lax.all_gather(last_e[None], "gx", axis=0, tiled=True),
            lax.all_gather(back_e[0][None], "gx", axis=0, tiled=True),
            lax.all_gather(scalars, "gx", axis=0, tiled=True),
        )
    else:
        gathered = (
            lax.all_gather(last_e[None], "gy", axis=0, tiled=True),
            lax.all_gather(back_e[0][None], "gy", axis=0, tiled=True),
            lax.all_gather(scalars, "gy", axis=0, tiled=True),
        )
    entering, leaving = reduced_solve(gathered, position)
    columns = []
    for offset in range(cells_line):
        solved = back_e[offset] + back_g[offset] * entering + reaches[offset] * leaving
        columns.append(solved * metric_block[offset])
    return jnp.stack(columns, axis=line_axis)


def place_points(amounts, targets, rows_block, depth):
    row_of = targets // depth
    depth_of = targets % depth
    row_hot = (row_of[:, None] == jnp.arange(rows_block, dtype=jnp.int32)[None, :]).astype(
        jnp.float32
    )
    depth_hot = (depth_of[:, None] == jnp.arange(depth, dtype=jnp.int32)[None, :]).astype(
        jnp.float32
    )
    weighted = amounts[:, :, None] * row_hot[None]
    return jnp.einsum("fpr,pz->frz", weighted, depth_hot, precision=lax.Precision.HIGHEST)


def observer_forcing(surf_values, surf_cells, surf_owner, rows_block, depth):
    devices = lax.axis_size("gx") * lax.axis_size("gy")
    owners = surf_owner[0, :, 0]
    cell_ids = surf_cells[0]
    payload = surf_values[0]
    fields = payload.shape[0]
    points = payload.shape[1]
    capacity = max(4, 2 * points // devices)
    onehot = (owners[:, None] == jnp.arange(devices, dtype=jnp.int32)[None, :]).astype(jnp.float32)
    lower_tri = (jnp.arange(points)[:, None] >= jnp.arange(points)[None, :]).astype(jnp.float32)
    running = jnp.dot(lower_tri, onehot, precision=lax.Precision.HIGHEST)
    ranks_in = jnp.sum(running * onehot, axis=1).astype(jnp.int32) - 1
    slots = owners * capacity + ranks_in
    slot_hot = (slots[:, None] == jnp.arange(devices * capacity, dtype=jnp.int32)[None, :]).astype(
        jnp.float32
    )
    packed = jnp.concatenate([payload, cell_ids[None].astype(jnp.float32)], axis=0)
    outgoing = jnp.dot(packed, slot_hot, precision=lax.Precision.HIGHEST)
    outgoing = outgoing.reshape(fields + 1, lax.axis_size("gx"), lax.axis_size("gy"), capacity)
    received = lax.all_to_all(
        lax.all_to_all(outgoing, "gx", split_axis=1, concat_axis=1, tiled=True),
        "gy",
        split_axis=2,
        concat_axis=2,
        tiled=True,
    )
    flattened = received.reshape(fields + 1, -1)
    targets = flattened[fields].astype(jnp.int32)
    amounts = flattened[:fields]
    return place_points(amounts, targets, rows_block, depth)


def on_device(
    adjoint, jac_x, jac_y, alpha_x, metric_x, alpha_y, metric_y, surf_values, surf_cells, surf_owner
):
    flux_x = flux_of(jac_x, adjoint)
    flux_y = flux_of(jac_y, adjoint)
    deriv_x = solve_line(flux_x, alpha_x, metric_x, 1, "x")
    deriv_y = solve_line(flux_y, alpha_y, metric_y, 2, "y")
    rows_block = adjoint.shape[1] * adjoint.shape[2]
    forcing = observer_forcing(surf_values, surf_cells, surf_owner, rows_block, adjoint.shape[3])
    forcing = forcing.reshape(adjoint.shape)
    return forcing - (deriv_x + deriv_y)


def solution(mesh):
    in_specs = (
        P(None, "gx", "gy", None),
        P(None, None, "gx", "gy", None),
        P(None, None, "gx", "gy", None),
        P(),
        P("gx"),
        P(),
        P("gy"),
        P(("gx", "gy"), None, None),
        P(("gx", "gy"), None),
        P(("gx", "gy"), None, None),
    )
    out_specs = P(None, "gx", "gy", None)
    return jax.shard_map(
        on_device, mesh=mesh, in_specs=in_specs, out_specs=out_specs, check_vma=False
    )
```

profile of v0, /device:TPU:0, one launch (start us, length us, event | category | flops | bytes accessed | tf_op | source)
XLA Modules:
  0.0 672.7 jit_solution(2915529472104012814)
XLA Ops:
  1.3 1.3 bitcast_convert_fusion.29
  2.7 0.9 bitcast_convert_fusion.1
  3.9 0.8 copy-done.1
  8.3 2.4 collective-permute-start.3
  10.7 1.3 collective-permute-start.2
  12.1 4.2 collective-permute-start.1
  16.3 1.3 collective-permute-start
  18.0 0.8 fusion
  18.9 0.7 reshape.1819
  19.7 4.9 all-to-all-start
  24.8 341.6 %while.93 = (s32[]{:T(128)}, f32[]{:T(128)}, f32[128]{0:T(128)S(1)}, f32[128]{0:T(128)S(1)}, f32[128]{0:T(128)S(1)}, /*index=5*/f32[128]{0:T(128)S(1)}, s32[]{:T(128)}, f32[]{:T(128)}) while((s32[]{:T(128)}, f32[]{:T(128)}, f32[128]{0:T(128)S(1)}, f32[128]{0:T(128)S(1)}, f32[128]{0:T(128)S(1)}, /*index=5*/f32[128]{0:T(128)S(1)}, s32[]{:T(128)}, ...), condition=%wide.region_8.9_spmd, body=%wide.region_7.8_spmd.sunk | while | flops 5 | bytes 177 | solution.py:34
  366.5 0.7 fusion.136
  367.2 0.7 fusion.135
  368.0 0.7 fusion.138
  377.3 0.7 fusion.137
  410.6 17.3 %all-reduce.1 = f32[24]{0:T(128)S(1)} all-reduce(f32[24]{0:T(128)S(1)} %maximum_dynamic-update-slice_fusion.1), channel_id=3, replica_groups=mesh['gx'=4,'gy'=8] {'gy'}, use_global_device_ids=true, to_apply=%add.1 | all-reduce | flops 24 | bytes 192
  429.2 40.1 %while.92 = (s32[]{:T(128)}, f32[]{:T(128)}, f32[16]{0:T(128)S(1)}, f32[16]{0:T(128)S(1)}, f32[16]{0:T(128)S(1)}, /*index=5*/f32[16]{0:T(128)S(1)}, s32[]{:T(128)}, f32[]{:T(128)}) while((s32[]{:T(128)}, f32[]{:T(128)}, f32[16]{0:T(128)S(1)}, f32[16]{0:T(128)S(1)}, f32[16]{0:T(128)S(1)}, /*index=5*/f32[16]{0:T(128)S(1)}, s32[]{:T(128)}, ...), condition=%wide.region_2.3_spmd, body=%wide.region_1.0_spmd.sunk | while | flops 5 | bytes 177 | solution.py:34
  481.5 10.1 %all-reduce = f32[12]{0:T(128)S(1)} all-reduce(f32[12]{0:T(128)S(1)} %maximum_dynamic-update-slice_fusion), channel_id=2, replica_groups=mesh['gx'=4,'gy'=8] {'gx'}, use_global_device_ids=true, to_apply=%add | all-reduce | flops 12 | bytes 96
  494.5 0.7 reduce.20
  495.4 0.7 reshape.1821
  496.1 3.3 all-to-all-start.1
  500.4 28.2 %bitcast_subtract_fusion.3 = (f32[1,5,4,256]{3,1,2,0:T(8,128)S(1)}, f32[1,5,4,256]{3,1,2,0:T(8,128)S(1)}) fusion(f32[5,4,1,256]{3,1,2,0:T(4,128)S(1)} %get-tuple-element.656, f32[]{:T(128)} %bitcast.136, f32[]{:T(128)} %bitcast.133, f32[]{:T(128)} %bitcast.130, f32[]{:T(128)} %bitcast.127, f32[]{:T(128)} %bitcast.124, f32[]{:T(128)} %bitcast.121, ...), kind=kLoop, calls=%fused_computation.254 | loop fusion | flops 384000 | bytes 368820 | tf_op jit(solution)/shard_map/sub | solution.py:108
  528.6 14.6 %all_gather.22 = f32[8,5,4,256]{3,2,1,0:T(4,128)S(1)} all-gather(f32[1,5,4,256]{3,2,1,0:T(4,128)S(1)} %copy.3892), channel_id=1, replica_groups=mesh['gx'=4,'gy'=8] {'gy'}, dimensions={0}, use_global_device_ids=true | all-gather | bytes 184320 | tf_op jit(solution)/shard_map/all_gather | solution.py:122
  543.2 10.5 %while.96 = (s32[]{:T(128)}, f32[5,4,256]{2,1,0:T(4,128)S(1)}, f32[8,5,4,256]{3,2,1,0:T(4,128)S(1)}, f32[8]{0:T(128)S(1)}, f32[8,5,4,256]{3,2,1,0:T(4,128)S(1)}, /*index=5*/s32[]{:T(128)}, s32[]{:T(128)}) while((s32[]{:T(128)}, f32[5,4,256]{2,1,0:T(4,128)S(1)}, f32[8,5,4,256]{3,2,1,0:T(4,128)S(1)}, f32[8]{0:T(128)S(1)}, ...), condition=%wide.region_10.11_spmd.clone, body=%wide.region_9.10_spmd.clone.sunk | while | flops 20483 | bytes 102520 | solution.py:55
  553.7 14.2 %all_gather.23 = f32[8,5,4,256]{3,2,1,0:T(4,128)S(1)} all-gather(f32[1,5,4,256]{3,2,1,0:T(4,128)S(1)} %copy.3895), channel_id=1, replica_groups=mesh['gx'=4,'gy'=8] {'gy'}, dimensions={0}, use_global_device_ids=true | all-gather | bytes 184320 | tf_op jit(solution)/shard_map/all_gather | solution.py:123
  568.0 10.5 %while.97 = (s32[]{:T(128)}, f32[5,4,256]{2,1,0:T(4,128)S(1)}, f32[8,5,4,256]{3,2,1,0:T(4,128)S(1)}, f32[8]{0:T(128)S(1)}, f32[8,5,4,256]{3,2,1,0:T(4,128)S(1)}, /*index=5*/s32[]{:T(128)}, s32[]{:T(128)}, s32[]{:T(128)}) while((s32[]{:T(128)}, f32[5,4,256]{2,1,0:T(4,128)S(1)}, f32[8,5,4,256]{3,2,1,0:T(4,128)S(1)}, ...), condition=%wide.region_12.13_spmd.clone, body=%wide.region_11.12_spmd.clone.sunk | while | flops 20484 | bytes 102540 | solution.py:62
  578.5 28.9 %constant_dynamic-update-slice_fusion.15 = (f32[5,4,16,256]{3,1,2,0:T(4,128)S(1)}, f32[5,4,1,256]{3,1,2,0:T(4,128)S(1)}, f32[5,4,1,256]{3,1,2,0:T(4,128)S(1)}, f...) fusion(f32[5,4,1,256]{3,1,2,0:T(4,128)S(1)} %get-tuple-element., ...), kind=kLoop, calls=%fused_computation.203 | loop fusion | flops 409599 | bytes 676036
  608.1 1.2 constant_dynamic-update-slice_fusion.13
  609.9 1.2 constant_dynamic-update-slice_fusion.11
  611.8 1.4 constant_dynamic-update-slice_fusion.9
  613.8 1.3 constant_dynamic-update-slice_fusion.7
  615.0 0.7 constant_dynamic-update-slice_fusion.6
  615.8 1.3 constant_dynamic-update-slice_fusion.5
  617.7 1.3 constant_dynamic-update-slice_fusion.3
  619.6 2.6 constant_dynamic-update-slice_fusion.1
  622.2 1.9 constant_dynamic-update-slice_fusion
  624.1 0.7 reduce.21
  625.3 1.0 fusion.1
  626.8 2.3 fusion.126
  629.2 5.9 bitcast_subtract_fusion
  635.1 8.3 %all_gather.20 = f32[4,5,16,256]{3,2,1,0:T(8,128)S(1)} all-gather(f32[1,5,16,256]{3,2,1,0:T(8,128)S(1)} %copy.3812), channel_id=1, replica_groups=mesh['gx'=4,'gy'=8] {'gx'}, dimensions={0}, use_global_device_ids=true | all-gather | bytes 409600 | tf_op jit(solution)/shard_map/all_gather | solution.py:117
  643.4 9.2 %all_gather.19 = f32[4,5,16,256]{3,2,1,0:T(8,128)S(1)} all-gather(f32[1,5,16,256]{3,2,1,0:T(8,128)S(1)} %copy.3809), channel_id=1, replica_groups=mesh['gx'=4,'gy'=8] {'gx'}, dimensions={0}, use_global_device_ids=true | all-gather | bytes 409600 | tf_op jit(solution)/shard_map/all_gather | solution.py:116
  652.6 5.2 while.94
  657.9 5.2 while.95
  663.2 5.3 fusion.33
  668.5 0.7 fusion.32
  669.3 2.1 fusion.31
  671.9 0.8 copy.3931
  (760 shorter events, 250.9 us)
Async XLA Ops:
  1.3 1.4 copy-start
  3.7 1.0 copy-start.1
  7.9 9.8 %copy-start.5 = (s32[1,512,1]{1,2,0:T(1,128)S(1)}, s32[1,512,1]{1,2,0:T(1,128)}, u32[]{:S(2)}) copy-start(s32[1,512,1]{1,2,0:T(1,128)} %param.39) | copy-start | bytes 6148
  7.9 10.1 %copy-start.6 = (s32[1,512]{1,0:T(1,128)S(1)}, s32[1,512]{1,0:T(1,128)}, u32[]{:S(2)}) copy-start(s32[1,512]{1,0:T(1,128)} %param.38) | copy-start | bytes 6148
  7.9 10.1 %copy-start.3 = (f32[1,5,512]{2,0,1:T(1,128)S(1)}, f32[1,5,512]{2,0,1:T(1,128)}, u32[]{:S(2)}) copy-start(f32[1,5,512]{2,0,1:T(1,128)} %param.37) | copy-start | bytes 30724
  8.3 491.2 %collective-permute-start.3 = (f32[5,4,2,256]{3,1,2,0:T(4,128)S(1)}, f32[5,4,2,256]{3,1,2,0:T(4,128)S(1)}, u32[]{:S(2)}, u32[]{:S(2)}) collective-permute-start(f32[5,4,2,256]{3,1,2,0:T(4,128)S(1)} %get-tuple-element.658), channel_id=1, source_target_pairs={{0,1},{1,2},{2,3},{3,4},{4,5},{5,6},{6,7},{8,9},{9,10},{10,11},{11... | collective-permute-start | bytes 122888 | tf_op jit(solution)/shard_map/ppermute | solution.py:12
  10.7 488.8 %collective-permute-start.2 = (f32[5,4,2,256]{3,1,2,0:T(4,128)S(1)}, f32[5,4,2,256]{3,1,2,0:T(4,128)S(1)}, u32[]{:S(2)}, u32[]{:S(2)}) collective-permute-start(f32[5,4,2,256]{3,1,2,0:T(4,128)S(1)} %get-tuple-element.657), channel_id=1, source_target_pairs={{1,0},{2,1},{3,2},{4,3},{5,4},{6,5},{7,6},{9,8},{10,9},{11,10},{12... | collective-permute-start | bytes 122888 | tf_op jit(solution)/shard_map/ppermute | solution.py:15
  12.1 614.1 %collective-permute-start.1 = (f32[5,2,16,256]{3,1,2,0:T(2,128)S(1)}, f32[5,2,16,256]{3,1,2,0:T(2,128)S(1)}, u32[]{:S(2)}, u32[]{:S(2)}) collective-permute-start(f32[5,2,16,256]{3,1,2,0:T(2,128)S(1)} %get-tuple-element.638), channel_id=1, source_target_pairs={{0,8},{8,16},{16,24},{1,9},{9,17},{17,25},{2,10},{10,18},{18,26},{... | collective-permute-start | bytes 491528 | tf_op jit(solution)/shard_map/ppermute | solution.py:12
  16.3 609.9 %collective-permute-start = (f32[5,2,16,256]{3,1,2,0:T(2,128)S(1)}, f32[5,2,16,256]{3,1,2,0:T(2,128)S(1)}, u32[]{:S(2)}, u32[]{:S(2)}) collective-permute-start(f32[5,2,16,256]{3,1,2,0:T(2,128)S(1)} %get-tuple-element.637), channel_id=1, source_target_pairs={{8,0},{16,8},{24,16},{9,1},{17,9},{25,17},{10,2},{18,10},{26,18},{... | collective-permute-start | bytes 491528 | tf_op jit(solution)/shard_map/ppermute | solution.py:15
  17.6 349.6 %copy-start.2 = (f32[16]{0:T(128)S(1)}, f32[16]{0:T(128)}, u32[]{:S(2)}) copy-start(f32[16]{0:T(128)} %param.36) | copy-start | bytes 196
  18.0 391.3 %copy-start.8 = (u32[32]{0:T(128)S(1)}, u32[32]{0:T(128)}, u32[]{:S(2)}) copy-start(u32[32]{0:T(128)} %constant.291) | copy-start | bytes 388
  18.0 410.0 %copy-start.7 = (u32[32]{0:T(128)S(1)}, u32[32]{0:T(128)}, u32[]{:S(2)}) copy-start(u32[32]{0:T(128)} %constant.286) | copy-start | bytes 388
  18.9 472.8 %copy-start.4 = (f32[4]{0:T(128)S(1)}, f32[4]{0:T(128)}, u32[]{:S(2)}) copy-start(f32[4]{0:T(128)} %param.34) | copy-start | bytes 52
  19.7 474.2 %all-to-all-start = ((f32[4,1,1536]{2,1,0:T(1,128)}), f32[4,1,1536]{2,1,0:T(1,128)S(1)}, u32[]{:S(2)}, u32[]{:S(2)}) async-start(f32[4,1,1536]{2,1,0:T(1,128)} %reshape.1819), calls=%async_computation | async-start | bytes 49152 | tf_op jit(solution)/shard_map/all_to_all | solution.py:167
  496.1 128.0 %all-to-all-start.1 = ((f32[8,1,768]{2,1,0:T(1,128)}), f32[8,1,768]{2,1,0:T(1,128)S(1)}, u32[]{:S(2)}, u32[]{:S(2)}) async-start(f32[8,1,768]{2,1,0:T(1,128)} %reshape.1821), calls=%async_computation.1 | async-start | bytes 49152 | tf_op jit(solution)/shard_map/all_to_all | solution.py:166
where the time goes:
time: 678 us; the launch traced here: 673 us
  local copies, waits for them, and re-layouts  230 us (34%)
  loops' own time  181 us (27%)
  other arithmetic  116 us (17%)
  blocking collectives  73.6 us (11%)
  between operations  52.6 us (8%)
  starting transfers between devices  17.4 us (3%)
    another operation x2, loops' own time, coefficients(): lax.scan(advance, jnp.zeros((), jnp.float32), (lower_diag, upper_diag))  180 us
    dynamic_slice x288, local copies, waits for them, and re-layouts, coefficients(): lax.scan(advance, jnp.zeros((), jnp.float32), (lower_diag, upper_diag))  171 us
    unnamed x28, other arithmetic  46.6 us
    sub x2, other arithmetic, solve_line(): back_e[offset] = eliminated[offset] - ratio_b[offset] * back_e[offset + 1]  34.1 us
    dynamic_update_slice x288, local copies, waits for them, and re-layouts, coefficients(): lax.scan(advance, jnp.zeros((), jnp.float32), (lower_diag, upper_diag))  31.2 us
    unnamed x2, blocking collectives  27.3 us
    dynamic_slice x24, local copies, waits for them, and re-layouts, reduced_solve(): lax.scan(forward, jnp.zeros_like(tail_maps[0]), (scalars[:, 0], tail_maps))  14.6 us
    all_gather x1, blocking collectives, solve_line(): lax.all_gather(last_e[None], 'gy', axis=0, tiled=True)  14.6 us
  transfers between devices with their start and end apart: 6, of which 0 were waited for; matrix products, arithmetic and copies ran while one was open for 46% of the time, Pallas kernels for 0%

commit v1 on v0

v1 whole, which is shorter than its diff:
```python
import functools

import jax
import jax.numpy as jnp
from jax import lax
from jax.experimental import pallas as pl
from jax.experimental.pallas import tpu as pltpu
from jax.sharding import PartitionSpec as P

F32 = jnp.float32
BF16 = jnp.bfloat16
NT = (((1,), (1,)), ((), ()))


def moved(row, by, lane, fill):
    lanes = row.shape[1]
    turned = pltpu.roll(row, by % lanes, 1)
    keep = (lane >= by) if by > 0 else (lane < lanes + by)
    return jnp.where(keep, turned, fill)


def running(parts, lane, direction):
    lanes = lane.shape[1]
    a, b, c, d = parts
    step = 1
    while step < lanes:
        shift = step * direction
        a0, b0 = moved(a, shift, lane, 1.0), moved(b, shift, lane, 0.0)
        c0, d0 = moved(c, shift, lane, 0.0), moved(d, shift, lane, 1.0)
        a, b, c, d = a * a0 + b * c0, a * b0 + b * d0, c * a0 + d * c0, c * b0 + d * d0
        step *= 2
    return a + b


def line_rows(alpha, sizes):
    axes, lanes = alpha.shape
    lane = lax.broadcasted_iota(jnp.int32, (axes, lanes), 1)
    which = lax.broadcasted_iota(jnp.int32, (axes, lanes), 0)
    count = jnp.zeros((axes, lanes), jnp.int32)
    for axis, size in enumerate(sizes):
        count = jnp.where(which == axis, size, count)
    inside = lane < count
    alpha = jnp.where(inside, alpha, 0.5)
    slack = 1.0 - 2.0 * alpha
    twice = 2.0 * alpha

    eps = slack + twice * moved(slack, 1, lane, 0.0)
    c = 1.0 - eps
    fwd = running((1.0 + eps, c, eps, c), lane, 1)
    eps = slack + twice * moved(slack, -1, lane, 0.0)
    c = 1.0 - eps
    bwd = running(
        (
            jnp.where(inside, 1.0 + eps, 1.0),
            jnp.where(inside, c, 0.0),
            jnp.where(inside, eps, 0.0),
            jnp.where(inside, c, 1.0),
        ),
        lane,
        -1,
    )
    weight = twice
    step = 1
    while step < lanes:
        weight = weight * moved(weight, step, lane, 1.0)
        step *= 2
    before_w = moved(weight, 1, lane, 1.0)
    before_f = moved(fwd, 1, lane, 1.0)
    after_g = moved(bwd, -1, lane, 1.0)
    whole = jnp.sum(jnp.where(lane == count - 1, fwd, 0.0), axis=1, keepdims=True)
    sign = jnp.where(lane % 2 == 0, 1.0, -1.0)

    p = jnp.where(inside, sign * weight * after_g, 0.0)
    u = jnp.where(inside, sign * before_f / before_w, 0.0)
    q = jnp.where(inside, 2.0 * sign * before_f / (weight * whole), 0.0)
    v = jnp.where(inside, 2.0 * sign * before_w * after_g / whole, 0.0)
    near = (alpha + 2.0) / 3.0
    far = (4.0 * alpha - 1.0) / 12.0

    def folded(row):
        one, two = row * near, row * far
        return (
            moved(one, 1, lane, 0.0)
            - moved(one, -1, lane, 0.0)
            + moved(two, 2, lane, 0.0)
            - moved(two, -2, lane, 0.0)
        )

    diag = p * (moved(q * near, 1, lane, 0.0) + moved(q * far, 2, lane, 0.0)) - u * (
        moved(v * near, -1, lane, 0.0) + moved(v * far, -2, lane, 0.0)
    )
    next_far = moved(jnp.where(inside, far, 0.0), -1, lane, 0.0)
    last_far = moved(far, 1, lane, 0.0)
    low = (p * moved(q, -1, lane, 0.0) - u * moved(v, -1, lane, 0.0)) * next_far
    high = (p * moved(q, 1, lane, 0.0) - u * moved(v, 1, lane, 0.0)) * last_far
    t = jnp.where(inside, folded(q), 0.0)
    s = jnp.where(inside, folded(v), 0.0)
    return [p, u, t, s, diag, low, high]


def packed_points(values, cells, owners, devices, capacity):
    fields, points = values.shape
    owner_of = lax.broadcasted_iota(jnp.int32, (devices, points), 0)
    hot = jnp.where(owner_of == owners, 1.0, 0.0)
    width = 128
    upper = jnp.where(
        lax.broadcasted_iota(jnp.int32, (width, width), 0)
        < lax.broadcasted_iota(jnp.int32, (width, width), 1),
        1.0,
        0.0,
    ).astype(BF16)
    carried = jnp.zeros((devices, 1), F32)
    ranks = []
    for start in range(0, points, width):
        piece = hot[:, start : start + width]
        counts = carried + jnp.dot(piece.astype(BF16), upper, preferred_element_type=F32)
        ranks.append(jnp.sum(piece * counts, axis=0, keepdims=True))
        carried = carried + jnp.sum(piece, axis=1, keepdims=True)
    rank = jnp.concatenate(ranks, axis=1).astype(jnp.int32)
    slot = lax.broadcasted_iota(jnp.int32, (capacity, points), 0) == rank
    rows = [jnp.where(slot, values[f : f + 1], 0.0) for f in range(fields)]
    rows.append(jnp.where(slot, cells.astype(F32), 0.0))
    spread = jnp.concatenate(rows, axis=0)
    top = spread.astype(BF16)
    rest = (spread - top.astype(F32)).astype(BF16)
    hot = hot.astype(BF16)
    return lax.dot_general(hot, top, NT, preferred_element_type=F32) + lax.dot_general(
        hot, rest, NT, preferred_element_type=F32
    )


def first_kernel(
    sizes,
    devices,
    capacity,
    alpha_x,
    alpha_y,
    metric_x,
    metric_y,
    values,
    cells,
    owners,
    adjoint,
    jac_x,
    jac_y,
    pack_out,
    flux_x_out,
    flux_y_out,
    send_x,
    send_y,
    coef_x_out,
    coef_y_out,
    adj,
    jx,
    jy,
    alpha_s,
    sems,
):
    copies = [
        pltpu.make_async_copy(source, target, sems.at[number])
        for number, (source, target) in enumerate(((adjoint, adj), (jac_x, jx), (jac_y, jy)))
    ]
    for copy in copies:
        copy.start()
    fields, cells_x, cells_y, depth = adj.shape
    lanes = alpha_s.shape[1]

    alpha_s[...] = jnp.full(alpha_s.shape, 0.5, F32)
    alpha_s[0:1, 0 : sizes[0]] = alpha_x[...]
    alpha_s[1:2, 0 : sizes[1]] = alpha_y[...]
    rows = line_rows(alpha_s[...], sizes)
    first_x = lax.axis_index("gx") * cells_x
    first_y = lax.axis_index("gy") * cells_y
    coef_x = jnp.concatenate([row[0:1] for row in rows] + [jnp.zeros((1, lanes), F32)], axis=0)
    coef_y = jnp.concatenate([row[1:2] for row in rows] + [jnp.zeros((1, lanes), F32)], axis=0)
    coef_x = pltpu.roll(coef_x, lax.rem(lanes - first_x, lanes), 1)[:, :128]
    coef_y = pltpu.roll(coef_y, lax.rem(lanes - first_y, lanes), 1)[:, :128]
    row_of = lax.broadcasted_iota(jnp.int32, (8, 128), 0)
    scaled = (row_of != 2) & (row_of != 3)
    gain_x = jnp.concatenate([metric_x[...], jnp.zeros((1, 128 - cells_x), F32)], axis=1)
    gain_y = jnp.concatenate([metric_y[...], jnp.zeros((1, 128 - cells_y), F32)], axis=1)
    coef_x = coef_x * jnp.where(scaled, gain_x, 1.0)
    coef_y = coef_y * jnp.where(scaled, gain_y, 1.0)
    coef_x_out[...] = coef_x
    columns_y = jnp.concatenate([coef_y, jnp.zeros((120, 128), F32)], axis=0).T[:cells_y]
    coef_y_out[...] = columns_y

    pack_out[...] = packed_points(values[...], cells[...], owners[...], devices, capacity)

    shape = (cells_y, depth)
    copies[0].wait()
    copies[1].wait()
    totals = [[None, None] for _ in range(fields)]
    for i in range(cells_x):
        state = [adj[k, i] for k in range(fields)]
        for target in range(fields):
            flux = jx[0, target, i].astype(F32) * state[0]
            for k in range(1, fields):
                flux = flux + jx[k, target, i].astype(F32) * state[k]
            flux_x_out[target, i] = flux
            for side in range(2):
                term = jnp.broadcast_to(coef_x[2 + side : 3 + side, i : i + 1], shape) * flux
                if i > 0:
                    term = totals[target][side] + term
                totals[target][side] = term
            if i == 0:
                send_x[2, target] = flux
            if i == cells_x - 1:
                send_x[3, target] = flux
    for target in range(fields):
        for side in range(2):
            send_x[side, target] = totals[target][side]

    weight_t = jnp.broadcast_to(columns_y[:, 2:3], shape)
    weight_s = jnp.broadcast_to(columns_y[:, 3:4], shape)
    copies[2].wait()
    for i in range(cells_x):
        state = [adj[k, i] for k in range(fields)]
        for target in range(fields):
            flux = jy[0, target, i].astype(F32) * state[0]
            for k in range(1, fields):
                flux = flux + jy[k, target, i].astype(F32) * state[k]
            flux_y_out[target, i] = flux
            line = target * cells_x + i
            send_y[0, line : line + 1] = jnp.sum(weight_t * flux, axis=0, keepdims=True)
            send_y[1, line : line + 1] = jnp.sum(weight_s * flux, axis=0, keepdims=True)
            send_y[2, line : line + 1] = flux[0:1]
            send_y[3, line : line + 1] = flux[cells_y - 1 : cells_y]


def flat_slots(received, number, capacity):
    senders = received.shape[0]
    part = received[:, number * capacity : (number + 1) * capacity]
    repeats = 128 // capacity
    tiled = jnp.concatenate([part] * repeats, axis=1)
    lane = lax.broadcasted_iota(jnp.int32, (senders, 128), 1) // capacity
    sender = lax.broadcasted_iota(jnp.int32, (senders, 128), 0)
    rows = []
    for group in range(senders // repeats):
        mine = sender == lane + group * repeats
        rows.append(jnp.sum(jnp.where(mine, tiled, 0.0), axis=0, keepdims=True))
    return jnp.concatenate(rows, axis=1)


def middle_kernel(capacity, received, flux_x, flux_y, coef_x_ref, coef_y_ref, out):
    fields, cells_x, cells_y, depth = out.shape
    rows_block = cells_x * cells_y
    shape = (cells_y, depth)
    got = received[...]
    slots = got.shape[0] * capacity
    flat = [flat_slots(got, f, capacity) for f in range(fields + 1)]
    cell = flat[fields].astype(jnp.int32)
    row_hot = lax.broadcasted_iota(jnp.int32, (rows_block, slots), 0) == cell // depth
    depth_hot = jnp.where(
        lax.broadcasted_iota(jnp.int32, (depth, slots), 0) == cell % depth, 1.0, 0.0
    ).astype(BF16)
    for f in range(fields):
        spread = jnp.where(row_hot, flat[f], 0.0)
        top = spread.astype(BF16)
        rest = (spread - top.astype(F32)).astype(BF16)
        both = lax.dot_general(
            jnp.concatenate([top, rest], axis=0), depth_hot, NT, preferred_element_type=F32
        )
        forcing = both[:rows_block] + both[rows_block:]
        for i in range(cells_x):
            out[f, i] = forcing[i * cells_y : (i + 1) * cells_y]

    coef_x = coef_x_ref[...]
    coef_y = coef_y_ref[...]

    def at_x(row, i):
        return jnp.broadcast_to(coef_x[row : row + 1, i : i + 1], shape)

    wide = [jnp.broadcast_to(coef_y[:, row : row + 1], shape) for row in range(7)]
    station = lax.broadcasted_iota(jnp.int32, shape, 0)

    for f in range(fields):
        stations = [flux_x[f, i] for i in range(cells_x)]
        before = [None] * cells_x
        after = [None] * cells_x
        for i in range(1, cells_x):
            term = at_x(2, i - 1) * stations[i - 1]
            before[i] = term if i == 1 else before[i - 1] + term
        for i in range(cells_x - 2, -1, -1):
            term = at_x(3, i + 1) * stations[i + 1]
            after[i] = term if i == cells_x - 2 else after[i + 1] + term
        for i in range(cells_x):
            total = at_x(4, i) * stations[i]
            if i > 0:
                total = total + at_x(0, i) * before[i] + at_x(5, i) * stations[i - 1]
            if i < cells_x - 1:
                total = total + at_x(1, i) * after[i] + at_x(6, i) * stations[i + 1]

            line = flux_y[f, i]
            below = wide[2] * line
            above = wide[3] * line
            low = jnp.where(station >= 1, pltpu.roll(line, 1, 0), 0.0)
            high = jnp.where(station < cells_y - 1, pltpu.roll(line, cells_y - 1, 0), 0.0)
            below = jnp.where(station >= 1, pltpu.roll(below, 1, 0), 0.0)
            above = jnp.where(station < cells_y - 1, pltpu.roll(above, cells_y - 1, 0), 0.0)
            step = 1
            while step < cells_y:
                below = below + jnp.where(station >= step, pltpu.roll(below, step, 0), 0.0)
                above = above + jnp.where(
                    station < cells_y - step, pltpu.roll(above, cells_y - step, 0), 0.0
                )
                step *= 2
            total = total + wide[0] * below + wide[1] * above
            total = total + wide[4] * line + wide[5] * low + wide[6] * high
            out[f, i] = out[f, i] - total


def last_kernel(base, ends_x, ends_y, coef_x_ref, coef_y_ref, out):
    fields, cells_x, cells_y, depth = out.shape
    shape = (cells_y, depth)
    coef_x = coef_x_ref[...]
    coef_y = coef_y_ref[...]

    def at_x(row, i):
        return jnp.broadcast_to(coef_x[row : row + 1, i : i + 1], shape)

    p_y = jnp.broadcast_to(coef_y[:, 0:1], shape)
    u_y = jnp.broadcast_to(coef_y[:, 1:2], shape)
    station = lax.broadcasted_iota(jnp.int32, shape, 0)
    low_y = jnp.where(station == 0, jnp.broadcast_to(coef_y[:, 5:6], shape), 0.0)
    high_y = jnp.where(station == cells_y - 1, jnp.broadcast_to(coef_y[:, 6:7], shape), 0.0)
    for i in range(cells_x):
        p_x, u_x = at_x(0, i), at_x(1, i)
        for f in range(fields):
            total = p_x * ends_x[0, f] + u_x * ends_x[1, f]
            if i == 0:
                total = total + at_x(5, i) * ends_x[2, f]
            if i == cells_x - 1:
                total = total + at_x(6, i) * ends_x[3, f]
            line = f * cells_x + i
            entering = ends_y[0, line : line + 1]
            leaving = ends_y[1, line : line + 1]
            left = ends_y[2, line : line + 1]
            right = ends_y[3, line : line + 1]
            total = total + p_y * entering + u_y * leaving + low_y * left + high_y * right
            out[f, i] = base[f, i] - total


def swept(own, axis, mirrored):
    count = lax.axis_size(axis)
    place = lax.axis_index(axis)
    zero = jnp.zeros_like(own[0])
    below, above, left, right = zero, zero, zero, zero
    sum_t, sum_u, first, last = own[0], own[1], own[2], own[3]
    bits = max(1, count.bit_length() - 1)
    for bit in range(bits):
        size = 1 << bit
        turn = 2 * size - 1 if mirrored else size
        pairs = [(i, i ^ turn) for i in range(count)]
        upper = (place // size) % 2 == 1
        inner = place % size
        if bit == bits - 1:
            sent = jnp.stack([jnp.where(upper, sum_u, sum_t), jnp.where(upper, first, last)])
            got = lax.ppermute(sent, axis, pairs)
            got_t = got_u = got[0]
            got_first = got_last = got[1]
        elif mirrored:
            sent = jnp.stack([sum_t, sum_u, jnp.where(upper, first, last)])
            got = lax.ppermute(sent, axis, pairs)
            got_t, got_u = got[0], got[1]
            got_first = got_last = got[2]
        else:
            got = lax.ppermute(jnp.stack([sum_t, sum_u, first, last]), axis, pairs)
            got_t, got_u, got_first, got_last = got[0], got[1], got[2], got[3]
        below = jnp.where(upper, below + got_t, below)
        above = jnp.where(upper, above, above + got_u)
        left = jnp.where(upper & (inner == 0), got_last, left)
        right = jnp.where(jnp.logical_not(upper) & (inner == size - 1), got_first, right)
        if bit < bits - 1:
            sum_t, sum_u = sum_t + got_t, sum_u + got_u
            if not mirrored:
                first, last = jnp.where(upper, got_first, first), jnp.where(upper, last, got_last)
    return jnp.stack([below, above, left, right])


def on_device(
    adjoint, jac_x, jac_y, alpha_x, metric_x, alpha_y, metric_y, surf_values, surf_cells, surf_owner
):
    fields, cells_x, cells_y, depth = adjoint.shape
    points = surf_values.shape[2]
    devices = lax.axis_size("gx") * lax.axis_size("gy")
    capacity = max(4, 2 * points // devices)
    sizes = (alpha_x.shape[0], alpha_y.shape[0])
    lanes = -(-max(sizes) // 128) * 128
    vmem = pl.BlockSpec(memory_space=pltpu.VMEM)
    far = pl.BlockSpec(memory_space=pl.ANY)

    def array(*shape):
        return jax.ShapeDtypeStruct(shape, F32)

    pack, flux_x, flux_y, own_x, own_y, coef_x, coef_y = pl.pallas_call(
        functools.partial(first_kernel, sizes, devices, capacity),
        in_specs=[vmem] * 7 + [far] * 3,
        out_specs=[vmem] * 7,
        out_shape=[
            array(devices, (fields + 1) * capacity),
            array(*adjoint.shape),
            array(*adjoint.shape),
            array(4, fields, cells_y, depth),
            array(4, fields * cells_x, depth),
            array(8, 128),
            array(cells_y, 128),
        ],
        scratch_shapes=[
            pltpu.VMEM(adjoint.shape, F32),
            pltpu.VMEM(jac_x.shape, BF16),
            pltpu.VMEM(jac_y.shape, BF16),
            pltpu.VMEM((8, lanes), F32),
            pltpu.SemaphoreType.DMA((3,)),
        ],
        compiler_params=pltpu.CompilerParams(vmem_limit_bytes=24 << 20),
        name="flux_and_sums",
    )(
        alpha_x.reshape(1, -1),
        alpha_y.reshape(1, -1),
        metric_x.reshape(1, -1),
        metric_y.reshape(1, -1),
        surf_values[0],
        surf_cells,
        surf_owner.reshape(1, points),
        adjoint,
        jac_x,
        jac_y,
    )
    received = lax.all_to_all(pack, ("gx", "gy"), 0, 0, tiled=True)
    ends_x = swept(own_x, "gx", True)
    ends_y = swept(own_y, "gy", False)
    base = pl.pallas_call(
        functools.partial(middle_kernel, capacity),
        in_specs=[vmem] * 5,
        out_specs=vmem,
        out_shape=array(*adjoint.shape),
        compiler_params=pltpu.CompilerParams(vmem_limit_bytes=24 << 20),
        name="forcing_and_block_part",
    )(received, flux_x, flux_y, coef_x, coef_y)
    return pl.pallas_call(
        last_kernel,
        in_specs=[vmem] * 5,
        out_specs=vmem,
        out_shape=array(*adjoint.shape),
        compiler_params=pltpu.CompilerParams(vmem_limit_bytes=24 << 20),
        name="far_part",
    )(base, ends_x, ends_y, coef_x, coef_y)


def solution(mesh):
    in_specs = (
        P(None, "gx", "gy", None),
        P(None, None, "gx", "gy", None),
        P(None, None, "gx", "gy", None),
        P(),
        P("gx"),
        P(),
        P("gy"),
        P(("gx", "gy"), None, None),
        P(("gx", "gy"), None),
        P(("gx", "gy"), None, None),
    )
    out_specs = P(None, "gx", "gy", None)
    return jax.shard_map(
        on_device, mesh=mesh, in_specs=in_specs, out_specs=out_specs, check_vma=False
    )
```

time: 678 us -> 37.7 us (0.06)
  local copies, waits for them, and re-layouts: 230 us -> 5.34 us
  loops' own time: 181 us -> 0 us
  other arithmetic: 116 us -> 0.24 us
  blocking collectives: 73.6 us -> 0 us
  between operations: 52.6 us -> 0.23 us
  waiting for transfers between devices: 0.02 us -> 11.4 us
    dynamic_slice x318 -> x0, local copies, waits for them, and re-layouts: 186 us -> none  [the longest x288 171 us: coefficients(): lax.scan(advance, jnp.zeros((), jnp.float32), (lower_diag, upper_diag))]
    another operation x6 -> x0, loops' own time: 181 us -> none  [the longest x2 180 us: coefficients(): lax.scan(advance, jnp.zeros((), jnp.float32), (lower_diag, upper_diag))]
    unnamed x28 -> x0, other arithmetic: 46.6 us -> none
    all_gather x4 -> x0, blocking collectives: 46.3 us -> none  [the longest x1 14.6 us: solve_line(): lax.all_gather(last_e[None], 'gy', axis=0, tiled=True)]
    sub x3 -> x0, other arithmetic: 34.6 us -> none  [the longest x2 34.1 us: solve_line(): back_e[offset] = eliminated[offset] - ratio_b[offset] * back_e[offset + 1]]
    dynamic_update_slice x288 -> x0, local copies, waits for them, and re-layouts: 31.2 us -> none  [coefficients(): lax.scan(advance, jnp.zeros((), jnp.float32), (lower_diag, upper_diag))]
    unnamed x2 -> x0, blocking collectives: 27.3 us -> none
    add x29 -> x1, other arithmetic: 16.7 us -> 0.02 us  [swept(): sum_t, sum_u = (sum_t + got_t, sum_u + got_u)]
  transfers between devices with their start and end apart: 6 -> 6, of which waited for: 0 -> 3; matrix products, arithmetic and copies ran while one was open for 46% -> 2% of each run, Pallas kernels for 0% -> 4%
where the time goes in v1:
time: 37.7 us; the launch traced here: 37.4 us
  starting transfers between devices  15.8 us (42%)
  waiting for transfers between devices  11.4 us (30%)
  local copies, waits for them, and re-layouts  5.34 us (14%)
  Pallas kernels  4.34 us (12%)
    ppermute x3, waiting for transfers between devices, swept(): got = lax.ppermute(sent, axis, pairs)  7.95 us
    all_to_all x1, starting transfers between devices, on_device(): received = lax.all_to_all(pack, ('gx', 'gy'), 0, 0, tiled=True)  6.96 us
    ppermute x3, starting transfers between devices, swept(): got = lax.ppermute(sent, axis, pairs)  6.5 us
    unnamed x20, local copies, waits for them, and re-layouts  4.68 us
    ppermute x2, waiting for transfers between devices, swept(): got = lax.ppermute(jnp.stack([sum_t, sum_u, first, last]), axis, pairs)  3.47 us
    ppermute x2, starting transfers between devices, swept(): got = lax.ppermute(jnp.stack([sum_t, sum_u, first, last]), axis, pairs)  2.35 us
    pallas_call x1, Pallas kernels, on_device(): pl.pallas_call(functools.partial(first_kernel, sizes, devices, capacity),...  1.86 us
    pallas_call x1, Pallas kernels, on_device(): pl.pallas_call(functools.partial(middle_kernel, capacity), in_specs=[vmem...  1.5 us
  transfers between devices with their start and end apart: 6, of which 3 were waited for; matrix products, arithmetic and copies ran while one was open for 2% of the time, Pallas kernels for 4%

profile of v1, /device:TPU:0, one launch (start us, length us, event | category | flops | bytes accessed | tf_op | source)
XLA Modules:
  0.0 37.4 jit_solution(6852628157144450902)
XLA Ops:
  0.0 0.7 %copy.17 = f32[1,5,512]{2,1,0:T(8,128)S(1)} copy(f32[1,5,512]{2,0,1:T(1,128)} %param.17) | data formatting | bytes 20480
  0.7 0.0 copy-start.8
  0.7 0.0 copy-start.4
  0.7 0.0 copy-start.3
  0.7 0.0 copy-start.5
  0.7 0.0 copy-start.6
  0.7 0.0 copy-start.7
  0.7 0.6 %copy-done.8 = f32[16]{0:T(128)S(1)} copy-done((f32[16]{0:T(128)S(1)}, f32[16]{0:T(128)}, u32[]{:S(2)}) %copy-start.8) | copy-done | bytes 88
  1.4 0.0 copy-done.4
  1.4 0.0 copy-done.3
  1.4 0.0 copy-done.5
  1.4 0.0 copy-done.6
  1.4 0.0 copy-done.7
  1.4 0.0 copy-start
  1.4 1.1 %copy-done = bf16[5,5,4,16,256]{4,3,2,1,0:T(8,128)(2,1)S(1)} copy-done((bf16[5,5,4,16,256]{4,3,2,1,0:T(8,128)(2,1)S(1)}, bf16[5,5,4,16,256]{4,3,2,1,0:T(8,128)(2,1)}, u32[]{:S(2)}) %copy-start) | copy-done | bytes 819224
  2.6 0.0 copy-start.1
  2.6 1.1 %copy-done.1 = bf16[5,5,4,16,256]{4,3,2,1,0:T(8,128)(2,1)S(1)} copy-done((bf16[5,5,4,16,256]{4,3,2,1,0:T(8,128)(2,1)S(1)}, bf16[5,5,4,16,256]{4,3,2,1,0:T(8,128)(2,1)}, u32[]{:S(2)}) %copy-start.1) | copy-done | bytes 819224
  3.7 0.0 copy-start.2
  3.7 1.0 %copy-done.2 = f32[5,4,16,256]{3,2,1,0:T(8,128)S(1)} copy-done((f32[5,4,16,256]{3,2,1,0:T(8,128)S(1)}, f32[5,4,16,256]{3,2,1,0:T(8,128)}, u32[]{:S(2)}) %copy-start.2) | copy-done | bytes 327704
  4.7 1.9 %flux_and_sums.1 = (f32[32,192]{1,0:T(8,128)S(1)}, f32[5,4,16,256]{3,2,1,0:T(8,128)S(1)}, f32[5,4,16,256]{3,2,1,0:T(8,128)S(1)}, f32[4,5,16,256]{3,2,1,0:T(8,128...) custom-call(f32[1,16]{1,0:T(1,128)S(1)} %bitcast.16, f32[1,128]{1,0:T(1,128)S(1)} %bitcast.17, ...), custom_call_target="tpu_custom_call" | custom-call | tf_op jit(solution)/shard_map/flux_and_sums/pallas_call | solution.py:396
  6.6 0.5 %collective-permute-start.2 = (f32[4,20,256]{2,1,0:T(8,128)S(1)}, f32[4,20,256]{2,1,0:T(8,128)S(1)}, u32[]{:S(2)}, u32[]{:S(2)}) collective-permute-start(f32[4,20,256]{2,1,0:T(8,128)S(1)} %get-tuple-element.18), channel_id=1, source_target_pairs={{0,1},{1,0},{2,3},{3,2},{4,5},{5,4},{6,7},{7,6},{8,9},{9,8},{10,11... | collective-permute-start | bytes 245768 | tf_op jit(solution)/shard_map/ppermute | solution.py:368
  7.1 0.6 %copy.11 = f32[32,1,192]{2,1,0:T(1,128)} copy(f32[32,1,192]{2,0,1:T(8,128)S(1)} %bitcast.14) | data formatting | bytes 49152 | tf_op jit(solution)/shard_map/all_to_all | solution.py:430
  7.7 7.0 %all-to-all-start = ((f32[32,1,192]{2,1,0:T(1,128)}), f32[32,1,192]{2,1,0:T(1,128)S(1)}, u32[]{:S(2)}, u32[]{:S(2)}) async-start(f32[32,1,192]{2,1,0:T(1,128)} %copy.11), calls=%async_computation | async-start | bytes 65536 | tf_op jit(solution)/shard_map/all_to_all | solution.py:430
  14.7 0.0 collective-permute-done.2
  14.8 1.8 %collective-permute-start.3 = (f32[4,20,256]{2,1,0:T(8,128)S(1)}, f32[4,20,256]{2,1,0:T(8,128)S(1)}, u32[]{:S(2)}, u32[]{:S(2)}) collective-permute-start(f32[4,20,256]{2,1,0:T(8,128)S(1)} %pad_maximum_fusion.3), channel_id=1, source_target_pairs={{0,2},{1,3},{2,0},{3,1},{4,6},{5,7},{6,4},{7,5},{8,10},{9,11},{10,... | collective-permute-start | bytes 245768 | tf_op jit(solution)/shard_map/ppermute | solution.py:368
  16.7 3.5 %collective-permute-done.3 = f32[4,20,256]{2,1,0:T(8,128)S(1)} collective-permute-done((f32[4,20,256]{2,1,0:T(8,128)S(1)}, f32[4,20,256]{2,1,0:T(8,128)S(1)}, u32[]{:S(2)}, u32[]{:S(2)}) %collective-permute-start.3) | collective-permute-done | bytes 81952 | tf_op jit(solution)/shard_map/ppermute | solution.py:368
  20.2 2.5 %collective-permute-start.4 = (f32[2,20,256]{2,1,0:T(8,128)S(1)}, f32[2,20,256]{2,1,0:T(8,128)S(1)}, u32[]{:S(2)}, u32[]{:S(2)}) collective-permute-start(f32[2,20,256]{2,1,0:T(8,128)S(1)} %pad_maximum_fusion.5), channel_id=1, source_target_pairs={{0,4},{1,5},{2,6},{3,7},{4,0},{5,1},{6,2},{7,3},{8,12},{9,13},{10,... | collective-permute-start | bytes 122888 | tf_op jit(solution)/shard_map/ppermute | solution.py:359
  22.7 1.5 %collective-permute-start = (f32[3,5,16,256]{3,2,1,0:T(8,128)S(1)}, f32[3,5,16,256]{3,2,1,0:T(8,128)S(1)}, u32[]{:S(2)}, u32[]{:S(2)}) collective-permute-start(f32[3,5,16,256]{3,2,1,0:T(8,128)S(1)} %pad_maximum_fusion.1), channel_id=1, source_target_pairs={{0,8},{8,0},{16,24},{24,16},{1,9},{9,1},{17,25},{25,17},{2,10},{10... | collective-permute-start | bytes 737288 | tf_op jit(solution)/shard_map/ppermute | solution.py:364
  24.3 0.0 all-to-all-done
  24.3 1.5 %forcing_and_block_part.1.base = f32[5,4,16,256]{3,2,1,0:T(8,128)S(1)} custom-call(f32[32,192]{1,0:T(8,128)S(1)} %bitcast.12, f32[5,4,16,256]{3,2,1,0:T(8,128)S(1)} %get-tuple-element.13.flux_x, f32[5,4,16,256]{3,2,1,0:T(8,128)S(1)} %get-tuple-element.14.flux_y, f32[8,128]{1,0:T(8,128)S(1)} %get-tuple-element.15.coef_x_ref, ...), custom_call_target="tpu_custom_call" | custom-call | tf_op jit(solution)/shard_map/forcing_and_block_part/pallas_call | solution.py:433
  25.8 0.0 collective-permute-done.4
  25.8 4.1 %collective-permute-done = f32[3,5,16,256]{3,2,1,0:T(8,128)S(1)} collective-permute-done((f32[3,5,16,256]{3,2,1,0:T(8,128)S(1)}, f32[3,5,16,256]{3,2,1,0:T(8,128)S(1)}, u32[]{:S(2)}, u32[]{:S(2)}) %collective-permute-start) | collective-permute-done | bytes 245792 | tf_op jit(solution)/shard_map/ppermute | solution.py:364
  30.0 2.5 %collective-permute-start.1 = (f32[2,5,16,256]{3,2,1,0:T(8,128)S(1)}, f32[2,5,16,256]{3,2,1,0:T(8,128)S(1)}, u32[]{:S(2)}, u32[]{:S(2)}) collective-permute-start(f32[2,5,16,256]{3,2,1,0:T(8,128)S(1)} %pad_maximum_fusion.2), channel_id=1, source_target_pairs={{0,24},{8,16},{16,8},{24,0},{1,25},{9,17},{17,9},{25,1},{2,26},{10... | collective-permute-start | bytes 491528 | tf_op jit(solution)/shard_map/ppermute | solution.py:359
  32.5 3.8 %collective-permute-done.1 = f32[2,5,16,256]{3,2,1,0:T(8,128)S(1)} collective-permute-done((f32[2,5,16,256]{3,2,1,0:T(8,128)S(1)}, f32[2,5,16,256]{3,2,1,0:T(8,128)S(1)}, u32[]{:S(2)}, u32[]{:S(2)}) %collective-permute-start.1) | collective-permute-done | bytes 163872 | tf_op jit(solution)/shard_map/ppermute | solution.py:359
  36.4 1.0 %far_part.1 = f32[5,4,16,256]{3,2,1,0:T(8,128)} custom-call(f32[5,4,16,256]{3,2,1,0:T(8,128)S(1)} %forcing_and_block_part.1.base, f32[4,5,16,256]{3,2,1,0:T(8,128)S(1)} %pad_maximum_fusion.ends_x, f32[4,20,256]{2,1,0:T(8,128)S(1)} %pad_maximum_fusion.4.ends_y, f32[8,128]{1,0:T(8,128)S(1)} %get-tuple-element.15.coef_x_ref, ...), custom_call_target="tpu_custom_call" | custom-call | tf_op jit(solution)/shard_map/far_part/pallas_call | solution.py:441
  (15 shorter events, 0.3 us)
Async XLA Ops:
  0.7 0.7 %copy-start.8 = (f32[16]{0:T(128)S(1)}, f32[16]{0:T(128)}, u32[]{:S(2)}) copy-start(f32[16]{0:T(128)} %param.16) | copy-start | bytes 196
  0.7 0.7 %copy-start.4 = (s32[1,512,1]{1,2,0:T(1,128)S(1)}, s32[1,512,1]{1,2,0:T(1,128)}, u32[]{:S(2)}) copy-start(s32[1,512,1]{1,2,0:T(1,128)} %param.19) | copy-start | bytes 6148
  0.7 0.7 %copy-start.3 = (s32[1,512]{1,0:T(1,128)S(1)}, s32[1,512]{1,0:T(1,128)}, u32[]{:S(2)}) copy-start(s32[1,512]{1,0:T(1,128)} %cells.1) | copy-start | bytes 6148
  0.7 0.7 %copy-start.5 = (f32[16]{0:T(128)S(1)}, f32[16]{0:T(128)}, u32[]{:S(2)}) copy-start(f32[16]{0:T(128)} %param.13) | copy-start | bytes 196
  0.7 0.7 %copy-start.6 = (f32[128]{0:T(128)S(1)}, f32[128]{0:T(128)}, u32[]{:S(2)}) copy-start(f32[128]{0:T(128)} %param.15) | copy-start | bytes 1540
  0.7 0.7 %copy-start.7 = (f32[4]{0:T(128)S(1)}, f32[4]{0:T(128)}, u32[]{:S(2)}) copy-start(f32[4]{0:T(128)} %param.14) | copy-start | bytes 52
  1.4 1.1 %copy-start = (bf16[5,5,4,16,256]{4,3,2,1,0:T(8,128)(2,1)S(1)}, bf16[5,5,4,16,256]{4,3,2,1,0:T(8,128)(2,1)}, u32[]{:S(2)}) copy-start(bf16[5,5,4,16,256]{4,3,2,1,0:T(8,128)(2,1)} %jac_x.1) | copy-start | bytes 2457604
  2.6 1.1 %copy-start.1 = (bf16[5,5,4,16,256]{4,3,2,1,0:T(8,128)(2,1)S(1)}, bf16[5,5,4,16,256]{4,3,2,1,0:T(8,128)(2,1)}, u32[]{:S(2)}) copy-start(bf16[5,5,4,16,256]{4,3,2,1,0:T(8,128)(2,1)} %jac_y.1) | copy-start | bytes 2457604
  3.7 1.0 %copy-start.2 = (f32[5,4,16,256]{3,2,1,0:T(8,128)S(1)}, f32[5,4,16,256]{3,2,1,0:T(8,128)}, u32[]{:S(2)}) copy-start(f32[5,4,16,256]{3,2,1,0:T(8,128)} %adjoint.1) | copy-start | bytes 983044
  6.6 8.2 %collective-permute-start.2 = (f32[4,20,256]{2,1,0:T(8,128)S(1)}, f32[4,20,256]{2,1,0:T(8,128)S(1)}, u32[]{:S(2)}, u32[]{:S(2)}) collective-permute-start(f32[4,20,256]{2,1,0:T(8,128)S(1)} %get-tuple-element.18), channel_id=1, source_target_pairs={{0,1},{1,0},{2,3},{3,2},{4,5},{5,4},{6,7},{7,6},{8,9},{9,8},{10,11... | collective-permute-start | bytes 245768 | tf_op jit(solution)/shard_map/ppermute | solution.py:368
  7.7 16.5 %all-to-all-start = ((f32[32,1,192]{2,1,0:T(1,128)}), f32[32,1,192]{2,1,0:T(1,128)S(1)}, u32[]{:S(2)}, u32[]{:S(2)}) async-start(f32[32,1,192]{2,1,0:T(1,128)} %copy.11), calls=%async_computation | async-start | bytes 65536 | tf_op jit(solution)/shard_map/all_to_all | solution.py:430
  14.8 5.4 %collective-permute-start.3 = (f32[4,20,256]{2,1,0:T(8,128)S(1)}, f32[4,20,256]{2,1,0:T(8,128)S(1)}, u32[]{:S(2)}, u32[]{:S(2)}) collective-permute-start(f32[4,20,256]{2,1,0:T(8,128)S(1)} %pad_maximum_fusion.3), channel_id=1, source_target_pairs={{0,2},{1,3},{2,0},{3,1},{4,6},{5,7},{6,4},{7,5},{8,10},{9,11},{10,... | collective-permute-start | bytes 245768 | tf_op jit(solution)/shard_map/ppermute | solution.py:368
  20.2 5.6 %collective-permute-start.4 = (f32[2,20,256]{2,1,0:T(8,128)S(1)}, f32[2,20,256]{2,1,0:T(8,128)S(1)}, u32[]{:S(2)}, u32[]{:S(2)}) collective-permute-start(f32[2,20,256]{2,1,0:T(8,128)S(1)} %pad_maximum_fusion.5), channel_id=1, source_target_pairs={{0,4},{1,5},{2,6},{3,7},{4,0},{5,1},{6,2},{7,3},{8,12},{9,13},{10,... | collective-permute-start | bytes 122888 | tf_op jit(solution)/shard_map/ppermute | solution.py:359
  22.7 7.2 %collective-permute-start = (f32[3,5,16,256]{3,2,1,0:T(8,128)S(1)}, f32[3,5,16,256]{3,2,1,0:T(8,128)S(1)}, u32[]{:S(2)}, u32[]{:S(2)}) collective-permute-start(f32[3,5,16,256]{3,2,1,0:T(8,128)S(1)} %pad_maximum_fusion.1), channel_id=1, source_target_pairs={{0,8},{8,0},{16,24},{24,16},{1,9},{9,1},{17,25},{25,17},{2,10},{10... | collective-permute-start | bytes 737288 | tf_op jit(solution)/shard_map/ppermute | solution.py:364
  30.0 6.3 %collective-permute-start.1 = (f32[2,5,16,256]{3,2,1,0:T(8,128)S(1)}, f32[2,5,16,256]{3,2,1,0:T(8,128)S(1)}, u32[]{:S(2)}, u32[]{:S(2)}) collective-permute-start(f32[2,5,16,256]{3,2,1,0:T(8,128)S(1)} %pad_maximum_fusion.2), channel_id=1, source_target_pairs={{0,24},{8,16},{16,8},{24,0},{1,25},{9,17},{17,9},{25,1},{2,26},{10... | collective-permute-start | bytes 491528 | tf_op jit(solution)/shard_map/ppermute | solution.py:359

commit v2 on v1

--- a/solution.py
+++ b/solution.py
@@ -99,7 +99,7 @@
 
 
 def packed_points(values, cells, owners, devices, capacity):
-    fields, points = values.shape
+    points = owners.shape[1]
     owner_of = lax.broadcasted_iota(jnp.int32, (devices, points), 0)
     hot = jnp.where(owner_of == owners, 1.0, 0.0)
     width = 128
@@ -118,53 +118,47 @@
         carried = carried + jnp.sum(piece, axis=1, keepdims=True)
     rank = jnp.concatenate(ranks, axis=1).astype(jnp.int32)
     slot = lax.broadcasted_iota(jnp.int32, (capacity, points), 0) == rank
-    rows = [jnp.where(slot, values[f : f + 1], 0.0) for f in range(fields)]
+    rows = [jnp.where(slot, row, 0.0) for row in values]
     rows.append(jnp.where(slot, cells.astype(F32), 0.0))
     spread = jnp.concatenate(rows, axis=0)
     top = spread.astype(BF16)
     rest = (spread - top.astype(F32)).astype(BF16)
     hot = hot.astype(BF16)
+    spare = -spread.shape[0] % 128
+    if spare:
+        top = jnp.concatenate([top, jnp.zeros((spare, points), BF16)], axis=0)
+        rest = jnp.concatenate([rest, jnp.zeros((spare, points), BF16)], axis=0)
     return lax.dot_general(hot, top, NT, preferred_element_type=F32) + lax.dot_general(
         hot, rest, NT, preferred_element_type=F32
     )
 
 
-def first_kernel(
-    sizes,
-    devices,
-    capacity,
-    alpha_x,
-    alpha_y,
-    metric_x,
-    metric_y,
-    values,
-    cells,
-    owners,
-    adjoint,
-    jac_x,
-    jac_y,
-    pack_out,
-    flux_x_out,
-    flux_y_out,
-    send_x,
-    send_y,
-    coef_x_out,
-    coef_y_out,
-    adj,
-    jx,
-    jy,
-    alpha_s,
-    sems,
-):
+def fetch(sources, targets, sems):
     copies = [
         pltpu.make_async_copy(source, target, sems.at[number])
-        for number, (source, target) in enumerate(((adjoint, adj), (jac_x, jx), (jac_y, jy)))
+        for number, (source, target) in enumerate(zip(sources, targets))
     ]
     for copy in copies:
         copy.start()
-    fields, cells_x, cells_y, depth = adj.shape
+    return copies
+
+
+def points_kernel(sizes, devices, capacity, *refs):
+    sources, refs = refs[:7], refs[7:]
+    pack, coef_x_out, coef_y_out = refs[:3]
+    targets, alpha_s, sems = refs[3:10], refs[10], refs[11]
+    alpha_x, alpha_y, metric_x, metric_y, values, cells, owners = targets
+    for copy in fetch(sources, targets, sems):
+        copy.wait()
+    fields = values.shape[0]
+    packed = packed_points(
+        [values[f] for f in range(fields)], cells[...], owners[...], devices, capacity
+    )
+    for device in range(devices):
+        pack[device] = packed[device : device + 1]
+
     lanes = alpha_s.shape[1]
-
+    cells_x, cells_y = metric_x.shape[1], metric_y.shape[1]
     alpha_s[...] = jnp.full(alpha_s.shape, 0.5, F32)
     alpha_s[0:1, 0 : sizes[0]] = alpha_x[...]
     alpha_s[1:2, 0 : sizes[1]] = alpha_y[...]
@@ -182,11 +176,18 @@
     coef_x = coef_x * jnp.where(scaled, gain_x, 1.0)
     coef_y = coef_y * jnp.where(scaled, gain_y, 1.0)
     coef_x_out[...] = coef_x
-    columns_y = jnp.concatenate([coef_y, jnp.zeros((120, 128), F32)], axis=0).T[:cells_y]
-    coef_y_out[...] = columns_y
-
-    pack_out[...] = packed_points(values[...], cells[...], owners[...], devices, capacity)
-
+    coef_y_out[...] = jnp.concatenate([coef_y, jnp.zeros((120, 128), F32)], axis=0).T[:cells_y]
+
+
+def flux_kernel(coef_x_ref, coef_y_ref, adjoint, jac_x, jac_y, *refs):
+    flux_x_out, flux_y_out, send_y = refs[:3]
+    faces, targets, sems = refs[3:-4], refs[-4:-1], refs[-1]
+    adj, jx, jy = targets
+    copies = fetch((adjoint, jac_x, jac_y), targets, sems)
+    fields, cells_x, cells_y, depth = adj.shape
+    coef_x = coef_x_ref[...]
+    columns_y = coef_y_ref[...]
+    lines = fields * cells_x
     shape = (cells_y, depth)
     copies[0].wait()
     copies[1].wait()
@@ -203,13 +204,20 @@
                 if i > 0:
                     term = totals[target][side] + term
                 totals[target][side] = term
-            if i == 0:
-                send_x[2, target] = flux
-            if i == cells_x - 1:
-                send_x[3, target] = flux
-    for target in range(fields):
-        for side in range(2):
-            send_x[side, target] = totals[target][side]
+    for bit, face in enumerate(faces):
+        upper = (lax.axis_index("gx") // (1 << bit)) % 2 == 1
+
+        @pl.when(upper)
+        def _(face=face):
+            for target in range(fields):
+                face[0, target] = totals[target][1]
+                face[1, target] = flux_x_out[target, 0]
+
+        @pl.when(jnp.logical_not(upper))
+        def _(face=face):
+            for target in range(fields):
+                face[0, target] = totals[target][0]
+                face[1, target] = flux_x_out[target, cells_x - 1]
 
     weight_t = jnp.broadcast_to(columns_y[:, 2:3], shape)
     weight_s = jnp.broadcast_to(columns_y[:, 3:4], shape)
@@ -222,10 +230,14 @@
                 flux = flux + jy[k, target, i].astype(F32) * state[k]
             flux_y_out[target, i] = flux
             line = target * cells_x + i
-            send_y[0, line : line + 1] = jnp.sum(weight_t * flux, axis=0, keepdims=True)
-            send_y[1, line : line + 1] = jnp.sum(weight_s * flux, axis=0, keepdims=True)
-            send_y[2, line : line + 1] = flux[0:1]
-            send_y[3, line : line + 1] = flux[cells_y - 1 : cells_y]
+            rows = (
+                jnp.sum(weight_t * flux, axis=0, keepdims=True),
+                jnp.sum(weight_s * flux, axis=0, keepdims=True),
+                flux[0:1],
+                flux[cells_y - 1 : cells_y],
+            )
+            for number, row in enumerate(rows):
+                send_y[number, line : line + 1] = row
 
 
 def flat_slots(received, number, capacity):
@@ -246,14 +258,24 @@
     fields, cells_x, cells_y, depth = out.shape
     rows_block = cells_x * cells_y
     shape = (cells_y, depth)
-    got = received[...]
-    slots = got.shape[0] * capacity
+    senders = received.shape[0]
+    got = jnp.concatenate([received[sender] for sender in range(senders)], axis=0)
+    slots = senders * capacity
     flat = [flat_slots(got, f, capacity) for f in range(fields + 1)]
     cell = flat[fields].astype(jnp.int32)
     row_hot = lax.broadcasted_iota(jnp.int32, (rows_block, slots), 0) == cell // depth
     depth_hot = jnp.where(
         lax.broadcasted_iota(jnp.int32, (depth, slots), 0) == cell % depth, 1.0, 0.0
     ).astype(BF16)
+    coef_x = coef_x_ref[...]
+    coef_y = coef_y_ref[...]
+
+    def at_x(row, i):
+        return jnp.broadcast_to(coef_x[row : row + 1, i : i + 1], shape)
+
+    wide = [jnp.broadcast_to(coef_y[:, row : row + 1], shape) for row in range(7)]
+    station = lax.broadcasted_iota(jnp.int32, shape, 0)
+
     for f in range(fields):
         spread = jnp.where(row_hot, flat[f], 0.0)
         top = spread.astype(BF16)
@@ -262,19 +284,7 @@
             jnp.concatenate([top, rest], axis=0), depth_hot, NT, preferred_element_type=F32
         )
         forcing = both[:rows_block] + both[rows_block:]
-        for i in range(cells_x):
-            out[f, i] = forcing[i * cells_y : (i + 1) * cells_y]
-
-    coef_x = coef_x_ref[...]
-    coef_y = coef_y_ref[...]
-
-    def at_x(row, i):
-        return jnp.broadcast_to(coef_x[row : row + 1, i : i + 1], shape)
-
-    wide = [jnp.broadcast_to(coef_y[:, row : row + 1], shape) for row in range(7)]
-    station = lax.broadcasted_iota(jnp.int32, shape, 0)
-
-    for f in range(fields):
+
         stations = [flux_x[f, i] for i in range(cells_x)]
         before = [None] * cells_x
         after = [None] * cells_x
@@ -307,14 +317,16 @@
                 step *= 2
             total = total + wide[0] * below + wide[1] * above
             total = total + wide[4] * line + wide[5] * low + wide[6] * high
-            out[f, i] = out[f, i] - total
-
-
-def last_kernel(base, ends_x, ends_y, coef_x_ref, coef_y_ref, out):
+            out[f, i] = forcing[i * cells_y : (i + 1) * cells_y] - total
+
+
+def last_kernel(turns, base, ends_y, coef_x_ref, coef_y_ref, *refs):
+    arrived, out = refs[:-1], refs[-1]
     fields, cells_x, cells_y, depth = out.shape
     shape = (cells_y, depth)
     coef_x = coef_x_ref[...]
     coef_y = coef_y_ref[...]
+    place = lax.axis_index("gx")
 
     def at_x(row, i):
         return jnp.broadcast_to(coef_x[row : row + 1, i : i + 1], shape)
@@ -324,48 +336,53 @@
     station = lax.broadcasted_iota(jnp.int32, shape, 0)
     low_y = jnp.where(station == 0, jnp.broadcast_to(coef_y[:, 5:6], shape), 0.0)
     high_y = jnp.where(station == cells_y - 1, jnp.broadcast_to(coef_y[:, 6:7], shape), 0.0)
+    sides = [(place // (1 << (turn.bit_length() - 1))) % 2 == 1 for turn in turns]
     for i in range(cells_x):
         p_x, u_x = at_x(0, i), at_x(1, i)
+        low_x, high_x = at_x(5, i), at_x(6, i)
+        weights = [jnp.where(upper, p_x, u_x) for upper in sides]
         for f in range(fields):
-            total = p_x * ends_x[0, f] + u_x * ends_x[1, f]
-            if i == 0:
-                total = total + at_x(5, i) * ends_x[2, f]
-            if i == cells_x - 1:
-                total = total + at_x(6, i) * ends_x[3, f]
+            total = base[f, i]
+            for turn, upper, weight, got in zip(turns, sides, weights, arrived):
+                total = total - weight * got[0, f]
+                size = 1 << (turn.bit_length() - 1)
+                if turn != 2 * size - 1:
+                    continue
+                if i == 0:
+                    near = upper & (place % size == 0)
+                    total = total - jnp.where(near, low_x, 0.0) * got[1, f]
+                if i == cells_x - 1:
+                    near = jnp.logical_not(upper) & (place % size == size - 1)
+                    total = total - jnp.where(near, high_x, 0.0) * got[1, f]
             line = f * cells_x + i
             entering = ends_y[0, line : line + 1]
             leaving = ends_y[1, line : line + 1]
             left = ends_y[2, line : line + 1]
             right = ends_y[3, line : line + 1]
-            total = total + p_y * entering + u_y * leaving + low_y * left + high_y * right
-            out[f, i] = base[f, i] - total
-
-
-def swept(own, axis, mirrored):
-    count = lax.axis_size(axis)
-    place = lax.axis_index(axis)
+            total = total - (p_y * entering + u_y * leaving + low_y * left + high_y * right)
+            out[f, i] = total
+
+
+def swept_y(own):
+    count = lax.axis_size("gy")
+    place = lax.axis_index("gy")
     zero = jnp.zeros_like(own[0])
     below, above, left, right = zero, zero, zero, zero
     sum_t, sum_u, first, last = own[0], own[1], own[2], own[3]
-    bits = max(1, count.bit_length() - 1)
+    bits = count.bit_length() - 1
     for bit in range(bits):
         size = 1 << bit
-        turn = 2 * size - 1 if mirrored else size
-        pairs = [(i, i ^ turn) for i in range(count)]
+        pairs = [(i, i ^ (size | 1)) for i in range(count)]
         upper = (place // size) % 2 == 1
         inner = place % size
-        if bit == bits - 1:
+        if bit == bits - 1 and bit > 0:
             sent = jnp.stack([jnp.where(upper, sum_u, sum_t), jnp.where(upper, first, last)])
-            got = lax.ppermute(sent, axis, pairs)
+            got = lax.ppermute(sent, "gy", pairs)
             got_t = got_u = got[0]
             got_first = got_last = got[1]
-        elif mirrored:
-            sent = jnp.stack([sum_t, sum_u, jnp.where(upper, first, last)])
-            got = lax.ppermute(sent, axis, pairs)
-            got_t, got_u = got[0], got[1]
-            got_first = got_last = got[2]
         else:
-            got = lax.ppermute(jnp.stack([sum_t, sum_u, first, last]), axis, pairs)
+            sent = own if bit == 0 else jnp.stack([sum_t, sum_u, first, last])
+            got = lax.ppermute(sent, "gy", pairs)
             got_t, got_u, got_first, got_last = got[0], got[1], got[2], got[3]
         below = jnp.where(upper, below + got_t, below)
         above = jnp.where(upper, above, above + got_u)
@@ -373,8 +390,7 @@
         right = jnp.where(jnp.logical_not(upper) & (inner == size - 1), got_first, right)
         if bit < bits - 1:
             sum_t, sum_u = sum_t + got_t, sum_u + got_u
-            if not mirrored:
-                first, last = jnp.where(upper, got_first, first), jnp.where(upper, last, got_last)
+            first, last = jnp.where(upper, got_first, first), jnp.where(upper, last, got_last)
     return jnp.stack([below, above, left, right])
 
 
@@ -383,69 +399,83 @@
 ):
     fields, cells_x, cells_y, depth = adjoint.shape
     points = surf_values.shape[2]
-    devices = lax.axis_size("gx") * lax.axis_size("gy")
+    n_x = lax.axis_size("gx")
+    devices = n_x * lax.axis_size("gy")
     capacity = max(4, 2 * points // devices)
     sizes = (alpha_x.shape[0], alpha_y.shape[0])
     lanes = -(-max(sizes) // 128) * 128
+    width = -(-(fields + 1) * capacity // 128) * 128
     vmem = pl.BlockSpec(memory_space=pltpu.VMEM)
-    far = pl.BlockSpec(memory_space=pl.ANY)
+    hbm = pl.BlockSpec(memory_space=pltpu.HBM)
 
     def array(*shape):
         return jax.ShapeDtypeStruct(shape, F32)
 
-    pack, flux_x, flux_y, own_x, own_y, coef_x, coef_y = pl.pallas_call(
-        functools.partial(first_kernel, sizes, devices, capacity),
-        in_specs=[vmem] * 7 + [far] * 3,
-        out_specs=[vmem] * 7,
-        out_shape=[
-            array(devices, (fields + 1) * capacity),
-            array(*adjoint.shape),
-            array(*adjoint.shape),
-            array(4, fields, cells_y, depth),
-            array(4, fields * cells_x, depth),
-            array(8, 128),
-            array(cells_y, 128),
-        ],
-        scratch_shapes=[
-            pltpu.VMEM(adjoint.shape, F32),
-            pltpu.VMEM(jac_x.shape, BF16),
-            pltpu.VMEM(jac_y.shape, BF16),
-            pltpu.VMEM((8, lanes), F32),
-            pltpu.SemaphoreType.DMA((3,)),
-        ],
-        compiler_params=pltpu.CompilerParams(vmem_limit_bytes=24 << 20),
-        name="flux_and_sums",
-    )(
+    def kept(arrays):
+        return [pltpu.with_memory_space_constraint(a, pltpu.HBM) for a in arrays]
+
+    params = pltpu.CompilerParams(vmem_limit_bytes=24 << 20)
+    small = [
         alpha_x.reshape(1, -1),
         alpha_y.reshape(1, -1),
         metric_x.reshape(1, -1),
         metric_y.reshape(1, -1),
-        surf_values[0],
+        jnp.transpose(surf_values, (1, 0, 2)),
         surf_cells,
         surf_owner.reshape(1, points),
-        adjoint,
-        jac_x,
-        jac_y,
-    )
+    ]
+    pack, coef_x, coef_y = pl.pallas_call(
+        functools.partial(points_kernel, sizes, devices, capacity),
+        in_specs=[hbm] * len(small),
+        out_specs=[vmem] * 3,
+        out_shape=[array(devices, 1, width), array(8, 128), array(cells_y, 128)],
+        scratch_shapes=[pltpu.VMEM(a.shape, a.dtype) for a in small]
+        + [pltpu.VMEM((8, lanes), F32), pltpu.SemaphoreType.DMA((len(small),))],
+        compiler_params=params,
+        name="points_and_coefficients",
+    )(*kept(small))
     received = lax.all_to_all(pack, ("gx", "gy"), 0, 0, tiled=True)
-    ends_x = swept(own_x, "gx", True)
-    ends_y = swept(own_y, "gy", False)
+
+    large = [adjoint, jac_x, jac_y]
+    bits = n_x.bit_length() - 1
+    flux_x, flux_y, own_y, *faces = pl.pallas_call(
+        flux_kernel,
+        in_specs=[vmem] * 2 + [hbm] * len(large),
+        out_specs=[vmem] * (3 + bits),
+        out_shape=[
+            array(*adjoint.shape),
+            array(*adjoint.shape),
+            array(4, fields * cells_x, depth),
+        ]
+        + [array(2, fields, cells_y, depth)] * bits,
+        scratch_shapes=[pltpu.VMEM(a.shape, a.dtype) for a in large]
+        + [pltpu.SemaphoreType.DMA((len(large),))],
+        compiler_params=params,
+        name="flux_and_sums",
+    )(coef_x, coef_y, *kept(large))
+    turns = tuple(range(n_x - 1, 0, -1))
+    arrived = []
+    for turn in turns:
+        bit = turn.bit_length() - 1
+        face = faces[bit] if turn == (2 << bit) - 1 else faces[bit][:1]
+        arrived.append(lax.ppermute(face, "gx", [(i, i ^ turn) for i in range(n_x)]))
+    ends_y = swept_y(own_y)
     base = pl.pallas_call(
         functools.partial(middle_kernel, capacity),
         in_specs=[vmem] * 5,
         out_specs=vmem,
         out_shape=array(*adjoint.shape),
-        compiler_params=pltpu.CompilerParams(vmem_limit_bytes=24 << 20),
+        compiler_params=params,
         name="forcing_and_block_part",
     )(received, flux_x, flux_y, coef_x, coef_y)
     return pl.pallas_call(
-        last_kernel,
-        in_specs=[vmem] * 5,
+        functools.partial(last_kernel, turns),
+        in_specs=[vmem] * (4 + len(turns)),
         out_specs=vmem,
         out_shape=array(*adjoint.shape),
-        compiler_params=pltpu.CompilerParams(vmem_limit_bytes=24 << 20),
+        compiler_params=params,
         name="far_part",
-    )(base, ends_x, ends_y, coef_x, coef_y)
+    )(base, ends_y, coef_x, coef_y, *arrived)
 
 
 def solution(mesh):

time: 37.7 us -> 28.1 us (0.75)
  local copies, waits for them, and re-layouts: 5.34 us -> 0.01 us
  waiting for transfers between devices: 11.4 us -> 6.8 us
  Pallas kernels: 4.34 us -> 6.71 us
  starting transfers between devices: 15.8 us -> 14.1 us
    ppermute x5 -> x6, waiting for transfers between devices: 11.4 us -> 5.52 us  [the longest x3 4.57 us: on_device(): lax.ppermute(face, 'gx', [(i, i ^ turn) for i in range(n_x)])]
    unnamed x20 -> x0, local copies, waits for them, and re-layouts: 4.68 us -> none
    pallas_call x2 -> x3, Pallas kernels: 2.84 us -> 5.2 us  [the longest x1 2.32 us: on_device(): pl.pallas_call(functools.partial(points_kernel, sizes, devices, capacity)...]
    all_to_all x1, starting transfers between devices: 6.96 us -> 4.85 us  [on_device(): received = lax.all_to_all(pack, ('gx', 'gy'), 0, 0, tiled=True)]
    all_to_all x1, waiting for transfers between devices: 0.01 us -> 1.28 us  [on_device(): received = lax.all_to_all(pack, ('gx', 'gy'), 0, 0, tiled=True)]
    all_to_all x1 -> x0, local copies, waits for them, and re-layouts: 0.65 us -> none  [on_device(): received = lax.all_to_all(pack, ('gx', 'gy'), 0, 0, tiled=True)]
    ppermute x5 -> x6, starting transfers between devices: 8.86 us -> 9.26 us  [the longest x3 5.76 us: swept_y(): got = lax.ppermute(sent, 'gy', pairs)]
  transfers between devices with their start and end apart: 6 -> 7, of which waited for: 3 -> 4; matrix products, arithmetic and copies ran while one was open for 2% -> 0% of each run, Pallas kernels for 4% -> 5%
where the time goes in v2:
time: 28.1 us; the launch traced here: 27.9 us
  starting transfers between devices  14.1 us (50%)
  waiting for transfers between devices  6.8 us (24%)
  Pallas kernels  6.71 us (24%)
    ppermute x3, starting transfers between devices, swept_y(): got = lax.ppermute(sent, 'gy', pairs)  5.76 us
    all_to_all x1, starting transfers between devices, on_device(): received = lax.all_to_all(pack, ('gx', 'gy'), 0, 0, tiled=True)  4.85 us
    ppermute x3, waiting for transfers between devices, on_device(): lax.ppermute(face, 'gx', [(i, i ^ turn) for i in range(n_x)])  4.57 us
    ppermute x3, starting transfers between devices, on_device(): lax.ppermute(face, 'gx', [(i, i ^ turn) for i in range(n_x)])  3.5 us
    pallas_call x1, Pallas kernels, on_device(): pl.pallas_call(functools.partial(points_kernel, sizes, devices, capacity)...  2.32 us
    pallas_call x1, Pallas kernels, on_device(): pl.pallas_call(flux_kernel, in_specs=[vmem] * 2 + [hbm] * len(large), out...  1.89 us
    pallas_call x1, Pallas kernels, on_device(): pl.pallas_call(functools.partial(middle_kernel, capacity), in_specs=[vmem...  1.51 us
    all_to_all x1, waiting for transfers between devices, on_device(): received = lax.all_to_all(pack, ('gx', 'gy'), 0, 0, tiled=True)  1.28 us
  transfers between devices with their start and end apart: 7, of which 4 were waited for; matrix products, arithmetic and copies ran while one was open for 0% of the time, Pallas kernels for 5%

profile of v2, /device:TPU:0, one launch (start us, length us, event | category | flops | bytes accessed | tf_op | source)
XLA Modules:
  0.0 27.9 jit_solution(12438323804825055453)
XLA Ops:
  0.0 2.3 %points_and_coefficients.1 = (f32[32,1,256]{2,1,0:T(1,128)}, f32[8,128]{1,0:T(8,128)S(1)}, f32[16,128]{1,0:T(8,128)S(1)}) custom-call(f32[1,16]{1,0:T(1,128)} %bitcast.8, f32[1,128]{1,0:T(1,128)} %bitcast.9, f32[1,4]{1,0:T(1,128)} %bitcast.10, f32[1,16]{1,0:T(1,128)} %bitcast.11, f32[5,1,512]{2,1,0:T(1,128)} %bitcast.6, s32[1,512]{1,0:T(1,128)} %refs_5_.1, ...), custom_call_target="tpu_custom_call" | custom-call | tf_op jit(solution)/shard_map/points_and_coefficients/pallas_call | solution.py:427
  2.3 1.9 %flux_and_sums.1 = (f32[5,4,16,256]{3,2,1,0:T(8,128)S(1)}, f32[5,4,16,256]{3,2,1,0:T(8,128)S(1)}, f32[4,20,256]{2,1,0:T(8,128)S(1)}, f32[2,5,16,256]{3,2,1,0:T(8,128)S(1)}, f32[2,5,16,256]{3,2,1,0:T(8,128)S(1)}) custom-call(f32[8,128]{1,0:T(8,128)S(1)} %get-tuple-element.14.coef_x_ref, f32[16,128]{1,0:T(8,128)S(1)} %get-tuple-element.15.coef_y_ref, ...), custom_call_target="tpu_custom_call" | custom-call | tf_op jit(solution)/shard_map/flux_and_sums/pallas_call | solution.py:441
  4.2 0.5 %collective-permute-start = (f32[4,20,256]{2,1,0:T(8,128)S(1)}, f32[4,20,256]{2,1,0:T(8,128)S(1)}, u32[]{:S(2)}, u32[]{:S(2)}) collective-permute-start(f32[4,20,256]{2,1,0:T(8,128)S(1)} %get-tuple-element.18), channel_id=1, source_target_pairs={{0,1},{1,0},{2,3},{3,2},{4,5},{5,4},{6,7},{7,6},{8,9},{9,8},{10,11... | collective-permute-start | bytes 245768 | tf_op jit(solution)/shard_map/ppermute | solution.py:385
  4.7 0.9 %collective-permute-done = f32[4,20,256]{2,1,0:T(8,128)S(1)} collective-permute-done((f32[4,20,256]{2,1,0:T(8,128)S(1)}, f32[4,20,256]{2,1,0:T(8,128)S(1)}, u32[]{:S(2)}, u32[]{:S(2)}) %collective-permute-start) | collective-permute-done | bytes 81952 | tf_op jit(solution)/shard_map/ppermute | solution.py:385
  5.7 2.8 %collective-permute-start.1 = (f32[4,20,256]{2,1,0:T(8,128)S(1)}, f32[4,20,256]{2,1,0:T(8,128)S(1)}, u32[]{:S(2)}, u32[]{:S(2)}) collective-permute-start(f32[4,20,256]{2,1,0:T(8,128)S(1)} %pad_maximum_fusion), channel_id=1, source_target_pairs={{0,3},{1,2},{2,1},{3,0},{4,7},{5,6},{6,5},{7,4},{8,11},{9,10},{10,... | collective-permute-start | bytes 245768 | tf_op jit(solution)/shard_map/ppermute | solution.py:385
  8.5 4.9 %all-to-all-start = ((f32[32,1,256]{2,1,0:T(1,128)}), f32[32,1,256]{2,1,0:T(1,128)S(1)}, u32[]{:S(2)}, u32[]{:S(2)}) async-start(f32[32,1,256]{2,1,0:T(1,128)} %get-tuple-element.13), calls=%async_computation | async-start | bytes 65536 | tf_op jit(solution)/shard_map/all_to_all | solution.py:437
  13.4 0.0 collective-permute-done.1
  13.4 2.5 %collective-permute-start.2 = (f32[2,20,256]{2,1,0:T(8,128)S(1)}, f32[2,20,256]{2,1,0:T(8,128)S(1)}, u32[]{:S(2)}, u32[]{:S(2)}) collective-permute-start(f32[2,20,256]{2,1,0:T(8,128)S(1)} %pad_maximum_fusion.2), channel_id=1, source_target_pairs={{0,5},{1,4},{2,7},{3,6},{4,1},{5,0},{6,3},{7,2},{8,13},{9,12},{10,... | collective-permute-start | bytes 122888 | tf_op jit(solution)/shard_map/ppermute | solution.py:380
  15.9 2.4 %collective-permute-start.3 = (f32[2,5,16,256]{3,2,1,0:T(8,128)S(1)}, f32[2,5,16,256]{3,2,1,0:T(8,128)S(1)}, u32[]{:S(2)}, u32[]{:S(2)}) collective-permute-start(f32[2,5,16,256]{3,2,1,0:T(8,128)S(1)} %get-tuple-element.19), channel_id=1, source_target_pairs={{0,24},{8,16},{16,8},{24,0},{1,25},{9,17},{17,9},{25,1},{2,26},{10... | collective-permute-start | bytes 491528 | tf_op jit(solution)/shard_map/ppermute | solution.py:461
  18.3 0.5 %collective-permute-start.4 = (f32[1,5,16,256]{3,2,1,0:T(8,128)S(1)}, f32[1,5,16,256]{3,2,1,0:T(8,128)S(1)}, u32[]{:S(2)}, u32[]{:S(2)}) collective-permute-start(f32[1,5,16,256]{3,2,1,0:T(8,128)S(1)} %slice.59), channel_id=1, source_target_pairs={{0,16},{8,24},{16,0},{24,8},{1,17},{9,25},{17,1},{25,9},{2,18},{10... | collective-permute-start | bytes 245768 | tf_op jit(solution)/shard_map/ppermute | solution.py:461
  18.9 0.6 %collective-permute-start.5 = (f32[2,5,16,256]{3,2,1,0:T(8,128)S(1)}, f32[2,5,16,256]{3,2,1,0:T(8,128)S(1)}, u32[]{:S(2)}, u32[]{:S(2)}) collective-permute-start(f32[2,5,16,256]{3,2,1,0:T(8,128)S(1)} %get-tuple-element.20), channel_id=1, source_target_pairs={{0,8},{8,0},{16,24},{24,16},{1,9},{9,1},{17,25},{25,17},{2,10},{10... | collective-permute-start | bytes 491528 | tf_op jit(solution)/shard_map/ppermute | solution.py:461
  19.4 1.3 %all-to-all-done.received = f32[32,1,256]{2,1,0:T(1,128)S(1)} async-done(((f32[32,1,256]{2,1,0:T(1,128)}), f32[32,1,256]{2,1,0:T(1,128)S(1)}, u32[]{:S(2)}, u32[]{:S(2)}) %all-to-all-start) | async-done | bytes 32800 | tf_op jit(solution)/shard_map/all_to_all | solution.py:437
  20.7 1.5 %forcing_and_block_part.1.base = f32[5,4,16,256]{3,2,1,0:T(8,128)S(1)} custom-call(f32[32,1,256]{2,1,0:T(1,128)S(1)} %all-to-all-done.received, f32[5,4,16,256]{3,2,1,0:T(8,128)S(1)} %get-tuple-element.16.flux_x, f32[5,4,16,256]{3,2,1,0:T(8,128)S(1)} %get-tuple-element.17.flux_y, f32[8,128]{1,0:T(8,128)S(1)} %get-tuple-element.14.coef_x_ref, ...), custom_call_target="tpu_custom_call" | custom-call | tf_op jit(solution)/shard_map/forcing_and_block_part/pallas_call | solution.py:463
  22.2 0.0 collective-permute-done.2
  22.3 2.8 %collective-permute-done.4.refs_1_ = f32[1,5,16,256]{3,2,1,0:T(8,128)S(1)} collective-permute-done((f32[1,5,16,256]{3,2,1,0:T(8,128)S(1)}, f32[1,5,16,256]{3,2,1,0:T(8,128)S(1)}, u32[]{:S(2)}, u32[]{:S(2)}) %collective-permute-start.4) | collective-permute-done | bytes 81952 | tf_op jit(solution)/shard_map/ppermute | solution.py:461
  25.1 0.0 collective-permute-done.3.refs_0_
  25.1 1.7 %collective-permute-done.5.refs_2_ = f32[2,5,16,256]{3,2,1,0:T(8,128)S(1)} collective-permute-done((f32[2,5,16,256]{3,2,1,0:T(8,128)S(1)}, f32[2,5,16,256]{3,2,1,0:T(8,128)S(1)}, u32[]{:S(2)}, u32[]{:S(2)}) %collective-permute-start.5) | collective-permute-done | bytes 163872 | tf_op jit(solution)/shard_map/ppermute | solution.py:461
  26.9 1.0 %far_part.1 = f32[5,4,16,256]{3,2,1,0:T(8,128)} custom-call(f32[5,4,16,256]{3,2,1,0:T(8,128)S(1)} %forcing_and_block_part.1.base, f32[4,20,256]{2,1,0:T(8,128)S(1)} %pad_maximum_fusion.1.ends_y, f32[8,128]{1,0:T(8,128)S(1)} %get-tuple-element.14.coef_x_ref, f32[16,128]{1,0:T(8,128)S(1)} %get-tuple-element.15.coef_y_ref, ...), custom_call_target="tpu_custom_call" | custom-call | tf_op jit(solution)/shard_map/far_part/pallas_call | solution.py:471
  (8 shorter events, 0.1 us)
Async XLA Ops:
  4.2 1.5 %collective-permute-start = (f32[4,20,256]{2,1,0:T(8,128)S(1)}, f32[4,20,256]{2,1,0:T(8,128)S(1)}, u32[]{:S(2)}, u32[]{:S(2)}) collective-permute-start(f32[4,20,256]{2,1,0:T(8,128)S(1)} %get-tuple-element.18), channel_id=1, source_target_pairs={{0,1},{1,0},{2,3},{3,2},{4,5},{5,4},{6,7},{7,6},{8,9},{9,8},{10,11... | collective-permute-start | bytes 245768 | tf_op jit(solution)/shard_map/ppermute | solution.py:385
  5.7 7.7 %collective-permute-start.1 = (f32[4,20,256]{2,1,0:T(8,128)S(1)}, f32[4,20,256]{2,1,0:T(8,128)S(1)}, u32[]{:S(2)}, u32[]{:S(2)}) collective-permute-start(f32[4,20,256]{2,1,0:T(8,128)S(1)} %pad_maximum_fusion), channel_id=1, source_target_pairs={{0,3},{1,2},{2,1},{3,0},{4,7},{5,6},{6,5},{7,4},{8,11},{9,10},{10,... | collective-permute-start | bytes 245768 | tf_op jit(solution)/shard_map/ppermute | solution.py:385
  8.5 12.2 %all-to-all-start = ((f32[32,1,256]{2,1,0:T(1,128)}), f32[32,1,256]{2,1,0:T(1,128)S(1)}, u32[]{:S(2)}, u32[]{:S(2)}) async-start(f32[32,1,256]{2,1,0:T(1,128)} %get-tuple-element.13), calls=%async_computation | async-start | bytes 65536 | tf_op jit(solution)/shard_map/all_to_all | solution.py:437
  13.4 8.8 %collective-permute-start.2 = (f32[2,20,256]{2,1,0:T(8,128)S(1)}, f32[2,20,256]{2,1,0:T(8,128)S(1)}, u32[]{:S(2)}, u32[]{:S(2)}) collective-permute-start(f32[2,20,256]{2,1,0:T(8,128)S(1)} %pad_maximum_fusion.2), channel_id=1, source_target_pairs={{0,5},{1,4},{2,7},{3,6},{4,1},{5,0},{6,3},{7,2},{8,13},{9,12},{10,... | collective-permute-start | bytes 122888 | tf_op jit(solution)/shard_map/ppermute | solution.py:380
  15.9 9.2 %collective-permute-start.3 = (f32[2,5,16,256]{3,2,1,0:T(8,128)S(1)}, f32[2,5,16,256]{3,2,1,0:T(8,128)S(1)}, u32[]{:S(2)}, u32[]{:S(2)}) collective-permute-start(f32[2,5,16,256]{3,2,1,0:T(8,128)S(1)} %get-tuple-element.19), channel_id=1, source_target_pairs={{0,24},{8,16},{16,8},{24,0},{1,25},{9,17},{17,9},{25,1},{2,26},{10... | collective-permute-start | bytes 491528 | tf_op jit(solution)/shard_map/ppermute | solution.py:461
  18.3 6.8 %collective-permute-start.4 = (f32[1,5,16,256]{3,2,1,0:T(8,128)S(1)}, f32[1,5,16,256]{3,2,1,0:T(8,128)S(1)}, u32[]{:S(2)}, u32[]{:S(2)}) collective-permute-start(f32[1,5,16,256]{3,2,1,0:T(8,128)S(1)} %slice.59), channel_id=1, source_target_pairs={{0,16},{8,24},{16,0},{24,8},{1,17},{9,25},{17,1},{25,9},{2,18},{10... | collective-permute-start | bytes 245768 | tf_op jit(solution)/shard_map/ppermute | solution.py:461
  18.9 8.0 %collective-permute-start.5 = (f32[2,5,16,256]{3,2,1,0:T(8,128)S(1)}, f32[2,5,16,256]{3,2,1,0:T(8,128)S(1)}, u32[]{:S(2)}, u32[]{:S(2)}) collective-permute-start(f32[2,5,16,256]{3,2,1,0:T(8,128)S(1)} %get-tuple-element.20), channel_id=1, source_target_pairs={{0,8},{8,0},{16,24},{24,16},{1,9},{9,1},{17,25},{25,17},{2,10},{10... | collective-permute-start | bytes 491528 | tf_op jit(solution)/shard_map/ppermute | solution.py:461

commit v3 on v2

v3 whole, which is shorter than its diff:
```python
import functools

import jax
import jax.numpy as jnp
from jax import lax
from jax.experimental import pallas as pl
from jax.experimental.pallas import tpu as pltpu
from jax.sharding import PartitionSpec as P

F32 = jnp.float32
BF16 = jnp.bfloat16
NT = (((1,), (1,)), ((), ()))


def moved(row, by, lane, fill):
    lanes = row.shape[1]
    turned = pltpu.roll(row, by % lanes, 1)
    keep = (lane >= by) if by > 0 else (lane < lanes + by)
    return jnp.where(keep, turned, fill)


def running(parts, lane, direction):
    lanes = lane.shape[1]
    a, b, c, d = parts
    step = 1
    while step < lanes:
        shift = step * direction
        a0, b0 = moved(a, shift, lane, 1.0), moved(b, shift, lane, 0.0)
        c0, d0 = moved(c, shift, lane, 0.0), moved(d, shift, lane, 1.0)
        a, b, c, d = a * a0 + b * c0, a * b0 + b * d0, c * a0 + d * c0, c * b0 + d * d0
        step *= 2
    return a + b


def line_rows(alpha, sizes):
    axes, lanes = alpha.shape
    lane = lax.broadcasted_iota(jnp.int32, (axes, lanes), 1)
    which = lax.broadcasted_iota(jnp.int32, (axes, lanes), 0)
    count = jnp.zeros((axes, lanes), jnp.int32)
    for axis, size in enumerate(sizes):
        count = jnp.where(which == axis, size, count)
    inside = lane < count
    alpha = jnp.where(inside, alpha, 0.5)
    slack = 1.0 - 2.0 * alpha
    twice = 2.0 * alpha

    eps = slack + twice * moved(slack, 1, lane, 0.0)
    c = 1.0 - eps
    fwd = running((1.0 + eps, c, eps, c), lane, 1)
    eps = slack + twice * moved(slack, -1, lane, 0.0)
    c = 1.0 - eps
    bwd = running(
        (
            jnp.where(inside, 1.0 + eps, 1.0),
            jnp.where(inside, c, 0.0),
            jnp.where(inside, eps, 0.0),
            jnp.where(inside, c, 1.0),
        ),
        lane,
        -1,
    )
    weight = twice
    step = 1
    while step < lanes:
        weight = weight * moved(weight, step, lane, 1.0)
        step *= 2
    before_w = moved(weight, 1, lane, 1.0)
    before_f = moved(fwd, 1, lane, 1.0)
    after_g = moved(bwd, -1, lane, 1.0)
    whole = jnp.sum(jnp.where(lane == count - 1, fwd, 0.0), axis=1, keepdims=True)
    sign = jnp.where(lane % 2 == 0, 1.0, -1.0)

    p = jnp.where(inside, sign * weight * after_g, 0.0)
    u = jnp.where(inside, sign * before_f / before_w, 0.0)
    q = jnp.where(inside, 2.0 * sign * before_f / (weight * whole), 0.0)
    v = jnp.where(inside, 2.0 * sign * before_w * after_g / whole, 0.0)
    near = (alpha + 2.0) / 3.0
    far = (4.0 * alpha - 1.0) / 12.0

    def folded(row):
        one, two = row * near, row * far
        return (
            moved(one, 1, lane, 0.0)
            - moved(one, -1, lane, 0.0)
            + moved(two, 2, lane, 0.0)
            - moved(two, -2, lane, 0.0)
        )

    diag = p * (moved(q * near, 1, lane, 0.0) + moved(q * far, 2, lane, 0.0)) - u * (
        moved(v * near, -1, lane, 0.0) + moved(v * far, -2, lane, 0.0)
    )
    next_far = moved(jnp.where(inside, far, 0.0), -1, lane, 0.0)
    last_far = moved(far, 1, lane, 0.0)
    low = (p * moved(q, -1, lane, 0.0) - u * moved(v, -1, lane, 0.0)) * next_far
    high = (p * moved(q, 1, lane, 0.0) - u * moved(v, 1, lane, 0.0)) * last_far
    t = jnp.where(inside, folded(q), 0.0)
    s = jnp.where(inside, folded(v), 0.0)
    return [p, u, t, s, diag, low, high]


def packed_points(values, cells, owners, devices, capacity, width):
    points = owners.shape[1]
    row = lax.broadcasted_iota(jnp.int32, (devices, points), 0)
    hot = jnp.where(row == owners, 1.0, 0.0)
    group = 128
    upper = jnp.where(
        lax.broadcasted_iota(jnp.int32, (group, group), 0)
        < lax.broadcasted_iota(jnp.int32, (group, group), 1),
        1.0,
        0.0,
    ).astype(BF16)
    carried = jnp.zeros((devices, 1), F32)
    ranks = []
    for start in range(0, points, group):
        piece = hot[:, start : start + group]
        counts = carried + jnp.dot(piece.astype(BF16), upper, preferred_element_type=F32)
        ranks.append(jnp.sum(piece * counts, axis=0, keepdims=True))
        carried = carried + jnp.sum(piece, axis=1, keepdims=True)
    rank = jnp.concatenate(ranks, axis=1).astype(jnp.int32)
    slot = lax.broadcasted_iota(jnp.int32, (capacity, points), 0) == rank
    rows = [jnp.where(slot, row, 0.0) for row in values]
    rows.append(jnp.where(slot, cells.astype(F32), 0.0))
    spread = jnp.concatenate(rows, axis=0)
    top = spread.astype(BF16)
    rest = (spread - top.astype(F32)).astype(BF16)
    hot = hot.astype(BF16)
    spare = width - spread.shape[0]
    if spare:
        top = jnp.concatenate([top, jnp.zeros((spare, points), BF16)], axis=0)
        rest = jnp.concatenate([rest, jnp.zeros((spare, points), BF16)], axis=0)
    return lax.dot_general(hot, top, NT, preferred_element_type=F32) + lax.dot_general(
        hot, rest, NT, preferred_element_type=F32
    )


def fetch(sources, targets, sems):
    copies = [
        pltpu.make_async_copy(source, target, sems.at[number])
        for number, (source, target) in enumerate(zip(sources, targets))
    ]
    for copy in copies:
        copy.start()
    return copies


def first_kernel(sizes, capacity, turns, *refs):
    sources, refs = refs[:10], refs[10:]
    flux_x_out, flux_y_out, send_y, coef_x_out, coef_y_out, pack_out = refs[:6]
    faces, targets, alpha_s, pack, sems = refs[6:-13], refs[-13:-3], refs[-3], refs[-2], refs[-1]
    alpha_x, alpha_y, metric_x, metric_y, values, cells, owners, adj, jx, jy = targets
    copies = fetch(sources, targets, sems)
    for copy in copies[:7]:
        copy.wait()
    fields, cells_x, cells_y, depth = adj.shape
    lanes = alpha_s.shape[1]
    place_x = lax.axis_index("gx")
    shape = (cells_y, depth)

    alpha_s[...] = jnp.full(alpha_s.shape, 0.5, F32)
    alpha_s[0:1, 0 : sizes[0]] = alpha_x[...]
    alpha_s[1:2, 0 : sizes[1]] = alpha_y[...]
    rows = line_rows(alpha_s[...], sizes)
    first_x = place_x * cells_x
    first_y = lax.axis_index("gy") * cells_y
    coef_x = jnp.concatenate([row[0:1] for row in rows] + [jnp.zeros((1, lanes), F32)], axis=0)
    coef_y = jnp.concatenate([row[1:2] for row in rows] + [jnp.zeros((1, lanes), F32)], axis=0)
    coef_x = pltpu.roll(coef_x, lax.rem(lanes - first_x, lanes), 1)[:, :128]
    coef_y = pltpu.roll(coef_y, lax.rem(lanes - first_y, lanes), 1)[:, :128]
    row_of = lax.broadcasted_iota(jnp.int32, (8, 128), 0)
    scaled = (row_of != 2) & (row_of != 3)
    gain_x = jnp.concatenate([metric_x[...], jnp.zeros((1, 128 - cells_x), F32)], axis=1)
    gain_y = jnp.concatenate([metric_y[...], jnp.zeros((1, 128 - cells_y), F32)], axis=1)
    coef_x = coef_x * jnp.where(scaled, gain_x, 1.0)
    coef_y = coef_y * jnp.where(scaled, gain_y, 1.0)
    coef_x_out[...] = coef_x
    columns_y = jnp.concatenate([coef_y, jnp.zeros((120, 128), F32)], axis=0).T[:cells_y]
    coef_y_out[...] = columns_y

    devices, _, width = pack.shape
    packed = packed_points(
        [values[f] for f in range(fields)], cells[...], owners[...], devices, capacity, width
    )
    for device in range(devices):
        pack[device] = packed[device : device + 1]
    leaving = pltpu.make_async_copy(pack, pack_out, sems.at[len(sources)])
    leaving.start()

    copies[7].wait()
    copies[8].wait()
    totals = [[None, None] for _ in range(fields)]
    for i in range(cells_x):
        state = [adj[k, i] for k in range(fields)]
        for target in range(fields):
            flux = jx[0, target, i].astype(F32) * state[0]
            for k in range(1, fields):
                flux = flux + jx[k, target, i].astype(F32) * state[k]
            flux_x_out[target, i] = flux
            for side in range(2):
                term = jnp.broadcast_to(coef_x[2 + side : 3 + side, i : i + 1], shape) * flux
                if i > 0:
                    term = totals[target][side] + term
                totals[target][side] = term
    for turn, face in zip(turns, faces):
        size = 1 << (turn.bit_length() - 1)
        upper = (place_x // size) % 2 == 1
        for target in range(fields):
            spot = target * cells_y
            face[spot : spot + cells_y] = jnp.where(upper, totals[target][1], totals[target][0])
            if touches(turn):
                spot = spot + fields * cells_y
                face[spot : spot + cells_y] = jnp.where(
                    upper, flux_x_out[target, 0], flux_x_out[target, cells_x - 1]
                )

    weight_t = jnp.broadcast_to(columns_y[:, 2:3], shape)
    weight_s = jnp.broadcast_to(columns_y[:, 3:4], shape)
    copies[9].wait()
    for i in range(cells_x):
        state = [adj[k, i] for k in range(fields)]
        for target in range(fields):
            flux = jy[0, target, i].astype(F32) * state[0]
            for k in range(1, fields):
                flux = flux + jy[k, target, i].astype(F32) * state[k]
            flux_y_out[target, i] = flux
            line = target * cells_x + i
            rows = (
                jnp.sum(weight_t * flux, axis=0, keepdims=True),
                jnp.sum(weight_s * flux, axis=0, keepdims=True),
                flux[0:1],
                flux[cells_y - 1 : cells_y],
            )
            for number, row in enumerate(rows):
                send_y[number, line : line + 1] = row
    leaving.wait()


def flat_slots(received, number, capacity):
    senders = received.shape[0]
    part = received[:, number * capacity : (number + 1) * capacity]
    repeats = 128 // capacity
    tiled = jnp.concatenate([part] * repeats, axis=1)
    lane = lax.broadcasted_iota(jnp.int32, (senders, 128), 1) // capacity
    sender = lax.broadcasted_iota(jnp.int32, (senders, 128), 0)
    rows = []
    for group in range(senders // repeats):
        mine = sender == lane + group * repeats
        rows.append(jnp.sum(jnp.where(mine, tiled, 0.0), axis=0, keepdims=True))
    return jnp.concatenate(rows, axis=1)


def touches(turn):
    return turn & (turn + 1) == 0


def upper_of(place, turn):
    return (place // (1 << (turn.bit_length() - 1))) % 2 == 1


def block_kernel(flux_x, flux_y, coef_x_ref, coef_y_ref, out):
    fields, cells_x, cells_y, depth = out.shape
    shape = (cells_y, depth)
    coef_x = coef_x_ref[...]
    coef_y = coef_y_ref[...]

    def at_x(row, i):
        return jnp.broadcast_to(coef_x[row : row + 1, i : i + 1], shape)

    wide = [jnp.broadcast_to(coef_y[:, row : row + 1], shape) for row in range(7)]
    station = lax.broadcasted_iota(jnp.int32, shape, 0)

    for f in range(fields):
        stations = [flux_x[f, i] for i in range(cells_x)]
        before = [None] * cells_x
        after = [None] * cells_x
        for i in range(1, cells_x):
            term = at_x(2, i - 1) * stations[i - 1]
            before[i] = term if i == 1 else before[i - 1] + term
        for i in range(cells_x - 2, -1, -1):
            term = at_x(3, i + 1) * stations[i + 1]
            after[i] = term if i == cells_x - 2 else after[i + 1] + term
        for i in range(cells_x):
            total = at_x(4, i) * stations[i]
            if i > 0:
                total = total + at_x(0, i) * before[i] + at_x(5, i) * stations[i - 1]
            if i < cells_x - 1:
                total = total + at_x(1, i) * after[i] + at_x(6, i) * stations[i + 1]

            line = flux_y[f, i]
            below = wide[2] * line
            above = wide[3] * line
            low = jnp.where(station >= 1, pltpu.roll(line, 1, 0), 0.0)
            high = jnp.where(station < cells_y - 1, pltpu.roll(line, cells_y - 1, 0), 0.0)
            below = jnp.where(station >= 1, pltpu.roll(below, 1, 0), 0.0)
            above = jnp.where(station < cells_y - 1, pltpu.roll(above, cells_y - 1, 0), 0.0)
            step = 1
            while step < cells_y:
                below = below + jnp.where(station >= step, pltpu.roll(below, step, 0), 0.0)
                above = above + jnp.where(
                    station < cells_y - step, pltpu.roll(above, cells_y - step, 0), 0.0
                )
                step *= 2
            total = total + wide[0] * below + wide[1] * above
            total = total + wide[4] * line + wide[5] * low + wide[6] * high
            out[f, i] = total


def far_x_kernel(turns_x, base, coef_x_ref, *refs):
    arrived_x, out = refs[:-1], refs[-1]
    fields, cells_x, cells_y, depth = out.shape
    shape = (cells_y, depth)
    coef_x = coef_x_ref[...]
    place = lax.axis_index("gx")
    sides = [upper_of(place, turn) for turn in turns_x]

    def at_x(row, i):
        return jnp.broadcast_to(coef_x[row : row + 1, i : i + 1], shape)

    for f in range(fields):
        for i in range(cells_x):
            total = base[f, i]
            for turn, upper, face in zip(turns_x, sides, arrived_x):
                spot = f * cells_y
                weight = jnp.where(upper, at_x(0, i), at_x(1, i))
                total = total + weight * face[spot : spot + cells_y]
                if not touches(turn):
                    continue
                size = (turn + 1) // 2
                spot = spot + fields * cells_y
                if i == 0:
                    near = upper & (place % size == 0)
                    total = total + jnp.where(near, at_x(5, i), 0.0) * face[spot : spot + cells_y]
                if i == cells_x - 1:
                    near = jnp.logical_not(upper) & (place % size == size - 1)
                    total = total + jnp.where(near, at_x(6, i), 0.0) * face[spot : spot + cells_y]
            out[f, i] = total


def place_kernel(capacity, received, out):
    fields, cells_x, cells_y, depth = out.shape
    rows_block = cells_x * cells_y
    got = jnp.concatenate([received[sender] for sender in range(received.shape[0])], axis=0)
    slots = got.shape[0] * capacity
    flat = [flat_slots(got, f, capacity) for f in range(fields + 1)]
    cell = flat[fields].astype(jnp.int32)
    row_hot = lax.broadcasted_iota(jnp.int32, (rows_block, slots), 0) == cell // depth
    depth_hot = jnp.where(
        lax.broadcasted_iota(jnp.int32, (depth, slots), 0) == cell % depth, 1.0, 0.0
    ).astype(BF16)
    halves = []
    for f in range(fields):
        spread = jnp.where(row_hot, flat[f], 0.0)
        top = spread.astype(BF16)
        halves += [top, (spread - top.astype(F32)).astype(BF16)]
    both = lax.dot_general(
        jnp.concatenate(halves, axis=0), depth_hot, NT, preferred_element_type=F32
    )
    for f in range(fields):
        top = both[2 * f * rows_block : (2 * f + 1) * rows_block]
        forcing = top + both[(2 * f + 1) * rows_block : (2 * f + 2) * rows_block]
        for i in range(cells_x):
            out[f, i] = forcing[i * cells_y : (i + 1) * cells_y]


def last_kernel(turns_z, forcing, base, pair, coef_y_ref, *refs):
    arrived_z, out = refs[:-3], refs[-3]
    held, sems = refs[-2:]
    fields, cells_x, cells_y, depth = out.shape
    shape = (cells_y, depth)
    chip = lax.axis_index("gy") // 2
    odd = lax.axis_index("gy") % 2 == 1

    entering = jnp.where(odd, pair[0], 0.0)
    leaving = jnp.where(odd, 0.0, pair[1])
    left = jnp.where(odd, pair[3], 0.0)
    right = jnp.where(odd, 0.0, pair[2])
    for turn, got in zip(turns_z, arrived_z):
        upper = upper_of(chip, turn)
        entering = entering + jnp.where(upper, got[0], 0.0)
        leaving = leaving + jnp.where(upper, 0.0, got[0])
        if touches(turn):
            size = (turn + 1) // 2
            first = jnp.logical_not(odd) & upper & (chip % size == 0)
            last = odd & jnp.logical_not(upper) & (chip % size == size - 1)
            left = jnp.where(first, got[1], left)
            right = jnp.where(last, got[1], right)

    coef_y = coef_y_ref[...]

    p_y = jnp.broadcast_to(coef_y[:, 0:1], shape)
    u_y = jnp.broadcast_to(coef_y[:, 1:2], shape)
    station = lax.broadcasted_iota(jnp.int32, shape, 0)
    low_y = jnp.where(station == 0, jnp.broadcast_to(coef_y[:, 5:6], shape), 0.0)
    high_y = jnp.where(station == cells_y - 1, jnp.broadcast_to(coef_y[:, 6:7], shape), 0.0)
    copies = []
    for f in range(fields):
        for i in range(cells_x):
            total = base[f, i]
            line = slice(f * cells_x + i, f * cells_x + i + 1)
            total = total + p_y * entering[line] + u_y * leaving[line]
            total = total + low_y * left[line] + high_y * right[line]
            held[f, i] = forcing[f, i] - total
        copies.append(pltpu.make_async_copy(held.at[f], out.at[f], sems.at[f]))
        copies[-1].start()
    for copy in copies:
        copy.wait()


def along_z(own, pair, turns):
    count = lax.axis_size("gy")
    place = lax.axis_index("gy")
    odd = place % 2 == 1
    sum_t, sum_u = own[0] + pair[0], own[1] + pair[1]
    first, last = jnp.where(odd, pair[2], own[2]), jnp.where(odd, own[3], pair[3])
    sent = {}
    for turn in turns:
        bit = turn.bit_length()
        if bit not in sent:
            upper = upper_of(place // 2, turn)
            sent[bit] = jnp.stack([jnp.where(upper, sum_u, sum_t), jnp.where(upper, first, last)])
    return [
        lax.ppermute(sent[turn.bit_length()], "gy", [(i, i ^ (2 * turn + 1)) for i in range(count)])
        for turn in turns
    ]


def on_device(
    adjoint, jac_x, jac_y, alpha_x, metric_x, alpha_y, metric_y, surf_values, surf_cells, surf_owner
):
    fields, cells_x, cells_y, depth = adjoint.shape
    points = surf_values.shape[2]
    n_x = lax.axis_size("gx")
    n_y = lax.axis_size("gy")
    devices = n_x * n_y
    capacity = max(4, 2 * points // devices)
    sizes = (alpha_x.shape[0], alpha_y.shape[0])
    lanes = -(-max(sizes) // 128) * 128
    lines = fields * cells_x
    vmem = pl.BlockSpec(memory_space=pltpu.VMEM)
    hbm = pl.BlockSpec(memory_space=pltpu.HBM)

    def array(*shape):
        return jax.ShapeDtypeStruct(shape, F32)

    def cost(micros):
        return pl.CostEstimate(
            flops=int(micros * 1e9), bytes_accessed=int(micros * 3.6e6), transcendentals=0
        )

    params = pltpu.CompilerParams(vmem_limit_bytes=24 << 20)
    inputs = [
        alpha_x.reshape(1, -1),
        alpha_y.reshape(1, -1),
        metric_x.reshape(1, -1),
        metric_y.reshape(1, -1),
        jnp.transpose(surf_values, (1, 0, 2)),
        surf_cells,
        surf_owner.reshape(1, points),
        adjoint,
        jac_x,
        jac_y,
    ]
    turns_x = tuple(range(n_x - 1, 0, -1))
    turns_z = tuple(range(n_y // 2 - 1, 0, -1))
    width = -(-(fields + 1) * capacity // 128) * 128
    face_rows = fields * cells_y
    flux_x, flux_y, own_y, coef_x, coef_y, pack, *faces = pl.pallas_call(
        functools.partial(first_kernel, sizes, capacity, turns_x),
        in_specs=[hbm] * len(inputs),
        out_specs=[vmem] * 5 + [pl.BlockSpec(memory_space=pl.ANY)] + [vmem] * len(turns_x),
        out_shape=[
            array(*adjoint.shape),
            array(*adjoint.shape),
            array(4, lines, depth),
            array(8, 128),
            array(cells_y, 128),
            array(devices, 1, width),
        ]
        + [array((2 if touches(turn) else 1) * face_rows, depth) for turn in turns_x],
        scratch_shapes=[pltpu.VMEM(a.shape, a.dtype) for a in inputs]
        + [
            pltpu.VMEM((8, lanes), F32),
            pltpu.VMEM((devices, 1, width), F32),
            pltpu.SemaphoreType.DMA((len(inputs) + 1,)),
        ],
        compiler_params=params,
        cost_estimate=cost(2.5),
        name="flux_and_sums",
    )(*[pltpu.with_memory_space_constraint(a, pltpu.HBM) for a in inputs])
    received = lax.all_to_all(pack, ("gx", "gy"), 0, 0, tiled=True)
    arrived_x = [
        lax.ppermute(face, "gx", [(i, i ^ turn) for i in range(n_x)])
        for turn, face in zip(turns_x, faces)
    ]
    pair = lax.ppermute(own_y, "gy", [(i, i ^ 1) for i in range(n_y)])
    arrived_z = along_z(own_y, pair, turns_z)
    base = pl.pallas_call(
        block_kernel,
        in_specs=[vmem] * 4,
        out_specs=vmem,
        out_shape=array(*adjoint.shape),
        compiler_params=params,
        cost_estimate=cost(5),
        name="block_part",
    )(flux_x, flux_y, coef_x, coef_y)
    base = pl.pallas_call(
        functools.partial(far_x_kernel, turns_x),
        in_specs=[vmem] * (2 + len(turns_x)),
        out_specs=vmem,
        out_shape=array(*adjoint.shape),
        compiler_params=params,
        cost_estimate=cost(0.01),
        name="far_x_part",
    )(base, coef_x, *arrived_x)
    forcing = pl.pallas_call(
        functools.partial(place_kernel, capacity),
        in_specs=[vmem],
        out_specs=vmem,
        out_shape=array(*adjoint.shape),
        compiler_params=params,
        cost_estimate=cost(0.01),
        name="placed_points",
    )(received)
    return pl.pallas_call(
        functools.partial(last_kernel, turns_z),
        in_specs=[vmem] * (4 + len(turns_z)),
        out_specs=pl.BlockSpec(memory_space=pl.ANY),
        out_shape=array(*adjoint.shape),
        scratch_shapes=[
            pltpu.VMEM(adjoint.shape, F32),
            pltpu.SemaphoreType.DMA((fields,)),
        ],
        compiler_params=params,
        cost_estimate=cost(1),
        name="far_part",
    )(forcing, base, pair, coef_y, *arrived_z)


def solution(mesh):
    in_specs = (
        P(None, "gx", "gy", None),
        P(None, None, "gx", "gy", None),
        P(None, None, "gx", "gy", None),
        P(),
        P("gx"),
        P(),
        P("gy"),
        P(("gx", "gy"), None, None),
        P(("gx", "gy"), None),
        P(("gx", "gy"), None, None),
    )
    out_specs = P(None, "gx", "gy", None)
    return jax.shard_map(
        on_device, mesh=mesh, in_specs=in_specs, out_specs=out_specs, check_vma=False
    )
```

time: 28.1 us -> 23.2 us (0.83)
  waiting for transfers between devices: 6.8 us -> 2.93 us
  Pallas kernels: 6.71 us -> 4.87 us
  starting transfers between devices: 14.1 us -> 15 us
    ppermute x3, waiting for transfers between devices: 4.57 us -> 0.01 us  [on_device(): lax.ppermute(face, 'gx', [(i, i ^ turn) for i in range(n_x)])]
    pallas_call x4 -> x5, Pallas kernels: 6.71 us -> 4.87 us  [the longest x1 2.4 us: on_device(): pl.pallas_call(functools.partial(first_kernel, sizes, capacity, turns_x),...]
    all_to_all x1, starting transfers between devices: 4.85 us -> 6.25 us  [on_device(): received = lax.all_to_all(pack, ('gx', 'gy'), 0, 0, tiled=True)]
    all_to_all x1, waiting for transfers between devices: 1.28 us -> 2.46 us  [on_device(): received = lax.all_to_all(pack, ('gx', 'gy'), 0, 0, tiled=True)]
    ppermute x3 -> x4, starting transfers between devices: 5.76 us -> 4.62 us  [the longest x3 4.1 us: along_z(): lax.ppermute(sent[turn.bit_length()], 'gy', [(i, i ^ 2 * turn + 1) for i...]
    ppermute x3, starting transfers between devices: 3.5 us -> 4.16 us  [on_device(): lax.ppermute(face, 'gx', [(i, i ^ turn) for i in range(n_x)])]
    ppermute x3 -> x4, waiting for transfers between devices: 0.95 us -> 0.47 us  [the longest x3 0.46 us: along_z(): lax.ppermute(sent[turn.bit_length()], 'gy', [(i, i ^ 2 * turn + 1) for i...]
  transfers between devices with their start and end apart: 7 -> 8, of which waited for: 4 -> 2; matrix products, arithmetic and copies ran while one was open for 0% -> 0% of each run, Pallas kernels for 5% -> 7%
where the time goes in v3:
time: 23.2 us; the launch traced here: 23 us
  starting transfers between devices  15 us (65%)
  Pallas kernels  4.87 us (21%)
  waiting for transfers between devices  2.93 us (13%)
    all_to_all x1, starting transfers between devices, on_device(): received = lax.all_to_all(pack, ('gx', 'gy'), 0, 0, tiled=True)  6.25 us
    ppermute x3, starting transfers between devices, on_device(): lax.ppermute(face, 'gx', [(i, i ^ turn) for i in range(n_x)])  4.16 us
    ppermute x3, starting transfers between devices, along_z(): lax.ppermute(sent[turn.bit_length()], 'gy', [(i, i ^ 2 * turn + 1) for i...  4.1 us
    all_to_all x1, waiting for transfers between devices, on_device(): received = lax.all_to_all(pack, ('gx', 'gy'), 0, 0, tiled=True)  2.46 us
    pallas_call x1, Pallas kernels, on_device(): pl.pallas_call(functools.partial(first_kernel, sizes, capacity, turns_x),...  2.4 us
    pallas_call x1, Pallas kernels, on_device(): pl.pallas_call(functools.partial(last_kernel, turns_z), in_specs=[vmem] *...  0.86 us
    pallas_call x1, Pallas kernels, on_device(): pl.pallas_call(functools.partial(place_kernel, capacity), in_specs=[vmem]...  0.76 us
    pallas_call x1, Pallas kernels, on_device(): pl.pallas_call(block_kernel, in_specs=[vmem] * 4, out_specs=vmem, out_sha...  0.68 us
  transfers between devices with their start and end apart: 8, of which 2 were waited for; matrix products, arithmetic and copies ran while one was open for 0% of the time, Pallas kernels for 7%

profile of v3, /device:TPU:0, one launch (start us, length us, event | category | flops | bytes accessed | tf_op | source)
XLA Modules:
  0.0 23.0 jit_solution(4562817574250354819)
XLA Ops:
  0.0 2.4 %flux_and_sums.1 = (f32[5,4,16,256]{3,2,1,0:T(8,128)S(1)}, f32[5,4,16,256]{3,2,1,0:T(8,128)S(1)}, f32[4,20,256]{2,1,0:T(8,128)S(1)}, f32[8,128]{1,0:T(8,128)S(1)...) custom-call(f32[1,16]{1,0:T(1,128)} %bitcast.8, ...), custom_call_target="tpu_custom_call" | custom-call | flops 2500000000 | bytes 9000000 | tf_op jit(solution)/shard_map/flux_and_sums/pallas_call | solution.py:466
  2.4 0.5 %collective-permute-start.3 = (f32[4,20,256]{2,1,0:T(8,128)S(1)}, f32[4,20,256]{2,1,0:T(8,128)S(1)}, u32[]{:S(2)}, u32[]{:S(2)}) collective-permute-start(f32[4,20,256]{2,1,0:T(8,128)S(1)} %get-tuple-element.22), channel_id=1, source_target_pairs={{0,1},{1,0},{2,3},{3,2},{4,5},{5,4},{6,7},{7,6},{8,9},{9,8},{10,11... | collective-permute-start | bytes 245768 | tf_op jit(solution)/shard_map/ppermute | solution.py:494
  2.9 3.5 %collective-permute-start = (f32[160,256]{1,0:T(8,128)S(1)}, f32[160,256]{1,0:T(8,128)S(1)}, u32[]{:S(2)}, u32[]{:S(2)}) collective-permute-start(f32[160,256]{1,0:T(8,128)S(1)} %get-tuple-element.19), channel_id=1, source_target_pairs={{0,24},{8,16},{16,8},{24,0},{1,25},{9,17},{17,9},{25,1},{2,26},{10... | collective-permute-start | bytes 491528 | tf_op jit(solution)/shard_map/ppermute | solution.py:491
  6.4 0.5 %collective-permute-start.2 = (f32[160,256]{1,0:T(8,128)S(1)}, f32[160,256]{1,0:T(8,128)S(1)}, u32[]{:S(2)}, u32[]{:S(2)}) collective-permute-start(f32[160,256]{1,0:T(8,128)S(1)} %get-tuple-element.21), channel_id=1, source_target_pairs={{0,8},{8,0},{16,24},{24,16},{1,9},{9,1},{17,25},{25,17},{2,10},{10... | collective-permute-start | bytes 491528 | tf_op jit(solution)/shard_map/ppermute | solution.py:491
  7.0 0.1 collective-permute-start.1
  7.1 6.2 %all-to-all-start = ((f32[32,1,256]{2,1,0:T(1,128)}), f32[32,1,256]{2,1,0:T(1,128)S(1)}, u32[]{:S(2)}, u32[]{:S(2)}) async-start(f32[32,1,256]{2,1,0:T(1,128)} %get-tuple-element.14), calls=%async_computation | async-start | bytes 65536 | tf_op jit(solution)/shard_map/all_to_all | solution.py:489
  13.4 0.0 collective-permute-done.3.pair
  13.5 3.4 %collective-permute-start.4 = (f32[2,20,256]{2,1,0:T(8,128)S(1)}, f32[2,20,256]{2,1,0:T(8,128)S(1)}, u32[]{:S(2)}, u32[]{:S(2)}) collective-permute-start(f32[2,20,256]{2,1,0:T(8,128)S(1)} %pad_maximum_fusion), channel_id=1, source_target_pairs={{0,7},{1,6},{2,5},{3,4},{4,3},{5,2},{6,1},{7,0},{8,15},{9,14},{10,... | collective-permute-start | bytes 122888 | tf_op jit(solution)/shard_map/ppermute | solution.py:421
  16.9 0.0 collective-permute-start.5
  16.9 0.0 collective-permute-done.1.refs_1_
  16.9 0.7 %collective-permute-start.6 = (f32[2,20,256]{2,1,0:T(8,128)S(1)}, f32[2,20,256]{2,1,0:T(8,128)S(1)}, u32[]{:S(2)}, u32[]{:S(2)}) collective-permute-start(f32[2,20,256]{2,1,0:T(8,128)S(1)} %pad_maximum_fusion.1), channel_id=1, source_target_pairs={{0,3},{1,2},{2,1},{3,0},{4,7},{5,6},{6,5},{7,4},{8,11},{9,10},{10,... | collective-permute-start | bytes 122888 | tf_op jit(solution)/shard_map/ppermute | solution.py:421
  17.6 0.7 %block_part.1.base = f32[5,4,16,256]{3,2,1,0:T(8,128)S(1)} custom-call(f32[5,4,16,256]{3,2,1,0:T(8,128)S(1)} %get-tuple-element.15.flux_x, f32[5,4,16,256]{3,2,1,0:T(8,128)S(1)} %get-tuple-element.16.flux_y, f32[8,128]{1,0:T(8,128)S(1)} %get-tuple-element.17.coef_x_ref, f32[16,128]{1,0:T(8,128)S(1)} %get-tuple-element.18.coef_y_ref), custom_call_target="tpu_custom_call" | custom-call | flops 5000000000 | bytes 18000000 | tf_op jit(solution)/shard_map/block_part/pallas_call | solution.py:496
  18.3 2.5 %all-to-all-done.received = f32[32,1,256]{2,1,0:T(1,128)S(1)} async-done(((f32[32,1,256]{2,1,0:T(1,128)}), f32[32,1,256]{2,1,0:T(1,128)S(1)}, u32[]{:S(2)}, u32[]{:S(2)}) %all-to-all-start) | async-done | bytes 32800 | tf_op jit(solution)/shard_map/all_to_all | solution.py:489
  20.7 0.8 %placed_points.1.forcing = f32[5,4,16,256]{3,2,1,0:T(8,128)S(1)} custom-call(f32[32,1,256]{2,1,0:T(1,128)S(1)} %all-to-all-done.received), custom_call_target="tpu_custom_call" | custom-call | flops 10000000 | bytes 36000 | tf_op jit(solution)/shard_map/placed_points/pallas_call | solution.py:514
  21.5 0.0 collective-permute-done.refs_0_
  21.5 0.0 collective-permute-done.2.refs_2_
  21.5 0.2 far_x_part.1.base
  21.7 0.0 collective-permute-done.6.refs_2_
  21.7 0.0 collective-permute-done.4.refs_0_
  21.7 0.5 %collective-permute-done.5.refs_1_ = f32[2,20,256]{2,1,0:T(8,128)S(1)} collective-permute-done((f32[2,20,256]{2,1,0:T(8,128)S(1)}, f32[2,20,256]{2,1,0:T(8,128)S(1)}, u32[]{:S(2)}, u32[]{:S(2)}) %collective-permute-start.5) | collective-permute-done | bytes 40992 | tf_op jit(solution)/shard_map/ppermute | solution.py:421
  22.2 0.9 %far_part.1 = f32[5,4,16,256]{3,2,1,0:T(8,128)} custom-call(f32[5,4,16,256]{3,2,1,0:T(8,128)S(1)} %placed_points.1.forcing, f32[5,4,16,256]{3,2,1,0:T(8,128)S(1)} %far_x_part.1.base, f32[4,20,256]{2,1,0:T(8,128)S(1)} %collective-permute-done.3.pair, f32[16,128]{1,0:T(8,128)S(1)} %get-tuple-element.18.coef_y_ref, ...), custom_call_target="tpu_custom_call" | custom-call | flops 1000000000 | bytes 3600000 | tf_op jit(solution)/shard_map/far_part/pallas_call | solution.py:523
  (3 shorter events, 0.0 us)
Async XLA Ops:
  2.4 11.0 %collective-permute-start.3 = (f32[4,20,256]{2,1,0:T(8,128)S(1)}, f32[4,20,256]{2,1,0:T(8,128)S(1)}, u32[]{:S(2)}, u32[]{:S(2)}) collective-permute-start(f32[4,20,256]{2,1,0:T(8,128)S(1)} %get-tuple-element.22), channel_id=1, source_target_pairs={{0,1},{1,0},{2,3},{3,2},{4,5},{5,4},{6,7},{7,6},{8,9},{9,8},{10,11... | collective-permute-start | bytes 245768 | tf_op jit(solution)/shard_map/ppermute | solution.py:494
  2.9 18.6 %collective-permute-start = (f32[160,256]{1,0:T(8,128)S(1)}, f32[160,256]{1,0:T(8,128)S(1)}, u32[]{:S(2)}, u32[]{:S(2)}) collective-permute-start(f32[160,256]{1,0:T(8,128)S(1)} %get-tuple-element.19), channel_id=1, source_target_pairs={{0,24},{8,16},{16,8},{24,0},{1,25},{9,17},{17,9},{25,1},{2,26},{10... | collective-permute-start | bytes 491528 | tf_op jit(solution)/shard_map/ppermute | solution.py:491
  6.4 15.1 %collective-permute-start.2 = (f32[160,256]{1,0:T(8,128)S(1)}, f32[160,256]{1,0:T(8,128)S(1)}, u32[]{:S(2)}, u32[]{:S(2)}) collective-permute-start(f32[160,256]{1,0:T(8,128)S(1)} %get-tuple-element.21), channel_id=1, source_target_pairs={{0,8},{8,0},{16,24},{24,16},{1,9},{9,1},{17,25},{25,17},{2,10},{10... | collective-permute-start | bytes 491528 | tf_op jit(solution)/shard_map/ppermute | solution.py:491
  7.0 9.9 %collective-permute-start.1 = (f32[80,256]{1,0:T(8,128)S(1)}, f32[80,256]{1,0:T(8,128)S(1)}, u32[]{:S(2)}, u32[]{:S(2)}) collective-permute-start(f32[80,256]{1,0:T(8,128)S(1)} %get-tuple-element.20), channel_id=1, source_target_pairs={{0,16},{8,24},{16,0},{24,8},{1,17},{9,25},{17,1},{25,9},{2,18},{10... | collective-permute-start | bytes 245768 | tf_op jit(solution)/shard_map/ppermute | solution.py:491
  7.1 13.6 %all-to-all-start = ((f32[32,1,256]{2,1,0:T(1,128)}), f32[32,1,256]{2,1,0:T(1,128)S(1)}, u32[]{:S(2)}, u32[]{:S(2)}) async-start(f32[32,1,256]{2,1,0:T(1,128)} %get-tuple-element.14), calls=%async_computation | async-start | bytes 65536 | tf_op jit(solution)/shard_map/all_to_all | solution.py:489
  13.5 8.2 %collective-permute-start.4 = (f32[2,20,256]{2,1,0:T(8,128)S(1)}, f32[2,20,256]{2,1,0:T(8,128)S(1)}, u32[]{:S(2)}, u32[]{:S(2)}) collective-permute-start(f32[2,20,256]{2,1,0:T(8,128)S(1)} %pad_maximum_fusion), channel_id=1, source_target_pairs={{0,7},{1,6},{2,5},{3,4},{4,3},{5,2},{6,1},{7,0},{8,15},{9,14},{10,... | collective-permute-start | bytes 122888 | tf_op jit(solution)/shard_map/ppermute | solution.py:421
  16.9 5.3 %collective-permute-start.5 = (f32[2,20,256]{2,1,0:T(8,128)S(1)}, f32[2,20,256]{2,1,0:T(8,128)S(1)}, u32[]{:S(2)}, u32[]{:S(2)}) collective-permute-start(f32[2,20,256]{2,1,0:T(8,128)S(1)} %pad_maximum_fusion), channel_id=1, source_target_pairs={{0,5},{1,4},{2,7},{3,6},{4,1},{5,0},{6,3},{7,2},{8,13},{9,12},{10,... | collective-permute-start | bytes 122888 | tf_op jit(solution)/shard_map/ppermute | solution.py:421
  16.9 4.8 %collective-permute-start.6 = (f32[2,20,256]{2,1,0:T(8,128)S(1)}, f32[2,20,256]{2,1,0:T(8,128)S(1)}, u32[]{:S(2)}, u32[]{:S(2)}) collective-permute-start(f32[2,20,256]{2,1,0:T(8,128)S(1)} %pad_maximum_fusion.1), channel_id=1, source_target_pairs={{0,3},{1,2},{2,1},{3,0},{4,7},{5,6},{6,5},{7,4},{8,11},{9,10},{10,... | collective-permute-start | bytes 122888 | tf_op jit(solution)/shard_map/ppermute | solution.py:421

commit v4 on v3

--- a/solution.py
+++ b/solution.py
@@ -487,10 +487,12 @@
         name="flux_and_sums",
     )(*[pltpu.with_memory_space_constraint(a, pltpu.HBM) for a in inputs])
     received = lax.all_to_all(pack, ("gx", "gy"), 0, 0, tiled=True)
-    arrived_x = [
-        lax.ppermute(face, "gx", [(i, i ^ turn) for i in range(n_x)])
-        for turn, face in zip(turns_x, faces)
-    ]
+    arrived = {}
+    for turn, face in sorted(zip(turns_x, faces), key=lambda item: not touches(item[0])):
+        if not touches(turn):
+            face, arrived[1] = lax.optimization_barrier((face, arrived[1]))
+        arrived[turn] = lax.ppermute(face, "gx", [(i, i ^ turn) for i in range(n_x)])
+    arrived_x = [arrived[turn] for turn in turns_x]
     pair = lax.ppermute(own_y, "gy", [(i, i ^ 1) for i in range(n_y)])
     arrived_z = along_z(own_y, pair, turns_z)
     base = pl.pallas_call(

time: 23.2 us -> 21.9 us (0.944)
  waiting for transfers between devices: 2.93 us -> 1.53 us
    all_to_all x1, waiting for transfers between devices: 2.46 us -> 0.86 us  [on_device(): received = lax.all_to_all(pack, ('gx', 'gy'), 0, 0, tiled=True)]
    ppermute x3, starting transfers between devices: 4.16 us -> 5.72 us  [on_device(): lax.ppermute(face, 'gx', [(i, i ^ turn) for i in range(n_x)])]
    all_to_all x1, starting transfers between devices: 6.25 us -> 4.89 us  [on_device(): received = lax.all_to_all(pack, ('gx', 'gy'), 0, 0, tiled=True)]
    ppermute x3, waiting for transfers between devices: 0.01 us -> 0.65 us  [on_device(): lax.ppermute(face, 'gx', [(i, i ^ turn) for i in range(n_x)])]
    ppermute x3, waiting for transfers between devices: 0.46 us -> 0.01 us  [along_z(): lax.ppermute(sent[turn.bit_length()], 'gy', [(i, i ^ 2 * turn + 1) for i...]
where the time goes in v4:
time: 21.9 us; the launch traced here: 21.8 us
  starting transfers between devices  15.2 us (69%)
  Pallas kernels  4.87 us (22%)
  waiting for transfers between devices  1.53 us (7%)
    ppermute x3, starting transfers between devices, on_device(): lax.ppermute(face, 'gx', [(i, i ^ turn) for i in range(n_x)])  5.72 us
    all_to_all x1, starting transfers between devices, on_device(): received = lax.all_to_all(pack, ('gx', 'gy'), 0, 0, tiled=True)  4.89 us
    ppermute x3, starting transfers between devices, along_z(): lax.ppermute(sent[turn.bit_length()], 'gy', [(i, i ^ 2 * turn + 1) for i...  4.04 us
    pallas_call x1, Pallas kernels, on_device(): pl.pallas_call(functools.partial(first_kernel, sizes, capacity, turns_x),...  2.4 us
    all_to_all x1, waiting for transfers between devices, on_device(): received = lax.all_to_all(pack, ('gx', 'gy'), 0, 0, tiled=True)  0.86 us
    pallas_call x1, Pallas kernels, on_device(): pl.pallas_call(functools.partial(last_kernel, turns_z), in_specs=[vmem] *...  0.86 us
    pallas_call x1, Pallas kernels, on_device(): pl.pallas_call(functools.partial(place_kernel, capacity), in_specs=[vmem]...  0.76 us
    pallas_call x1, Pallas kernels, on_device(): pl.pallas_call(block_kernel, in_specs=[vmem] * 4, out_specs=vmem, out_sha...  0.68 us
  transfers between devices with their start and end apart: 8, of which 2 were waited for; matrix products, arithmetic and copies ran while one was open for 0% of the time, Pallas kernels for 7%

profile of v4, /device:TPU:0, one launch (start us, length us, event | category | flops | bytes accessed | tf_op | source)
XLA Modules:
  0.0 21.8 jit_solution(12406466882143029618)
XLA Ops:
  0.0 2.4 %flux_and_sums.1 = (f32[5,4,16,256]{3,2,1,0:T(8,128)S(1)}, f32[5,4,16,256]{3,2,1,0:T(8,128)S(1)}, f32[4,20,256]{2,1,0:T(8,128)S(1)}, f32[8,128]{1,0:T(8,128)S(1)...) custom-call(f32[1,16]{1,0:T(1,128)} %bitcast.8, ...), custom_call_target="tpu_custom_call" | custom-call | flops 2500000000 | bytes 9000000 | tf_op jit(solution)/shard_map/flux_and_sums/pallas_call | solution.py:466
  2.4 0.5 %collective-permute-start.3 = (f32[4,20,256]{2,1,0:T(8,128)S(1)}, f32[4,20,256]{2,1,0:T(8,128)S(1)}, u32[]{:S(2)}, u32[]{:S(2)}) collective-permute-start(f32[4,20,256]{2,1,0:T(8,128)S(1)} %get-tuple-element.26), channel_id=1, source_target_pairs={{0,1},{1,0},{2,3},{3,2},{4,5},{5,4},{6,7},{7,6},{8,9},{9,8},{10,11... | collective-permute-start | bytes 245768 | tf_op jit(solution)/shard_map/ppermute | solution.py:496
  2.9 2.6 %collective-permute-start.1 = (f32[160,256]{1,0:T(8,128)S(1)}, f32[160,256]{1,0:T(8,128)S(1)}, u32[]{:S(2)}, u32[]{:S(2)}) collective-permute-start(f32[160,256]{1,0:T(8,128)S(1)} %get-tuple-element.23), channel_id=1, source_target_pairs={{0,8},{8,0},{16,24},{24,16},{1,9},{9,1},{17,25},{25,17},{2,10},{10... | collective-permute-start | bytes 491528 | tf_op jit(solution)/shard_map/ppermute | solution.py:494
  5.5 1.5 %collective-permute-start = (f32[160,256]{1,0:T(8,128)S(1)}, f32[160,256]{1,0:T(8,128)S(1)}, u32[]{:S(2)}, u32[]{:S(2)}) collective-permute-start(f32[160,256]{1,0:T(8,128)S(1)} %get-tuple-element.21), channel_id=1, source_target_pairs={{0,24},{8,16},{16,8},{24,0},{1,25},{9,17},{17,9},{25,1},{2,26},{10... | collective-permute-start | bytes 491528 | tf_op jit(solution)/shard_map/ppermute | solution.py:494
  7.0 4.9 %all-to-all-start = ((f32[32,1,256]{2,1,0:T(1,128)}), f32[32,1,256]{2,1,0:T(1,128)S(1)}, u32[]{:S(2)}, u32[]{:S(2)}) async-start(f32[32,1,256]{2,1,0:T(1,128)} %get-tuple-element.16), calls=%async_computation | async-start | bytes 65536 | tf_op jit(solution)/shard_map/all_to_all | solution.py:489
  11.9 0.0 collective-permute-done.3.pair
  12.0 3.4 %collective-permute-start.4 = (f32[2,20,256]{2,1,0:T(8,128)S(1)}, f32[2,20,256]{2,1,0:T(8,128)S(1)}, u32[]{:S(2)}, u32[]{:S(2)}) collective-permute-start(f32[2,20,256]{2,1,0:T(8,128)S(1)} %pad_maximum_fusion), channel_id=1, source_target_pairs={{0,7},{1,6},{2,5},{3,4},{4,3},{5,2},{6,1},{7,0},{8,15},{9,14},{10,... | collective-permute-start | bytes 122888 | tf_op jit(solution)/shard_map/ppermute | solution.py:421
  15.4 0.0 collective-permute-start.5
  15.4 0.6 %collective-permute-start.6 = (f32[2,20,256]{2,1,0:T(8,128)S(1)}, f32[2,20,256]{2,1,0:T(8,128)S(1)}, u32[]{:S(2)}, u32[]{:S(2)}) collective-permute-start(f32[2,20,256]{2,1,0:T(8,128)S(1)} %pad_maximum_fusion.1), channel_id=1, source_target_pairs={{0,3},{1,2},{2,1},{3,0},{4,7},{5,6},{6,5},{7,4},{8,11},{9,10},{10,... | collective-permute-start | bytes 122888 | tf_op jit(solution)/shard_map/ppermute | solution.py:421
  16.1 0.0 collective-permute-done.1.refs_2_
  16.1 1.7 %collective-permute-start.2 = (f32[80,256]{1,0:T(8,128)S(1)}, f32[80,256]{1,0:T(8,128)S(1)}, u32[]{:S(2)}, u32[]{:S(2)}) collective-permute-start(f32[80,256]{1,0:T(8,128)S(1)} %get-tuple-element.24), channel_id=1, source_target_pairs={{0,16},{8,24},{16,0},{24,8},{1,17},{9,25},{17,1},{25,9},{2,18},{10... | collective-permute-start | bytes 245768 | tf_op jit(solution)/shard_map/ppermute | solution.py:494
  17.7 0.7 %block_part.1.base = f32[5,4,16,256]{3,2,1,0:T(8,128)S(1)} custom-call(f32[5,4,16,256]{3,2,1,0:T(8,128)S(1)} %get-tuple-element.17.flux_x, f32[5,4,16,256]{3,2,1,0:T(8,128)S(1)} %get-tuple-element.18.flux_y, f32[8,128]{1,0:T(8,128)S(1)} %get-tuple-element.19.coef_x_ref, f32[16,128]{1,0:T(8,128)S(1)} %get-tuple-element.20.coef_y_ref), custom_call_target="tpu_custom_call" | custom-call | flops 5000000000 | bytes 18000000 | tf_op jit(solution)/shard_map/block_part/pallas_call | solution.py:498
  18.4 0.9 %all-to-all-done.received = f32[32,1,256]{2,1,0:T(1,128)S(1)} async-done(((f32[32,1,256]{2,1,0:T(1,128)}), f32[32,1,256]{2,1,0:T(1,128)S(1)}, u32[]{:S(2)}, u32[]{:S(2)}) %all-to-all-start) | async-done | bytes 32800 | tf_op jit(solution)/shard_map/all_to_all | solution.py:489
  19.3 0.8 %placed_points.1.forcing = f32[5,4,16,256]{3,2,1,0:T(8,128)S(1)} custom-call(f32[32,1,256]{2,1,0:T(1,128)S(1)} %all-to-all-done.received), custom_call_target="tpu_custom_call" | custom-call | flops 10000000 | bytes 36000 | tf_op jit(solution)/shard_map/placed_points/pallas_call | solution.py:516
  20.0 0.0 collective-permute-done.refs_0_
  20.0 0.6 %collective-permute-done.2.refs_1_ = f32[80,256]{1,0:T(8,128)S(1)} collective-permute-done((f32[80,256]{1,0:T(8,128)S(1)}, f32[80,256]{1,0:T(8,128)S(1)}, u32[]{:S(2)}, u32[]{:S(2)}) %collective-permute-start.2) | collective-permute-done | bytes 81952 | tf_op jit(solution)/shard_map/ppermute | solution.py:494
  20.7 0.2 far_x_part.1.base
  20.9 0.0 collective-permute-done.6.refs_2_
  20.9 0.0 collective-permute-done.4.refs_0_
  20.9 0.0 collective-permute-done.5.refs_1_
  20.9 0.9 %far_part.1 = f32[5,4,16,256]{3,2,1,0:T(8,128)} custom-call(f32[5,4,16,256]{3,2,1,0:T(8,128)S(1)} %placed_points.1.forcing, f32[5,4,16,256]{3,2,1,0:T(8,128)S(1)} %far_x_part.1.base, f32[4,20,256]{2,1,0:T(8,128)S(1)} %collective-permute-done.3.pair, f32[16,128]{1,0:T(8,128)S(1)} %get-tuple-element.20.coef_y_ref, ...), custom_call_target="tpu_custom_call" | custom-call | flops 1000000000 | bytes 3600000 | tf_op jit(solution)/shard_map/far_part/pallas_call | solution.py:525
  (3 shorter events, 0.0 us)
Async XLA Ops:
  2.4 9.5 %collective-permute-start.3 = (f32[4,20,256]{2,1,0:T(8,128)S(1)}, f32[4,20,256]{2,1,0:T(8,128)S(1)}, u32[]{:S(2)}, u32[]{:S(2)}) collective-permute-start(f32[4,20,256]{2,1,0:T(8,128)S(1)} %get-tuple-element.26), channel_id=1, source_target_pairs={{0,1},{1,0},{2,3},{3,2},{4,5},{5,4},{6,7},{7,6},{8,9},{9,8},{10,11... | collective-permute-start | bytes 245768 | tf_op jit(solution)/shard_map/ppermute | solution.py:496
  2.9 13.1 %collective-permute-start.1 = (f32[160,256]{1,0:T(8,128)S(1)}, f32[160,256]{1,0:T(8,128)S(1)}, u32[]{:S(2)}, u32[]{:S(2)}) collective-permute-start(f32[160,256]{1,0:T(8,128)S(1)} %get-tuple-element.23), channel_id=1, source_target_pairs={{0,8},{8,0},{16,24},{24,16},{1,9},{9,1},{17,25},{25,17},{2,10},{10... | collective-permute-start | bytes 491528 | tf_op jit(solution)/shard_map/ppermute | solution.py:494
  5.5 14.5 %collective-permute-start = (f32[160,256]{1,0:T(8,128)S(1)}, f32[160,256]{1,0:T(8,128)S(1)}, u32[]{:S(2)}, u32[]{:S(2)}) collective-permute-start(f32[160,256]{1,0:T(8,128)S(1)} %get-tuple-element.21), channel_id=1, source_target_pairs={{0,24},{8,16},{16,8},{24,0},{1,25},{9,17},{17,9},{25,1},{2,26},{10... | collective-permute-start | bytes 491528 | tf_op jit(solution)/shard_map/ppermute | solution.py:494
  7.0 12.3 %all-to-all-start = ((f32[32,1,256]{2,1,0:T(1,128)}), f32[32,1,256]{2,1,0:T(1,128)S(1)}, u32[]{:S(2)}, u32[]{:S(2)}) async-start(f32[32,1,256]{2,1,0:T(1,128)} %get-tuple-element.16), calls=%async_computation | async-start | bytes 65536 | tf_op jit(solution)/shard_map/all_to_all | solution.py:489
  12.0 8.9 %collective-permute-start.4 = (f32[2,20,256]{2,1,0:T(8,128)S(1)}, f32[2,20,256]{2,1,0:T(8,128)S(1)}, u32[]{:S(2)}, u32[]{:S(2)}) collective-permute-start(f32[2,20,256]{2,1,0:T(8,128)S(1)} %pad_maximum_fusion), channel_id=1, source_target_pairs={{0,7},{1,6},{2,5},{3,4},{4,3},{5,2},{6,1},{7,0},{8,15},{9,14},{10,... | collective-permute-start | bytes 122888 | tf_op jit(solution)/shard_map/ppermute | solution.py:421
  15.4 5.5 %collective-permute-start.5 = (f32[2,20,256]{2,1,0:T(8,128)S(1)}, f32[2,20,256]{2,1,0:T(8,128)S(1)}, u32[]{:S(2)}, u32[]{:S(2)}) collective-permute-start(f32[2,20,256]{2,1,0:T(8,128)S(1)} %pad_maximum_fusion), channel_id=1, source_target_pairs={{0,5},{1,4},{2,7},{3,6},{4,1},{5,0},{6,3},{7,2},{8,13},{9,12},{10,... | collective-permute-start | bytes 122888 | tf_op jit(solution)/shard_map/ppermute | solution.py:421
  15.4 5.4 %collective-permute-start.6 = (f32[2,20,256]{2,1,0:T(8,128)S(1)}, f32[2,20,256]{2,1,0:T(8,128)S(1)}, u32[]{:S(2)}, u32[]{:S(2)}) collective-permute-start(f32[2,20,256]{2,1,0:T(8,128)S(1)} %pad_maximum_fusion.1), channel_id=1, source_target_pairs={{0,3},{1,2},{2,1},{3,0},{4,7},{5,6},{6,5},{7,4},{8,11},{9,10},{10,... | collective-permute-start | bytes 122888 | tf_op jit(solution)/shard_map/ppermute | solution.py:421
  16.1 4.6 %collective-permute-start.2 = (f32[80,256]{1,0:T(8,128)S(1)}, f32[80,256]{1,0:T(8,128)S(1)}, u32[]{:S(2)}, u32[]{:S(2)}) collective-permute-start(f32[80,256]{1,0:T(8,128)S(1)} %get-tuple-element.24), channel_id=1, source_target_pairs={{0,16},{8,24},{16,0},{24,8},{1,17},{9,25},{17,1},{25,9},{2,18},{10... | collective-permute-start | bytes 245768 | tf_op jit(solution)/shard_map/ppermute | solution.py:494

commit v5 on v4

--- a/solution.py
+++ b/solution.py
@@ -460,7 +460,7 @@
         jac_y,
     ]
     turns_x = tuple(range(n_x - 1, 0, -1))
-    turns_z = tuple(range(n_y // 2 - 1, 0, -1))
+    turns_z = tuple(range(1, n_y // 2))
     width = -(-(fields + 1) * capacity // 128) * 128
     face_rows = fields * cells_y
     flux_x, flux_y, own_y, coef_x, coef_y, pack, *faces = pl.pallas_call(
@@ -490,7 +490,7 @@
     arrived = {}
     for turn, face in sorted(zip(turns_x, faces), key=lambda item: not touches(item[0])):
         if not touches(turn):
-            face, arrived[1] = lax.optimization_barrier((face, arrived[1]))
+            face, arrived[n_x - 1] = lax.optimization_barrier((face, arrived[n_x - 1]))
         arrived[turn] = lax.ppermute(face, "gx", [(i, i ^ turn) for i in range(n_x)])
     arrived_x = [arrived[turn] for turn in turns_x]
     pair = lax.ppermute(own_y, "gy", [(i, i ^ 1) for i in range(n_y)])
@@ -510,7 +510,7 @@
         out_specs=vmem,
         out_shape=array(*adjoint.shape),
         compiler_params=params,
-        cost_estimate=cost(0.01),
+        cost_estimate=cost(0.33),
         name="far_x_part",
     )(base, coef_x, *arrived_x)
     forcing = pl.pallas_call(

time: 21.9 us -> 21.8 us (level)
  no operation moved by 1% of the time
where the time goes in v5:
time: 21.8 us; the launch traced here: 21.7 us
  starting transfers between devices  15 us (69%)
  Pallas kernels  4.88 us (22%)
  waiting for transfers between devices  1.59 us (7%)
    ppermute x3, starting transfers between devices, on_device(): lax.ppermute(face, 'gx', [(i, i ^ turn) for i in range(n_x)])  5.55 us
    all_to_all x1, starting transfers between devices, on_device(): received = lax.all_to_all(pack, ('gx', 'gy'), 0, 0, tiled=True)  4.89 us
    ppermute x3, starting transfers between devices, along_z(): lax.ppermute(sent[turn.bit_length()], 'gy', [(i, i ^ 2 * turn + 1) for i...  4.04 us
    pallas_call x1, Pallas kernels, on_device(): pl.pallas_call(functools.partial(first_kernel, sizes, capacity, turns_x),...  2.4 us
    all_to_all x1, waiting for transfers between devices, on_device(): received = lax.all_to_all(pack, ('gx', 'gy'), 0, 0, tiled=True)  1.04 us
    pallas_call x1, Pallas kernels, on_device(): pl.pallas_call(functools.partial(last_kernel, turns_z), in_specs=[vmem] *...  0.86 us
    pallas_call x1, Pallas kernels, on_device(): pl.pallas_call(functools.partial(place_kernel, capacity), in_specs=[vmem]...  0.76 us
    pallas_call x1, Pallas kernels, on_device(): pl.pallas_call(block_kernel, in_specs=[vmem] * 4, out_specs=vmem, out_sha...  0.68 us
  transfers between devices with their start and end apart: 8, of which 2 were waited for; matrix products, arithmetic and copies ran while one was open for 0% of the time, Pallas kernels for 7%

profile of v5, /device:TPU:0, one launch (start us, length us, event | category | flops | bytes accessed | tf_op | source)
XLA Modules:
  0.0 21.7 jit_solution(18438571592450057627)
XLA Ops:
  0.0 2.4 %flux_and_sums.1 = (f32[5,4,16,256]{3,2,1,0:T(8,128)S(1)}, f32[5,4,16,256]{3,2,1,0:T(8,128)S(1)}, f32[4,20,256]{2,1,0:T(8,128)S(1)}, f32[8,128]{1,0:T(8,128)S(1)...) custom-call(f32[1,16]{1,0:T(1,128)} %bitcast.8, ...), custom_call_target="tpu_custom_call" | custom-call | flops 2500000000 | bytes 9000000 | tf_op jit(solution)/shard_map/flux_and_sums/pallas_call | solution.py:466
  2.4 0.5 %collective-permute-start.3 = (f32[4,20,256]{2,1,0:T(8,128)S(1)}, f32[4,20,256]{2,1,0:T(8,128)S(1)}, u32[]{:S(2)}, u32[]{:S(2)}) collective-permute-start(f32[4,20,256]{2,1,0:T(8,128)S(1)} %get-tuple-element.26), channel_id=1, source_target_pairs={{0,1},{1,0},{2,3},{3,2},{4,5},{5,4},{6,7},{7,6},{8,9},{9,8},{10,11... | collective-permute-start | bytes 245768 | tf_op jit(solution)/shard_map/ppermute | solution.py:496
  2.9 3.5 %collective-permute-start = (f32[160,256]{1,0:T(8,128)S(1)}, f32[160,256]{1,0:T(8,128)S(1)}, u32[]{:S(2)}, u32[]{:S(2)}) collective-permute-start(f32[160,256]{1,0:T(8,128)S(1)} %get-tuple-element.22), channel_id=1, source_target_pairs={{0,24},{8,16},{16,8},{24,0},{1,25},{9,17},{17,9},{25,1},{2,26},{10... | collective-permute-start | bytes 491528 | tf_op jit(solution)/shard_map/ppermute | solution.py:494
  6.4 0.5 %collective-permute-start.2 = (f32[160,256]{1,0:T(8,128)S(1)}, f32[160,256]{1,0:T(8,128)S(1)}, u32[]{:S(2)}, u32[]{:S(2)}) collective-permute-start(f32[160,256]{1,0:T(8,128)S(1)} %get-tuple-element.25), channel_id=1, source_target_pairs={{0,8},{8,0},{16,24},{24,16},{1,9},{9,1},{17,25},{25,17},{2,10},{10... | collective-permute-start | bytes 491528 | tf_op jit(solution)/shard_map/ppermute | solution.py:494
  7.0 4.9 %all-to-all-start = ((f32[32,1,256]{2,1,0:T(1,128)}), f32[32,1,256]{2,1,0:T(1,128)S(1)}, u32[]{:S(2)}, u32[]{:S(2)}) async-start(f32[32,1,256]{2,1,0:T(1,128)} %get-tuple-element.16), calls=%async_computation | async-start | bytes 65536 | tf_op jit(solution)/shard_map/all_to_all | solution.py:489
  11.9 0.0 collective-permute-done.3.pair
  12.0 2.5 %collective-permute-start.5 = (f32[2,20,256]{2,1,0:T(8,128)S(1)}, f32[2,20,256]{2,1,0:T(8,128)S(1)}, u32[]{:S(2)}, u32[]{:S(2)}) collective-permute-start(f32[2,20,256]{2,1,0:T(8,128)S(1)} %pad_maximum_fusion.1), channel_id=1, source_target_pairs={{0,5},{1,4},{2,7},{3,6},{4,1},{5,0},{6,3},{7,2},{8,13},{9,12},{10,... | collective-permute-start | bytes 122888 | tf_op jit(solution)/shard_map/ppermute | solution.py:421
  14.5 1.4 %collective-permute-start.6 = (f32[2,20,256]{2,1,0:T(8,128)S(1)}, f32[2,20,256]{2,1,0:T(8,128)S(1)}, u32[]{:S(2)}, u32[]{:S(2)}) collective-permute-start(f32[2,20,256]{2,1,0:T(8,128)S(1)} %pad_maximum_fusion.1), channel_id=1, source_target_pairs={{0,7},{1,6},{2,5},{3,4},{4,3},{5,2},{6,1},{7,0},{8,15},{9,14},{10,... | collective-permute-start | bytes 122888 | tf_op jit(solution)/shard_map/ppermute | solution.py:421
  15.9 0.1 collective-permute-start.4
  16.0 0.0 collective-permute-done.refs_0_
  16.0 1.5 %collective-permute-start.1 = (f32[80,256]{1,0:T(8,128)S(1)}, f32[80,256]{1,0:T(8,128)S(1)}, u32[]{:S(2)}, u32[]{:S(2)}) collective-permute-start(f32[80,256]{1,0:T(8,128)S(1)} %get-tuple-element.24), channel_id=1, source_target_pairs={{0,16},{8,24},{16,0},{24,8},{1,17},{9,25},{17,1},{25,9},{2,18},{10... | collective-permute-start | bytes 245768 | tf_op jit(solution)/shard_map/ppermute | solution.py:494
  17.5 0.7 %block_part.1.base = f32[5,4,16,256]{3,2,1,0:T(8,128)S(1)} custom-call(f32[5,4,16,256]{3,2,1,0:T(8,128)S(1)} %get-tuple-element.17.flux_x, f32[5,4,16,256]{3,2,1,0:T(8,128)S(1)} %get-tuple-element.18.flux_y, f32[8,128]{1,0:T(8,128)S(1)} %get-tuple-element.19.coef_x_ref, f32[16,128]{1,0:T(8,128)S(1)} %get-tuple-element.20.coef_y_ref), custom_call_target="tpu_custom_call" | custom-call | flops 5000000000 | bytes 18000000 | tf_op jit(solution)/shard_map/block_part/pallas_call | solution.py:498
  18.2 1.0 %all-to-all-done.received = f32[32,1,256]{2,1,0:T(1,128)S(1)} async-done(((f32[32,1,256]{2,1,0:T(1,128)}), f32[32,1,256]{2,1,0:T(1,128)S(1)}, u32[]{:S(2)}, u32[]{:S(2)}) %all-to-all-start) | async-done | bytes 32800 | tf_op jit(solution)/shard_map/all_to_all | solution.py:489
  19.3 0.8 %placed_points.1.forcing = f32[5,4,16,256]{3,2,1,0:T(8,128)S(1)} custom-call(f32[32,1,256]{2,1,0:T(1,128)S(1)} %all-to-all-done.received), custom_call_target="tpu_custom_call" | custom-call | flops 10000000 | bytes 36000 | tf_op jit(solution)/shard_map/placed_points/pallas_call | solution.py:516
  20.0 0.0 collective-permute-done.2.refs_2_
  20.0 0.5 %collective-permute-done.1.refs_1_ = f32[80,256]{1,0:T(8,128)S(1)} collective-permute-done((f32[80,256]{1,0:T(8,128)S(1)}, f32[80,256]{1,0:T(8,128)S(1)}, u32[]{:S(2)}, u32[]{:S(2)}) %collective-permute-start.1) | collective-permute-done | bytes 81952 | tf_op jit(solution)/shard_map/ppermute | solution.py:494
  20.6 0.2 far_x_part.1.base
  20.8 0.0 collective-permute-done.5.refs_1_
  20.8 0.0 collective-permute-done.6.refs_2_
  20.8 0.0 collective-permute-done.4.refs_0_
  20.8 0.9 %far_part.1 = f32[5,4,16,256]{3,2,1,0:T(8,128)} custom-call(f32[5,4,16,256]{3,2,1,0:T(8,128)S(1)} %placed_points.1.forcing, f32[5,4,16,256]{3,2,1,0:T(8,128)S(1)} %far_x_part.1.base, f32[4,20,256]{2,1,0:T(8,128)S(1)} %collective-permute-done.3.pair, f32[16,128]{1,0:T(8,128)S(1)} %get-tuple-element.20.coef_y_ref, ...), custom_call_target="tpu_custom_call" | custom-call | flops 1000000000 | bytes 3600000 | tf_op jit(solution)/shard_map/far_part/pallas_call | solution.py:525
  (3 shorter events, 0.0 us)
Async XLA Ops:
  2.4 9.5 %collective-permute-start.3 = (f32[4,20,256]{2,1,0:T(8,128)S(1)}, f32[4,20,256]{2,1,0:T(8,128)S(1)}, u32[]{:S(2)}, u32[]{:S(2)}) collective-permute-start(f32[4,20,256]{2,1,0:T(8,128)S(1)} %get-tuple-element.26), channel_id=1, source_target_pairs={{0,1},{1,0},{2,3},{3,2},{4,5},{5,4},{6,7},{7,6},{8,9},{9,8},{10,11... | collective-permute-start | bytes 245768 | tf_op jit(solution)/shard_map/ppermute | solution.py:496
  2.9 13.1 %collective-permute-start = (f32[160,256]{1,0:T(8,128)S(1)}, f32[160,256]{1,0:T(8,128)S(1)}, u32[]{:S(2)}, u32[]{:S(2)}) collective-permute-start(f32[160,256]{1,0:T(8,128)S(1)} %get-tuple-element.22), channel_id=1, source_target_pairs={{0,24},{8,16},{16,8},{24,0},{1,25},{9,17},{17,9},{25,1},{2,26},{10... | collective-permute-start | bytes 491528 | tf_op jit(solution)/shard_map/ppermute | solution.py:494
  6.4 13.6 %collective-permute-start.2 = (f32[160,256]{1,0:T(8,128)S(1)}, f32[160,256]{1,0:T(8,128)S(1)}, u32[]{:S(2)}, u32[]{:S(2)}) collective-permute-start(f32[160,256]{1,0:T(8,128)S(1)} %get-tuple-element.25), channel_id=1, source_target_pairs={{0,8},{8,0},{16,24},{24,16},{1,9},{9,1},{17,25},{25,17},{2,10},{10... | collective-permute-start | bytes 491528 | tf_op jit(solution)/shard_map/ppermute | solution.py:494
  7.0 12.3 %all-to-all-start = ((f32[32,1,256]{2,1,0:T(1,128)}), f32[32,1,256]{2,1,0:T(1,128)S(1)}, u32[]{:S(2)}, u32[]{:S(2)}) async-start(f32[32,1,256]{2,1,0:T(1,128)} %get-tuple-element.16), calls=%async_computation | async-start | bytes 65536 | tf_op jit(solution)/shard_map/all_to_all | solution.py:489
  12.0 8.8 %collective-permute-start.5 = (f32[2,20,256]{2,1,0:T(8,128)S(1)}, f32[2,20,256]{2,1,0:T(8,128)S(1)}, u32[]{:S(2)}, u32[]{:S(2)}) collective-permute-start(f32[2,20,256]{2,1,0:T(8,128)S(1)} %pad_maximum_fusion.1), channel_id=1, source_target_pairs={{0,5},{1,4},{2,7},{3,6},{4,1},{5,0},{6,3},{7,2},{8,13},{9,12},{10,... | collective-permute-start | bytes 122888 | tf_op jit(solution)/shard_map/ppermute | solution.py:421
  14.5 6.3 %collective-permute-start.6 = (f32[2,20,256]{2,1,0:T(8,128)S(1)}, f32[2,20,256]{2,1,0:T(8,128)S(1)}, u32[]{:S(2)}, u32[]{:S(2)}) collective-permute-start(f32[2,20,256]{2,1,0:T(8,128)S(1)} %pad_maximum_fusion.1), channel_id=1, source_target_pairs={{0,7},{1,6},{2,5},{3,4},{4,3},{5,2},{6,1},{7,0},{8,15},{9,14},{10,... | collective-permute-start | bytes 122888 | tf_op jit(solution)/shard_map/ppermute | solution.py:421
  15.9 4.9 %collective-permute-start.4 = (f32[2,20,256]{2,1,0:T(8,128)S(1)}, f32[2,20,256]{2,1,0:T(8,128)S(1)}, u32[]{:S(2)}, u32[]{:S(2)}) collective-permute-start(f32[2,20,256]{2,1,0:T(8,128)S(1)} %pad_maximum_fusion), channel_id=1, source_target_pairs={{0,3},{1,2},{2,1},{3,0},{4,7},{5,6},{6,5},{7,4},{8,11},{9,10},{10,... | collective-permute-start | bytes 122888 | tf_op jit(solution)/shard_map/ppermute | solution.py:421
  16.0 4.5 %collective-permute-start.1 = (f32[80,256]{1,0:T(8,128)S(1)}, f32[80,256]{1,0:T(8,128)S(1)}, u32[]{:S(2)}, u32[]{:S(2)}) collective-permute-start(f32[80,256]{1,0:T(8,128)S(1)} %get-tuple-element.24), channel_id=1, source_target_pairs={{0,16},{8,24},{16,0},{24,8},{1,17},{9,25},{17,1},{25,9},{2,18},{10... | collective-permute-start | bytes 245768 | tf_op jit(solution)/shard_map/ppermute | solution.py:494

commit v6 on v5

--- a/solution.py
+++ b/solution.py
@@ -156,6 +156,15 @@
     place_x = lax.axis_index("gx")
     shape = (cells_y, depth)
 
+    devices, _, width = pack.shape
+    packed = packed_points(
+        [values[f] for f in range(fields)], cells[...], owners[...], devices, capacity, width
+    )
+    for device in range(devices):
+        pack[device] = packed[device : device + 1]
+    leaving = pltpu.make_async_copy(pack, pack_out, sems.at[len(sources)])
+    leaving.start()
+
     alpha_s[...] = jnp.full(alpha_s.shape, 0.5, F32)
     alpha_s[0:1, 0 : sizes[0]] = alpha_x[...]
     alpha_s[1:2, 0 : sizes[1]] = alpha_y[...]
@@ -175,15 +184,6 @@
     coef_x_out[...] = coef_x
     columns_y = jnp.concatenate([coef_y, jnp.zeros((120, 128), F32)], axis=0).T[:cells_y]
     coef_y_out[...] = columns_y
-
-    devices, _, width = pack.shape
-    packed = packed_points(
-        [values[f] for f in range(fields)], cells[...], owners[...], devices, capacity, width
-    )
-    for device in range(devices):
-        pack[device] = packed[device : device + 1]
-    leaving = pltpu.make_async_copy(pack, pack_out, sems.at[len(sources)])
-    leaving.start()
 
     copies[7].wait()
     copies[8].wait()

time: 21.8 us -> 21.8 us (level)
  no operation moved by 1% of the time
where the time goes in v6:
time: 21.8 us; the launch traced here: 21.7 us
  starting transfers between devices  15 us (69%)
  Pallas kernels  4.87 us (22%)
  waiting for transfers between devices  1.59 us (7%)
    ppermute x3, starting transfers between devices, on_device(): lax.ppermute(face, 'gx', [(i, i ^ turn) for i in range(n_x)])  5.55 us
    all_to_all x1, starting transfers between devices, on_device(): received = lax.all_to_all(pack, ('gx', 'gy'), 0, 0, tiled=True)  4.89 us
    ppermute x3, starting transfers between devices, along_z(): lax.ppermute(sent[turn.bit_length()], 'gy', [(i, i ^ 2 * turn + 1) for i...  4.04 us
    pallas_call x1, Pallas kernels, on_device(): pl.pallas_call(functools.partial(first_kernel, sizes, capacity, turns_x),...  2.4 us
    all_to_all x1, waiting for transfers between devices, on_device(): received = lax.all_to_all(pack, ('gx', 'gy'), 0, 0, tiled=True)  1.04 us
    pallas_call x1, Pallas kernels, on_device(): pl.pallas_call(functools.partial(last_kernel, turns_z), in_specs=[vmem] *...  0.86 us
    pallas_call x1, Pallas kernels, on_device(): pl.pallas_call(functools.partial(place_kernel, capacity), in_specs=[vmem]...  0.76 us
    pallas_call x1, Pallas kernels, on_device(): pl.pallas_call(block_kernel, in_specs=[vmem] * 4, out_specs=vmem, out_sha...  0.68 us
  transfers between devices with their start and end apart: 8, of which 2 were waited for; matrix products, arithmetic and copies ran while one was open for 0% of the time, Pallas kernels for 7%

profile of v6, /device:TPU:0, one launch (start us, length us, event | category | flops | bytes accessed | tf_op | source)
XLA Modules:
  0.0 21.7 jit_solution(13930221554181752880)
XLA Ops:
  0.0 2.4 %flux_and_sums.1 = (f32[5,4,16,256]{3,2,1,0:T(8,128)S(1)}, f32[5,4,16,256]{3,2,1,0:T(8,128)S(1)}, f32[4,20,256]{2,1,0:T(8,128)S(1)}, f32[8,128]{1,0:T(8,128)S(1)...) custom-call(f32[1,16]{1,0:T(1,128)} %bitcast.8, ...), custom_call_target="tpu_custom_call" | custom-call | flops 2500000000 | bytes 9000000 | tf_op jit(solution)/shard_map/flux_and_sums/pallas_call | solution.py:466
  2.4 0.5 %collective-permute-start.3 = (f32[4,20,256]{2,1,0:T(8,128)S(1)}, f32[4,20,256]{2,1,0:T(8,128)S(1)}, u32[]{:S(2)}, u32[]{:S(2)}) collective-permute-start(f32[4,20,256]{2,1,0:T(8,128)S(1)} %get-tuple-element.26), channel_id=1, source_target_pairs={{0,1},{1,0},{2,3},{3,2},{4,5},{5,4},{6,7},{7,6},{8,9},{9,8},{10,11... | collective-permute-start | bytes 245768 | tf_op jit(solution)/shard_map/ppermute | solution.py:496
  2.9 3.5 %collective-permute-start = (f32[160,256]{1,0:T(8,128)S(1)}, f32[160,256]{1,0:T(8,128)S(1)}, u32[]{:S(2)}, u32[]{:S(2)}) collective-permute-start(f32[160,256]{1,0:T(8,128)S(1)} %get-tuple-element.22), channel_id=1, source_target_pairs={{0,24},{8,16},{16,8},{24,0},{1,25},{9,17},{17,9},{25,1},{2,26},{10... | collective-permute-start | bytes 491528 | tf_op jit(solution)/shard_map/ppermute | solution.py:494
  6.4 0.5 %collective-permute-start.2 = (f32[160,256]{1,0:T(8,128)S(1)}, f32[160,256]{1,0:T(8,128)S(1)}, u32[]{:S(2)}, u32[]{:S(2)}) collective-permute-start(f32[160,256]{1,0:T(8,128)S(1)} %get-tuple-element.25), channel_id=1, source_target_pairs={{0,8},{8,0},{16,24},{24,16},{1,9},{9,1},{17,25},{25,17},{2,10},{10... | collective-permute-start | bytes 491528 | tf_op jit(solution)/shard_map/ppermute | solution.py:494
  7.0 4.9 %all-to-all-start = ((f32[32,1,256]{2,1,0:T(1,128)}), f32[32,1,256]{2,1,0:T(1,128)S(1)}, u32[]{:S(2)}, u32[]{:S(2)}) async-start(f32[32,1,256]{2,1,0:T(1,128)} %get-tuple-element.16), calls=%async_computation | async-start | bytes 65536 | tf_op jit(solution)/shard_map/all_to_all | solution.py:489
  11.9 0.0 collective-permute-done.3.pair
  12.0 2.5 %collective-permute-start.5 = (f32[2,20,256]{2,1,0:T(8,128)S(1)}, f32[2,20,256]{2,1,0:T(8,128)S(1)}, u32[]{:S(2)}, u32[]{:S(2)}) collective-permute-start(f32[2,20,256]{2,1,0:T(8,128)S(1)} %pad_maximum_fusion.1), channel_id=1, source_target_pairs={{0,5},{1,4},{2,7},{3,6},{4,1},{5,0},{6,3},{7,2},{8,13},{9,12},{10,... | collective-permute-start | bytes 122888 | tf_op jit(solution)/shard_map/ppermute | solution.py:421
  14.5 1.4 %collective-permute-start.6 = (f32[2,20,256]{2,1,0:T(8,128)S(1)}, f32[2,20,256]{2,1,0:T(8,128)S(1)}, u32[]{:S(2)}, u32[]{:S(2)}) collective-permute-start(f32[2,20,256]{2,1,0:T(8,128)S(1)} %pad_maximum_fusion.1), channel_id=1, source_target_pairs={{0,7},{1,6},{2,5},{3,4},{4,3},{5,2},{6,1},{7,0},{8,15},{9,14},{10,... | collective-permute-start | bytes 122888 | tf_op jit(solution)/shard_map/ppermute | solution.py:421
  15.9 0.1 collective-permute-start.4
  16.0 0.0 collective-permute-done.refs_0_
  16.0 1.5 %collective-permute-start.1 = (f32[80,256]{1,0:T(8,128)S(1)}, f32[80,256]{1,0:T(8,128)S(1)}, u32[]{:S(2)}, u32[]{:S(2)}) collective-permute-start(f32[80,256]{1,0:T(8,128)S(1)} %get-tuple-element.24), channel_id=1, source_target_pairs={{0,16},{8,24},{16,0},{24,8},{1,17},{9,25},{17,1},{25,9},{2,18},{10... | collective-permute-start | bytes 245768 | tf_op jit(solution)/shard_map/ppermute | solution.py:494
  17.5 0.7 %block_part.1.base = f32[5,4,16,256]{3,2,1,0:T(8,128)S(1)} custom-call(f32[5,4,16,256]{3,2,1,0:T(8,128)S(1)} %get-tuple-element.17.flux_x, f32[5,4,16,256]{3,2,1,0:T(8,128)S(1)} %get-tuple-element.18.flux_y, f32[8,128]{1,0:T(8,128)S(1)} %get-tuple-element.19.coef_x_ref, f32[16,128]{1,0:T(8,128)S(1)} %get-tuple-element.20.coef_y_ref), custom_call_target="tpu_custom_call" | custom-call | flops 5000000000 | bytes 18000000 | tf_op jit(solution)/shard_map/block_part/pallas_call | solution.py:498
  18.2 1.0 %all-to-all-done.received = f32[32,1,256]{2,1,0:T(1,128)S(1)} async-done(((f32[32,1,256]{2,1,0:T(1,128)}), f32[32,1,256]{2,1,0:T(1,128)S(1)}, u32[]{:S(2)}, u32[]{:S(2)}) %all-to-all-start) | async-done | bytes 32800 | tf_op jit(solution)/shard_map/all_to_all | solution.py:489
  19.3 0.8 %placed_points.1.forcing = f32[5,4,16,256]{3,2,1,0:T(8,128)S(1)} custom-call(f32[32,1,256]{2,1,0:T(1,128)S(1)} %all-to-all-done.received), custom_call_target="tpu_custom_call" | custom-call | flops 10000000 | bytes 36000 | tf_op jit(solution)/shard_map/placed_points/pallas_call | solution.py:516
  20.0 0.0 collective-permute-done.2.refs_2_
  20.0 0.5 %collective-permute-done.1.refs_1_ = f32[80,256]{1,0:T(8,128)S(1)} collective-permute-done((f32[80,256]{1,0:T(8,128)S(1)}, f32[80,256]{1,0:T(8,128)S(1)}, u32[]{:S(2)}, u32[]{:S(2)}) %collective-permute-start.1) | collective-permute-done | bytes 81952 | tf_op jit(solution)/shard_map/ppermute | solution.py:494
  20.6 0.2 far_x_part.1.base
  20.8 0.0 collective-permute-done.5.refs_1_
  20.8 0.0 collective-permute-done.6.refs_2_
  20.8 0.0 collective-permute-done.4.refs_0_
  20.8 0.9 %far_part.1 = f32[5,4,16,256]{3,2,1,0:T(8,128)} custom-call(f32[5,4,16,256]{3,2,1,0:T(8,128)S(1)} %placed_points.1.forcing, f32[5,4,16,256]{3,2,1,0:T(8,128)S(1)} %far_x_part.1.base, f32[4,20,256]{2,1,0:T(8,128)S(1)} %collective-permute-done.3.pair, f32[16,128]{1,0:T(8,128)S(1)} %get-tuple-element.20.coef_y_ref, ...), custom_call_target="tpu_custom_call" | custom-call | flops 1000000000 | bytes 3600000 | tf_op jit(solution)/shard_map/far_part/pallas_call | solution.py:525
  (3 shorter events, 0.0 us)
Async XLA Ops:
  2.4 9.5 %collective-permute-start.3 = (f32[4,20,256]{2,1,0:T(8,128)S(1)}, f32[4,20,256]{2,1,0:T(8,128)S(1)}, u32[]{:S(2)}, u32[]{:S(2)}) collective-permute-start(f32[4,20,256]{2,1,0:T(8,128)S(1)} %get-tuple-element.26), channel_id=1, source_target_pairs={{0,1},{1,0},{2,3},{3,2},{4,5},{5,4},{6,7},{7,6},{8,9},{9,8},{10,11... | collective-permute-start | bytes 245768 | tf_op jit(solution)/shard_map/ppermute | solution.py:496
  2.9 13.1 %collective-permute-start = (f32[160,256]{1,0:T(8,128)S(1)}, f32[160,256]{1,0:T(8,128)S(1)}, u32[]{:S(2)}, u32[]{:S(2)}) collective-permute-start(f32[160,256]{1,0:T(8,128)S(1)} %get-tuple-element.22), channel_id=1, source_target_pairs={{0,24},{8,16},{16,8},{24,0},{1,25},{9,17},{17,9},{25,1},{2,26},{10... | collective-permute-start | bytes 491528 | tf_op jit(solution)/shard_map/ppermute | solution.py:494
  6.4 13.6 %collective-permute-start.2 = (f32[160,256]{1,0:T(8,128)S(1)}, f32[160,256]{1,0:T(8,128)S(1)}, u32[]{:S(2)}, u32[]{:S(2)}) collective-permute-start(f32[160,256]{1,0:T(8,128)S(1)} %get-tuple-element.25), channel_id=1, source_target_pairs={{0,8},{8,0},{16,24},{24,16},{1,9},{9,1},{17,25},{25,17},{2,10},{10... | collective-permute-start | bytes 491528 | tf_op jit(solution)/shard_map/ppermute | solution.py:494
  7.0 12.3 %all-to-all-start = ((f32[32,1,256]{2,1,0:T(1,128)}), f32[32,1,256]{2,1,0:T(1,128)S(1)}, u32[]{:S(2)}, u32[]{:S(2)}) async-start(f32[32,1,256]{2,1,0:T(1,128)} %get-tuple-element.16), calls=%async_computation | async-start | bytes 65536 | tf_op jit(solution)/shard_map/all_to_all | solution.py:489
  12.0 8.8 %collective-permute-start.5 = (f32[2,20,256]{2,1,0:T(8,128)S(1)}, f32[2,20,256]{2,1,0:T(8,128)S(1)}, u32[]{:S(2)}, u32[]{:S(2)}) collective-permute-start(f32[2,20,256]{2,1,0:T(8,128)S(1)} %pad_maximum_fusion.1), channel_id=1, source_target_pairs={{0,5},{1,4},{2,7},{3,6},{4,1},{5,0},{6,3},{7,2},{8,13},{9,12},{10,... | collective-permute-start | bytes 122888 | tf_op jit(solution)/shard_map/ppermute | solution.py:421
  14.5 6.3 %collective-permute-start.6 = (f32[2,20,256]{2,1,0:T(8,128)S(1)}, f32[2,20,256]{2,1,0:T(8,128)S(1)}, u32[]{:S(2)}, u32[]{:S(2)}) collective-permute-start(f32[2,20,256]{2,1,0:T(8,128)S(1)} %pad_maximum_fusion.1), channel_id=1, source_target_pairs={{0,7},{1,6},{2,5},{3,4},{4,3},{5,2},{6,1},{7,0},{8,15},{9,14},{10,... | collective-permute-start | bytes 122888 | tf_op jit(solution)/shard_map/ppermute | solution.py:421
  15.9 4.9 %collective-permute-start.4 = (f32[2,20,256]{2,1,0:T(8,128)S(1)}, f32[2,20,256]{2,1,0:T(8,128)S(1)}, u32[]{:S(2)}, u32[]{:S(2)}) collective-permute-start(f32[2,20,256]{2,1,0:T(8,128)S(1)} %pad_maximum_fusion), channel_id=1, source_target_pairs={{0,3},{1,2},{2,1},{3,0},{4,7},{5,6},{6,5},{7,4},{8,11},{9,10},{10,... | collective-permute-start | bytes 122888 | tf_op jit(solution)/shard_map/ppermute | solution.py:421
  16.0 4.5 %collective-permute-start.1 = (f32[80,256]{1,0:T(8,128)S(1)}, f32[80,256]{1,0:T(8,128)S(1)}, u32[]{:S(2)}, u32[]{:S(2)}) collective-permute-start(f32[80,256]{1,0:T(8,128)S(1)} %get-tuple-element.24), channel_id=1, source_target_pairs={{0,16},{8,24},{16,0},{24,8},{1,17},{9,25},{17,1},{25,9},{2,18},{10... | collective-permute-start | bytes 245768 | tf_op jit(solution)/shard_map/ppermute | solution.py:494

commit v7 on v5

--- a/solution.py
+++ b/solution.py
@@ -460,7 +460,7 @@
         jac_y,
     ]
     turns_x = tuple(range(n_x - 1, 0, -1))
-    turns_z = tuple(range(1, n_y // 2))
+    turns_z = tuple(sorted(range(1, n_y // 2), key=lambda turn: (touches(turn), turn)))
     width = -(-(fields + 1) * capacity // 128) * 128
     face_rows = fields * cells_y
     flux_x, flux_y, own_y, coef_x, coef_y, pack, *faces = pl.pallas_call(

time: 21.8 us -> 21.8 us (level)
  no operation moved by 1% of the time
where the time goes in v7:
time: 21.8 us; the launch traced here: 21.7 us
  starting transfers between devices  15 us (69%)
  Pallas kernels  4.88 us (22%)
  waiting for transfers between devices  1.59 us (7%)
    ppermute x3, starting transfers between devices, on_device(): lax.ppermute(face, 'gx', [(i, i ^ turn) for i in range(n_x)])  5.55 us
    all_to_all x1, starting transfers between devices, on_device(): received = lax.all_to_all(pack, ('gx', 'gy'), 0, 0, tiled=True)  4.89 us
    ppermute x3, starting transfers between devices, along_z(): lax.ppermute(sent[turn.bit_length()], 'gy', [(i, i ^ 2 * turn + 1) for i...  4.04 us
    pallas_call x1, Pallas kernels, on_device(): pl.pallas_call(functools.partial(first_kernel, sizes, capacity, turns_x),...  2.4 us
    all_to_all x1, waiting for transfers between devices, on_device(): received = lax.all_to_all(pack, ('gx', 'gy'), 0, 0, tiled=True)  1.04 us
    pallas_call x1, Pallas kernels, on_device(): pl.pallas_call(functools.partial(last_kernel, turns_z), in_specs=[vmem] *...  0.86 us
    pallas_call x1, Pallas kernels, on_device(): pl.pallas_call(functools.partial(place_kernel, capacity), in_specs=[vmem]...  0.76 us
    pallas_call x1, Pallas kernels, on_device(): pl.pallas_call(block_kernel, in_specs=[vmem] * 4, out_specs=vmem, out_sha...  0.68 us
  transfers between devices with their start and end apart: 8, of which 2 were waited for; matrix products, arithmetic and copies ran while one was open for 0% of the time, Pallas kernels for 7%

profile of v7, /device:TPU:0, one launch (start us, length us, event | category | flops | bytes accessed | tf_op | source)
XLA Modules:
  0.0 21.7 jit_solution(13763085622102472847)
XLA Ops:
  0.0 2.4 %flux_and_sums.1 = (f32[5,4,16,256]{3,2,1,0:T(8,128)S(1)}, f32[5,4,16,256]{3,2,1,0:T(8,128)S(1)}, f32[4,20,256]{2,1,0:T(8,128)S(1)}, f32[8,128]{1,0:T(8,128)S(1)...) custom-call(f32[1,16]{1,0:T(1,128)} %bitcast.8, ...), custom_call_target="tpu_custom_call" | custom-call | flops 2500000000 | bytes 9000000 | tf_op jit(solution)/shard_map/flux_and_sums/pallas_call | solution.py:466
  2.4 0.5 %collective-permute-start.3 = (f32[4,20,256]{2,1,0:T(8,128)S(1)}, f32[4,20,256]{2,1,0:T(8,128)S(1)}, u32[]{:S(2)}, u32[]{:S(2)}) collective-permute-start(f32[4,20,256]{2,1,0:T(8,128)S(1)} %get-tuple-element.26), channel_id=1, source_target_pairs={{0,1},{1,0},{2,3},{3,2},{4,5},{5,4},{6,7},{7,6},{8,9},{9,8},{10,11... | collective-permute-start | bytes 245768 | tf_op jit(solution)/shard_map/ppermute | solution.py:496
  2.9 3.5 %collective-permute-start = (f32[160,256]{1,0:T(8,128)S(1)}, f32[160,256]{1,0:T(8,128)S(1)}, u32[]{:S(2)}, u32[]{:S(2)}) collective-permute-start(f32[160,256]{1,0:T(8,128)S(1)} %get-tuple-element.22), channel_id=1, source_target_pairs={{0,24},{8,16},{16,8},{24,0},{1,25},{9,17},{17,9},{25,1},{2,26},{10... | collective-permute-start | bytes 491528 | tf_op jit(solution)/shard_map/ppermute | solution.py:494
  6.4 0.5 %collective-permute-start.2 = (f32[160,256]{1,0:T(8,128)S(1)}, f32[160,256]{1,0:T(8,128)S(1)}, u32[]{:S(2)}, u32[]{:S(2)}) collective-permute-start(f32[160,256]{1,0:T(8,128)S(1)} %get-tuple-element.25), channel_id=1, source_target_pairs={{0,8},{8,0},{16,24},{24,16},{1,9},{9,1},{17,25},{25,17},{2,10},{10... | collective-permute-start | bytes 491528 | tf_op jit(solution)/shard_map/ppermute | solution.py:494
  7.0 4.9 %all-to-all-start = ((f32[32,1,256]{2,1,0:T(1,128)}), f32[32,1,256]{2,1,0:T(1,128)S(1)}, u32[]{:S(2)}, u32[]{:S(2)}) async-start(f32[32,1,256]{2,1,0:T(1,128)} %get-tuple-element.16), calls=%async_computation | async-start | bytes 65536 | tf_op jit(solution)/shard_map/all_to_all | solution.py:489
  11.9 0.0 collective-permute-done.3.pair
  12.0 2.5 %collective-permute-start.4 = (f32[2,20,256]{2,1,0:T(8,128)S(1)}, f32[2,20,256]{2,1,0:T(8,128)S(1)}, u32[]{:S(2)}, u32[]{:S(2)}) collective-permute-start(f32[2,20,256]{2,1,0:T(8,128)S(1)} %pad_maximum_fusion), channel_id=1, source_target_pairs={{0,5},{1,4},{2,7},{3,6},{4,1},{5,0},{6,3},{7,2},{8,13},{9,12},{10,... | collective-permute-start | bytes 122888 | tf_op jit(solution)/shard_map/ppermute | solution.py:421
  14.5 1.4 %collective-permute-start.6 = (f32[2,20,256]{2,1,0:T(8,128)S(1)}, f32[2,20,256]{2,1,0:T(8,128)S(1)}, u32[]{:S(2)}, u32[]{:S(2)}) collective-permute-start(f32[2,20,256]{2,1,0:T(8,128)S(1)} %pad_maximum_fusion), channel_id=1, source_target_pairs={{0,7},{1,6},{2,5},{3,4},{4,3},{5,2},{6,1},{7,0},{8,15},{9,14},{10,... | collective-permute-start | bytes 122888 | tf_op jit(solution)/shard_map/ppermute | solution.py:421
  15.9 0.1 collective-permute-start.5
  16.0 0.0 collective-permute-done.refs_0_
  16.0 1.5 %collective-permute-start.1 = (f32[80,256]{1,0:T(8,128)S(1)}, f32[80,256]{1,0:T(8,128)S(1)}, u32[]{:S(2)}, u32[]{:S(2)}) collective-permute-start(f32[80,256]{1,0:T(8,128)S(1)} %get-tuple-element.24), channel_id=1, source_target_pairs={{0,16},{8,24},{16,0},{24,8},{1,17},{9,25},{17,1},{25,9},{2,18},{10... | collective-permute-start | bytes 245768 | tf_op jit(solution)/shard_map/ppermute | solution.py:494
  17.5 0.7 %block_part.1.base = f32[5,4,16,256]{3,2,1,0:T(8,128)S(1)} custom-call(f32[5,4,16,256]{3,2,1,0:T(8,128)S(1)} %get-tuple-element.17.flux_x, f32[5,4,16,256]{3,2,1,0:T(8,128)S(1)} %get-tuple-element.18.flux_y, f32[8,128]{1,0:T(8,128)S(1)} %get-tuple-element.19.coef_x_ref, f32[16,128]{1,0:T(8,128)S(1)} %get-tuple-element.20.coef_y_ref), custom_call_target="tpu_custom_call" | custom-call | flops 5000000000 | bytes 18000000 | tf_op jit(solution)/shard_map/block_part/pallas_call | solution.py:498
  18.2 1.0 %all-to-all-done.received = f32[32,1,256]{2,1,0:T(1,128)S(1)} async-done(((f32[32,1,256]{2,1,0:T(1,128)}), f32[32,1,256]{2,1,0:T(1,128)S(1)}, u32[]{:S(2)}, u32[]{:S(2)}) %all-to-all-start) | async-done | bytes 32800 | tf_op jit(solution)/shard_map/all_to_all | solution.py:489
  19.3 0.8 %placed_points.1.forcing = f32[5,4,16,256]{3,2,1,0:T(8,128)S(1)} custom-call(f32[32,1,256]{2,1,0:T(1,128)S(1)} %all-to-all-done.received), custom_call_target="tpu_custom_call" | custom-call | flops 10000000 | bytes 36000 | tf_op jit(solution)/shard_map/placed_points/pallas_call | solution.py:516
  20.0 0.0 collective-permute-done.2.refs_2_
  20.0 0.5 %collective-permute-done.1.refs_1_ = f32[80,256]{1,0:T(8,128)S(1)} collective-permute-done((f32[80,256]{1,0:T(8,128)S(1)}, f32[80,256]{1,0:T(8,128)S(1)}, u32[]{:S(2)}, u32[]{:S(2)}) %collective-permute-start.1) | collective-permute-done | bytes 81952 | tf_op jit(solution)/shard_map/ppermute | solution.py:494
  20.6 0.2 far_x_part.1.base
  20.8 0.0 collective-permute-done.5.refs_1_
  20.8 0.0 collective-permute-done.4.refs_0_
  20.8 0.0 collective-permute-done.6.refs_2_
  20.8 0.9 %far_part.1 = f32[5,4,16,256]{3,2,1,0:T(8,128)} custom-call(f32[5,4,16,256]{3,2,1,0:T(8,128)S(1)} %placed_points.1.forcing, f32[5,4,16,256]{3,2,1,0:T(8,128)S(1)} %far_x_part.1.base, f32[4,20,256]{2,1,0:T(8,128)S(1)} %collective-permute-done.3.pair, f32[16,128]{1,0:T(8,128)S(1)} %get-tuple-element.20.coef_y_ref, ...), custom_call_target="tpu_custom_call" | custom-call | flops 1000000000 | bytes 3600000 | tf_op jit(solution)/shard_map/far_part/pallas_call | solution.py:525
  (3 shorter events, 0.0 us)
Async XLA Ops:
  2.4 9.5 %collective-permute-start.3 = (f32[4,20,256]{2,1,0:T(8,128)S(1)}, f32[4,20,256]{2,1,0:T(8,128)S(1)}, u32[]{:S(2)}, u32[]{:S(2)}) collective-permute-start(f32[4,20,256]{2,1,0:T(8,128)S(1)} %get-tuple-element.26), channel_id=1, source_target_pairs={{0,1},{1,0},{2,3},{3,2},{4,5},{5,4},{6,7},{7,6},{8,9},{9,8},{10,11... | collective-permute-start | bytes 245768 | tf_op jit(solution)/shard_map/ppermute | solution.py:496
  2.9 13.1 %collective-permute-start = (f32[160,256]{1,0:T(8,128)S(1)}, f32[160,256]{1,0:T(8,128)S(1)}, u32[]{:S(2)}, u32[]{:S(2)}) collective-permute-start(f32[160,256]{1,0:T(8,128)S(1)} %get-tuple-element.22), channel_id=1, source_target_pairs={{0,24},{8,16},{16,8},{24,0},{1,25},{9,17},{17,9},{25,1},{2,26},{10... | collective-permute-start | bytes 491528 | tf_op jit(solution)/shard_map/ppermute | solution.py:494
  6.4 13.6 %collective-permute-start.2 = (f32[160,256]{1,0:T(8,128)S(1)}, f32[160,256]{1,0:T(8,128)S(1)}, u32[]{:S(2)}, u32[]{:S(2)}) collective-permute-start(f32[160,256]{1,0:T(8,128)S(1)} %get-tuple-element.25), channel_id=1, source_target_pairs={{0,8},{8,0},{16,24},{24,16},{1,9},{9,1},{17,25},{25,17},{2,10},{10... | collective-permute-start | bytes 491528 | tf_op jit(solution)/shard_map/ppermute | solution.py:494
  7.0 12.3 %all-to-all-start = ((f32[32,1,256]{2,1,0:T(1,128)}), f32[32,1,256]{2,1,0:T(1,128)S(1)}, u32[]{:S(2)}, u32[]{:S(2)}) async-start(f32[32,1,256]{2,1,0:T(1,128)} %get-tuple-element.16), calls=%async_computation | async-start | bytes 65536 | tf_op jit(solution)/shard_map/all_to_all | solution.py:489
  12.0 8.8 %collective-permute-start.4 = (f32[2,20,256]{2,1,0:T(8,128)S(1)}, f32[2,20,256]{2,1,0:T(8,128)S(1)}, u32[]{:S(2)}, u32[]{:S(2)}) collective-permute-start(f32[2,20,256]{2,1,0:T(8,128)S(1)} %pad_maximum_fusion), channel_id=1, source_target_pairs={{0,5},{1,4},{2,7},{3,6},{4,1},{5,0},{6,3},{7,2},{8,13},{9,12},{10,... | collective-permute-start | bytes 122888 | tf_op jit(solution)/shard_map/ppermute | solution.py:421
  14.5 6.3 %collective-permute-start.6 = (f32[2,20,256]{2,1,0:T(8,128)S(1)}, f32[2,20,256]{2,1,0:T(8,128)S(1)}, u32[]{:S(2)}, u32[]{:S(2)}) collective-permute-start(f32[2,20,256]{2,1,0:T(8,128)S(1)} %pad_maximum_fusion), channel_id=1, source_target_pairs={{0,7},{1,6},{2,5},{3,4},{4,3},{5,2},{6,1},{7,0},{8,15},{9,14},{10,... | collective-permute-start | bytes 122888 | tf_op jit(solution)/shard_map/ppermute | solution.py:421
  15.9 4.8 %collective-permute-start.5 = (f32[2,20,256]{2,1,0:T(8,128)S(1)}, f32[2,20,256]{2,1,0:T(8,128)S(1)}, u32[]{:S(2)}, u32[]{:S(2)}) collective-permute-start(f32[2,20,256]{2,1,0:T(8,128)S(1)} %pad_maximum_fusion.1), channel_id=1, source_target_pairs={{0,3},{1,2},{2,1},{3,0},{4,7},{5,6},{6,5},{7,4},{8,11},{9,10},{10,... | collective-permute-start | bytes 122888 | tf_op jit(solution)/shard_map/ppermute | solution.py:421
  16.0 4.5 %collective-permute-start.1 = (f32[80,256]{1,0:T(8,128)S(1)}, f32[80,256]{1,0:T(8,128)S(1)}, u32[]{:S(2)}, u32[]{:S(2)}) collective-permute-start(f32[80,256]{1,0:T(8,128)S(1)} %get-tuple-element.24), channel_id=1, source_target_pairs={{0,16},{8,24},{16,0},{24,8},{1,17},{9,25},{17,1},{25,9},{2,18},{10... | collective-permute-start | bytes 245768 | tf_op jit(solution)/shard_map/ppermute | solution.py:494
